TPU v7x, 256 devices: a whole 4x4x8 slice. The times are simulated.
256 devices in a mesh: group: 2 (over core), lat: 4 (over z_lo), lon: 32 (over y, z_hi, x).
Axes of the slice: x: 4, y: 4, z: 8 (z_hi: 2, z_lo: 4; z = z_hi * 4 + z_lo), core: 2. Of those that a mesh axis runs over, the one named last changes fastest.
Arguments:
- states: bfloat16 [2, 64, 1536, 512], P('group', 'lat', 'lon'), may hold values from -6 to 6
- cotangent: bfloat16 [2, 64, 1536, 512], P('group', 'lat', 'lon'), may hold values from -6 to 6
- depth_kernel: float32 [2, 7, 7, 512], P('group'), may hold values from -0.875 to 0.875
- norm_gain: float32 [2, 512], P('group'), may hold values from 0.5 to 1.5
- w_in: bfloat16 [2, 2048, 512], P('group'), may hold values from -0.25 to 0.25
- w_out: bfloat16 [2, 2048, 512], P('group'), may hold values from -0.125 to 0.125
- source_tiles: int32 [2, 4, 32, 4], P('group', 'lat', 'lon'), may hold values from 0 to 127, as said below
- regrid_weights: float32 [2, 64, 1536, 4], P('group', 'lat', 'lon'), may hold values from 0.2 to 1
- land_mask: int32 [64, 1536], P('lat', 'lon'), may hold values 0 or 1
Outputs:
- advanced: bfloat16 [2, 64, 1536, 512], P('group', 'lat', 'lon')
- state_grad: bfloat16 [2, 64, 1536, 512], P('group', 'lat', 'lon')
- grad_w_in: float32 [2, 2048, 512], P('group', ('lat', 'lon'))
- grad_w_out: float32 [2, 2048, 512], P('group', ('lat', 'lon'))
Inputs may be any that keep to these rules, and one draw needn't show every extreme that they name: `source_tiles`: entry 0 of each list names the destination tile itself; every entry names a tile whose latitude tile differs from the destination's by at most one and whose longitude tile differs by at most one around the longitude cycle.
All inputs are finite; a program needn't handle non-finite values. No bound on the sum of `land_mask` on one device may be relied on, other than what follows from the above.
Results may differ from a plain program's by a relative error of at most 0.017.
Values may be sent and summed in bfloat16 or wider, within the bound.
No kernel may reach another device: no remote copies, remote signals or barrier semaphores. Data moves between devices by JAX's collectives and lax.ppermute only.
A program may use at most 128 MiB of HBM per device.

v0:
```python
import jax
import jax.numpy as jnp
from jax import lax
from jax.sharding import PartitionSpec as P

Q = 8
K = 4


EPS = 1e-06


def from_partner(x, axis, distance):
    return lax.ppermute(x, axis, [(i, i ^ 1 << distance) for i in range(lax.axis_size(axis))])


def extended(block, sides, width):
    for axis, dim in sides:
        count = lax.axis_size(axis)
        forward = [(i, i + 1) for i in range(count - 1)]
        forward.append((count - 1, 0))
        backward = [(target, source) for source, target in forward]
        low = lax.ppermute(
            lax.slice_in_dim(block, block.shape[dim] - width, None, axis=dim), axis, forward
        )
        high = lax.ppermute(lax.slice_in_dim(block, 0, width, axis=dim), axis, backward)
        block = jnp.concatenate([low, block, high], axis=dim)
    return block


def open_rim(padded, rim_width):
    lat_index = lax.axis_index("lat")
    lat_total = lax.axis_size("lat")
    row_ids = jnp.arange(padded.shape[0])
    inside = ((row_ids >= rim_width) | (lat_index > 0)) & (
        (row_ids < padded.shape[0] - rim_width) | (lat_index < lat_total - 1)
    )
    return jnp.where(inside[:, None, None], padded, jnp.zeros_like(padded))


def conv_taps(padded, kernel, lat_cells, lon_cells, flipped):
    side = kernel.shape[0]
    rim_width = side // 2
    running = jnp.zeros((lat_cells, lon_cells, kernel.shape[2]), jnp.float32)
    for row_off in range(side):
        for col_off in range(side):
            if flipped:
                row_at = 2 * rim_width - row_off
                col_at = 2 * rim_width - col_off
            else:
                row_at = row_off
                col_at = col_off
            window = padded[row_at : row_at + lat_cells, col_at : col_at + lon_cells]
            running = running + kernel[row_off, col_off] * window.astype(jnp.float32)
    return running


def body(
    states, cotangent, depth_kernel, norm_gain, w_in, w_out, source_tiles, regrid_weights, land_mask
):
    current = states[0]
    upstream = cotangent[0]
    kernel = depth_kernel[0]
    norm_scale = norm_gain[0]
    w_first = w_in[0]
    w_second = w_out[0]
    lat_cells, lon_cells, channels = current.shape
    cell_count = lat_cells * lon_cells
    rim_width = kernel.shape[0] // 2
    export = current[:, :, :Q]
    partner = from_partner(export, "group", 0)
    sources = source_tiles[0, 0, 0]
    beside_all = extended(partner[None, None], (("lat", 0), ("lon", 1)), 1)
    beside_all = beside_all.reshape(9, lat_cells, lon_cells, Q)
    lon_total = lax.axis_size("lon")
    src_lat = sources // lon_total
    src_lon = sources % lon_total
    lat_step = src_lat - lax.axis_index("lat") + 1
    lon_step = (src_lon - lax.axis_index("lon") + 1 + lon_total) % lon_total
    chosen = beside_all[lat_step * 3 + lon_step]
    running = jnp.zeros((lat_cells, lon_cells, Q), jnp.float32)
    for pair_idx in range(K):
        running = running + regrid_weights[0, :, :, pair_idx, None] * chosen[pair_idx].astype(
            jnp.float32
        )
    forcing = (current[:, :, Q : 2 * Q].astype(jnp.float32) + running).astype(jnp.bfloat16)
    forced = jnp.concatenate([current[:, :, :Q], forcing, current[:, :, 2 * Q :]], axis=2)
    padded = extended(forced, (("lat", 0), ("lon", 1)), rim_width)
    hidden = conv_taps(open_rim(padded, rim_width), kernel, lat_cells, lon_cells, False)
    centre = jnp.mean(hidden, axis=-1, keepdims=True)
    variance = jnp.mean(jnp.square(hidden - centre), axis=-1, keepdims=True)
    inv_std = lax.rsqrt(variance + EPS)
    normal_hat = (hidden - centre) * inv_std
    normed = (normal_hat * norm_scale).astype(jnp.bfloat16).reshape(cell_count, channels)
    pre_act = jnp.einsum("pc,fc->pf", normed, w_first, preferred_element_type=jnp.float32)
    active, gelu_back = jax.vjp(jax.nn.gelu, pre_act)
    act_bf = active.astype(jnp.bfloat16)
    update = jnp.einsum("pf,fc->pc", act_bf, w_second, preferred_element_type=jnp.float32)
    group_index = lax.axis_index("group")
    ocean_keep = jnp.where(group_index == 1, land_mask.astype(jnp.float32), 1.0).reshape(
        cell_count, 1
    )
    flat_now = current.reshape(cell_count, channels)
    advanced = (flat_now.astype(jnp.float32) + ocean_keep * update).astype(jnp.bfloat16)
    d_update = (ocean_keep * upstream.reshape(cell_count, channels).astype(jnp.float32)).astype(
        jnp.bfloat16
    )
    d_active = jnp.einsum("pc,fc->pf", d_update, w_second, preferred_element_type=jnp.float32)
    d_pre = gelu_back(d_active)[0].astype(jnp.bfloat16)
    grad_first = jnp.einsum("pf,pc->fc", d_pre, normed, preferred_element_type=jnp.float32)
    grad_second = jnp.einsum("pf,pc->fc", act_bf, d_update, preferred_element_type=jnp.float32)
    summed = lax.psum_scatter(
        jnp.concatenate([grad_first, grad_second], axis=1),
        ("lat", "lon"),
        scatter_dimension=0,
        tiled=True,
    )
    d_normed = jnp.einsum("pf,fc->pc", d_pre, w_first, preferred_element_type=jnp.float32)
    scaled = d_normed.reshape(lat_cells, lon_cells, channels) * norm_scale
    mean_plain = jnp.mean(scaled, axis=-1, keepdims=True)
    mean_mixed = jnp.mean(scaled * normal_hat, axis=-1, keepdims=True)
    d_hidden = (inv_std * (scaled - mean_plain - normal_hat * mean_mixed)).astype(jnp.bfloat16)
    grad_pad = extended(d_hidden, (("lat", 0), ("lon", 1)), rim_width)
    d_forced = conv_taps(open_rim(grad_pad, rim_width), kernel, lat_cells, lon_cells, True)
    state_grad = (upstream.astype(jnp.float32) + d_forced).astype(jnp.bfloat16)
    return (
        advanced.reshape(1, lat_cells, lon_cells, channels),
        state_grad[None],
        summed[:, :channels][None],
        summed[:, channels:][None],
    )


def solution(mesh):
    placed = (
        P("group", "lat", "lon", None),
        P("group", "lat", "lon", None),
        P("group", None, None, None),
        P("group", None),
        P("group", None, None),
        P("group", None, None),
        P("group", "lat", "lon", None),
        P("group", "lat", "lon", None),
        P("lat", "lon"),
    )
    return jax.shard_map(
        body,
        mesh=mesh,
        in_specs=placed,
        out_specs=(
            P("group", "lat", "lon", None),
            P("group", "lat", "lon", None),
            P("group", ("lat", "lon"), None),
            P("group", ("lat", "lon"), None),
        ),
        check_vma=False,
    )
```

profile of v0, /device:TPU:32, one launch (start us, length us, event | category | flops | bytes accessed | tf_op | source)
XLA Modules:
  0.0 966.2 jit_solution(5871069468599439393)
XLA Ops:
  9.2 1.5 fusion.42
  12.4 2.3 multiply_convert_fusion.2
  16.5 1.9 collective-permute-start.2
  18.7 5.3 collective-permute-done.2
  24.1 6.7 collective-permute-done.1
  31.0 9.2 collective-permute-start.4
  40.2 1.5 slice.731
  43.3 11.4 %collective-permute-done.3 = bf16[3,1,16,48,8]{3,4,2,1,0:T(8,128)(2,1)} collective-permute-done((bf16[3,1,16,48,8]{3,4,2,1,0:T(8,128)(2,1)S(1)}, bf16[3,1,16,48,8]{3,4,2,1,0:T(8,128)(2,1)}, u32[]{:S(2)}, u32[]{:S(2)}) %collective-permute-start.3) | collective-permute-done | bytes 36896 | tf_op jit(solution)/shard_map/ppermute | solution.py:23
  57.9 1.6 copy.24
  60.3 1.7 fusion.25
  63.1 1.2 collective-permute-start.6
  64.3 1.2 fusion.40
  65.5 2.6 collective-permute-done.5
  68.1 1.2 collective-permute-done.6
  70.0 10.1 %collective-permute-start.8 = (bf16[22,3,512]{2,1,0:T(4,128)(2,1)S(1)}, bf16[22,3,512]{2,1,0:T(4,128)(2,1)S(1)}, u32[]{:S(2)}, u32[]{:S(2)}) collective-permute-start(bf16[22,3,512]{2,1,0:T(4,128)(2,1)S(1)} %get-tuple-element.21), channel_id=1, source_target_pairs={{1,0},{2,1},{3,2},{4,3},{5,4},{6,5},{7,6},{8,7},{9,8},{10,9},{11,1... | collective-permute-start | bytes 202760 | tf_op jit(solution)/shard_map/ppermute | solution.py:26
  80.2 2.5 collective-permute-done.7
  82.7 1.3 maximum_select_fusion
  84.4 12.0 %fusion.35 = (f32[16,48]{1,0:T(8,128)S(1)}, f32[16,48,512]{2,1,0:T(8,128)S(1)}) fusion(bf16[22,54,512]{2,1,0:T(8,128)(2,1)S(1)} %maximum_select_fusion, f32[512]{0:T(512)S(1)} %bitcast.193, f32[512]{0:T(512)S(1)} %bitcast.195, f32[512]{0:T(512)S(1)} %bitcast.197, f32[512]{0:T(512)S(1)} %bitcast.199, f32[512]{0:T(512)S(1)} %bitcast.201, f32[512]{0:T(512)S(1)} %bitcast.203, ...), kind=kLoop, calls=%fused_computation.83 | loop fusion | flops 57801984 | bytes 40211456 | tf_op jit(solution)/shard_map/reduce_sum | solution.py:90
  97.5 1.8 fusion.12
  99.4 2.9 fusion.33
  103.3 5.2 fusion.6
  108.6 1.7 copy-done.55
  110.3 1.8 fusion.43
  112.2 3.9 pad_maximum_fusion
  116.0 9.3 copy.29
  125.4 4.4 fusion.34
  132.5 4.3 collective-permute-done.9
  136.9 1.6 collective-permute-done.10
  138.7 12.6 %collective-permute-start.12 = (bf16[22,3,512]{2,1,0:T(4,128)(2,1)S(1)}, bf16[22,3,512]{2,1,0:T(4,128)(2,1)S(1)}, u32[]{:S(2)}, u32[]{:S(2)}) collective-permute-start(bf16[22,3,512]{2,1,0:T(4,128)(2,1)S(1)} %get-tuple-element.25), channel_id=1, source_target_pairs={{1,0},{2,1},{3,2},{4,3},{5,4},{6,5},{7,6},{8,7},{9,8},{10,9},{11,1... | collective-permute-start | bytes 202760 | tf_op jit(solution)/shard_map/ppermute | solution.py:26
  151.3 5.9 fusion.14
  158.3 12.3 %fusion.22 = bf16[1,16,48,512]{3,2,1,0:T(8,128)(2,1)} fusion(bf16[22,54,512]{2,1,0:T(8,128)(2,1)S(1)} %maximum_select_fusion.1, f32[512]{0:T(512)S(1)} %bitcast.194, f32[512]{0:T(512)S(1)} %bitcast.196, f32[512]{0:T(512)S(1)} %bitcast.198, f32[512]{0:T(512)S(1)} %bitcast.200, f32[512]{0:T(512)S(1)} %bitcast.202, f32[512]{0:T(512)S(1)} %bitcast.204, ...), kind=kLoop, calls=%fused_computation.35 | loop fusion | flops 58589184 | bytes 40208384 | tf_op jit(solution)/shard_map/broadcast_in_dim | solution.py:128
  170.5 786.4 %reduce-scatter.4.cloned.1.call-done = f32[16,1024]{1,0:T(8,128)} async-done(((f32[2048,1024]{1,0:T(8,128)}), f32[16,1024]{1,0:T(8,128)}) %reduce-scatter.4.cloned.1.call-update) | async-done | bytes 65552
  (162 shorter events, 21.8 us)
Async XLA Ops:
  7.2 90.3 %copy-start = (bf16[1,2048,512]{2,1,0:T(8,128)(2,1)S(1)}, bf16[1,2048,512]{2,1,0:T(8,128)(2,1)}, u32[]{:S(2)}) copy-start(bf16[1,2048,512]{2,1,0:T(8,128)(2,1)} %param.13) | copy-start | bytes 6291460
  7.2 949.7 %reduce-scatter.4.cloned.1.call-start = ((), (), s32[]{:S(2)}) async-start(), calls=%async_computation.1 | async-start | bytes 8454144
  8.4 8.1 collective-permute-start
  16.5 7.6 collective-permute-start.2
  18.4 12.4 %collective-permute-start.1 = (bf16[1,1,16,48,8]{4,3,2,1,0:T(8,128)(2,1)S(1)}, bf16[1,1,16,48,8]{4,3,2,1,0:T(8,128)(2,1)S(1)}, u32[]{:S(2)}, u32[]{:S(2)}) collective-permute-start(bf16[1,1,16,48,8]{4,3,2,1,0:T(8,128)(2,1)S(1)} %bitcast.147), channel_id=1, source_target_pairs={{0,32},{32,64},{64,96},{96,0},{1,33},{33,65},{65,97},{97,1},{2,34}... | collective-permute-start | bytes 36872 | tf_op jit(solution)/shard_map/ppermute | solution.py:23
  31.0 11.7 %collective-permute-start.4 = (bf16[3,1,16,48,8]{3,4,2,1,0:T(8,128)(2,1)S(1)}, bf16[3,1,16,48,8]{3,4,2,1,0:T(8,128)(2,1)S(1)}, u32[]{:S(2)}, u32[]{:S(2)}) collective-permute-start(bf16[3,1,16,48,8]{3,4,2,1,0:T(8,128)(2,1)S(1)} %pad_maximum_fusion.5), channel_id=1, source_target_pairs={{1,0},{2,1},{3,2},{4,3},{5,4},{6,5},{7,6},{8,7},{9,8},{10,9},{11,1... | collective-permute-start | bytes 110600 | tf_op jit(solution)/shard_map/ppermute | solution.py:26
  40.2 14.5 %collective-permute-start.3 = (bf16[3,1,16,48,8]{3,4,2,1,0:T(8,128)(2,1)S(1)}, bf16[3,1,16,48,8]{3,4,2,1,0:T(8,128)(2,1)}, u32[]{:S(2)}, u32[]{:S(2)}) collective-permute-start(bf16[3,1,16,48,8]{3,4,2,1,0:T(8,128)(2,1)S(1)} %pad_maximum_fusion.5), channel_id=1, source_target_pairs={{0,1},{1,2},{2,3},{3,4},{4,5},{5,6},{6,7},{7,8},{8,9},{9,10},{10,1... | collective-permute-start | bytes 110600 | tf_op jit(solution)/shard_map/ppermute | solution.py:23
  62.2 6.0 collective-permute-start.5
  63.1 6.3 collective-permute-start.6
  69.6 14.4 %copy-start.12 = (f32[1,1,512]{2,1,0:T(1,128)S(1)}, f32[1,1,512]{2,1,0:T(1,128)}, u32[]{:S(2)}) copy-start(f32[1,1,512]{2,1,0:T(1,128)} %get-tuple-element.52) | copy-start | bytes 6148
  69.6 14.4 %copy-start.13 = (f32[1,1,512]{2,1,0:T(1,128)S(1)}, f32[1,1,512]{2,1,0:T(1,128)}, u32[]{:S(2)}) copy-start(f32[1,1,512]{2,1,0:T(1,128)} %get-tuple-element.53) | copy-start | bytes 6148
  69.6 14.4 %copy-start.14 = (f32[1,1,512]{2,1,0:T(1,128)S(1)}, f32[1,1,512]{2,1,0:T(1,128)}, u32[]{:S(2)}) copy-start(f32[1,1,512]{2,1,0:T(1,128)} %get-tuple-element.54) | copy-start | bytes 6148
  69.6 14.4 %copy-start.15 = (f32[1,1,512]{2,1,0:T(1,128)S(1)}, f32[1,1,512]{2,1,0:T(1,128)}, u32[]{:S(2)}) copy-start(f32[1,1,512]{2,1,0:T(1,128)} %get-tuple-element.55) | copy-start | bytes 6148
  69.6 14.4 %copy-start.16 = (f32[1,1,512]{2,1,0:T(1,128)S(1)}, f32[1,1,512]{2,1,0:T(1,128)}, u32[]{:S(2)}) copy-start(f32[1,1,512]{2,1,0:T(1,128)} %get-tuple-element.56) | copy-start | bytes 6148
  69.6 14.4 %copy-start.17 = (f32[1,1,512]{2,1,0:T(1,128)S(1)}, f32[1,1,512]{2,1,0:T(1,128)}, u32[]{:S(2)}) copy-start(f32[1,1,512]{2,1,0:T(1,128)} %get-tuple-element.57) | copy-start | bytes 6148
  69.6 14.4 %copy-start.18 = (f32[1,1,512]{2,1,0:T(1,128)S(1)}, f32[1,1,512]{2,1,0:T(1,128)}, u32[]{:S(2)}) copy-start(f32[1,1,512]{2,1,0:T(1,128)} %get-tuple-element.58) | copy-start | bytes 6148
  69.6 14.4 %copy-start.19 = (f32[1,1,512]{2,1,0:T(1,128)S(1)}, f32[1,1,512]{2,1,0:T(1,128)}, u32[]{:S(2)}) copy-start(f32[1,1,512]{2,1,0:T(1,128)} %get-tuple-element.59) | copy-start | bytes 6148
  69.7 14.4 %copy-start.20 = (f32[1,1,512]{2,1,0:T(1,128)S(1)}, f32[1,1,512]{2,1,0:T(1,128)}, u32[]{:S(2)}) copy-start(f32[1,1,512]{2,1,0:T(1,128)} %get-tuple-element.60) | copy-start | bytes 6148
  69.7 14.4 %copy-start.21 = (f32[1,1,512]{2,1,0:T(1,128)S(1)}, f32[1,1,512]{2,1,0:T(1,128)}, u32[]{:S(2)}) copy-start(f32[1,1,512]{2,1,0:T(1,128)} %get-tuple-element.61) | copy-start | bytes 6148
  69.7 14.4 %copy-start.22 = (f32[1,1,512]{2,1,0:T(1,128)S(1)}, f32[1,1,512]{2,1,0:T(1,128)}, u32[]{:S(2)}) copy-start(f32[1,1,512]{2,1,0:T(1,128)} %get-tuple-element.62) | copy-start | bytes 6148
  69.7 14.4 %copy-start.23 = (f32[1,1,512]{2,1,0:T(1,128)S(1)}, f32[1,1,512]{2,1,0:T(1,128)}, u32[]{:S(2)}) copy-start(f32[1,1,512]{2,1,0:T(1,128)} %get-tuple-element.63) | copy-start | bytes 6148
  69.7 14.4 %copy-start.24 = (f32[1,1,512]{2,1,0:T(1,128)S(1)}, f32[1,1,512]{2,1,0:T(1,128)}, u32[]{:S(2)}) copy-start(f32[1,1,512]{2,1,0:T(1,128)} %get-tuple-element.64) | copy-start | bytes 6148
  69.7 14.4 %copy-start.25 = (f32[1,1,512]{2,1,0:T(1,128)S(1)}, f32[1,1,512]{2,1,0:T(1,128)}, u32[]{:S(2)}) copy-start(f32[1,1,512]{2,1,0:T(1,128)} %get-tuple-element.65) | copy-start | bytes 6148
  69.9 12.7 %collective-permute-start.7 = (bf16[22,3,512]{2,1,0:T(4,128)(2,1)S(1)}, bf16[22,3,512]{2,1,0:T(4,128)(2,1)S(1)}, u32[]{:S(2)}, u32[]{:S(2)}) collective-permute-start(bf16[22,3,512]{2,1,0:T(4,128)(2,1)S(1)} %get-tuple-element.20), channel_id=1, source_target_pairs={{0,1},{1,2},{2,3},{3,4},{4,5},{5,6},{6,7},{7,8},{8,9},{9,10},{10,1... | collective-permute-start | bytes 202760 | tf_op jit(solution)/shard_map/ppermute | solution.py:23
  70.0 12.6 %collective-permute-start.8 = (bf16[22,3,512]{2,1,0:T(4,128)(2,1)S(1)}, bf16[22,3,512]{2,1,0:T(4,128)(2,1)S(1)}, u32[]{:S(2)}, u32[]{:S(2)}) collective-permute-start(bf16[22,3,512]{2,1,0:T(4,128)(2,1)S(1)} %get-tuple-element.21), channel_id=1, source_target_pairs={{1,0},{2,1},{3,2},{4,3},{5,4},{6,5},{7,6},{8,7},{9,8},{10,9},{11,1... | collective-permute-start | bytes 202760 | tf_op jit(solution)/shard_map/ppermute | solution.py:26
  129.8 21.4 %copy-start.54 = (bf16[1,2048,512]{2,1,0:T(8,128)(2,1)S(1)}, bf16[1,2048,512]{2,1,0:T(8,128)(2,1)}, u32[]{:S(2)}) copy-start(bf16[1,2048,512]{2,1,0:T(8,128)(2,1)} %param.14) | copy-start | bytes 6291460
  130.4 20.9 %copy-start.6 = (bf16[1,16,48,512]{3,2,1,0:T(8,128)(2,1)S(1)}, bf16[1,16,48,512]{3,2,1,0:T(8,128)(2,1)}, u32[]{:S(2)}) copy-start(bf16[1,16,48,512]{3,2,1,0:T(8,128)(2,1)} %param.9) | copy-start | bytes 2359300
  130.4 20.9 %copy-start.50 = (f32[768]{0:T(1024)S(1)}, f32[768]{0:T(1024)}, u32[]{:S(2)}) copy-start(f32[768]{0:T(1024)} %copy-done.49) | copy-start | bytes 9220
  130.4 6.4 collective-permute-start.9
  131.6 6.9 collective-permute-start.10
  138.6 18.6 %collective-permute-start.11 = (bf16[22,3,512]{2,1,0:T(4,128)(2,1)S(1)}, bf16[22,3,512]{2,1,0:T(4,128)(2,1)S(1)}, u32[]{:S(2)}, u32[]{:S(2)}) collective-permute-start(bf16[22,3,512]{2,1,0:T(4,128)(2,1)S(1)} %get-tuple-element.24), channel_id=1, source_target_pairs={{0,1},{1,2},{2,3},{3,4},{4,5},{5,6},{6,7},{7,8},{8,9},{9,10},{10,1... | collective-permute-start | bytes 202760 | tf_op jit(solution)/shard_map/ppermute | solution.py:23
  138.7 18.5 %collective-permute-start.12 = (bf16[22,3,512]{2,1,0:T(4,128)(2,1)S(1)}, bf16[22,3,512]{2,1,0:T(4,128)(2,1)S(1)}, u32[]{:S(2)}, u32[]{:S(2)}) collective-permute-start(bf16[22,3,512]{2,1,0:T(4,128)(2,1)S(1)} %get-tuple-element.25), channel_id=1, source_target_pairs={{1,0},{2,1},{3,2},{4,3},{5,4},{6,5},{7,6},{8,7},{9,8},{10,9},{11,1... | collective-permute-start | bytes 202760 | tf_op jit(solution)/shard_map/ppermute | solution.py:26
  (38 other events, 392.0 us)
Sparse Core Ops, SparseCore 0:
  125.5 831.3 reduce-scatter.3
where the time goes:
time: 967 us; the launch traced here: 966 us
  waiting for transfers between devices  823 us (85%)
  other arithmetic  38.7 us (4%)
  starting transfers between devices  38.6 us (4%)
  local copies, waits for them, and re-layouts  29 us (3%)
  matrix products  22.1 us (2%)
  between operations  15 us (2%)
    unnamed x2, waiting for transfers between devices  786 us
    ppermute x6, starting transfers between devices, extended(): lax.ppermute(lax.slice_in_dim(block, 0, width, axis=dim), axis, backward)  36 us
    ppermute x6, waiting for transfers between devices, extended(): lax.ppermute(lax.slice_in_dim(block, block.shape[dim] - width, None, axis...  27.5 us
  transfers between devices with their start and end apart: 14, of which 10 were waited for; matrix products, arithmetic and copies ran while one was open for 4% of the time, Pallas kernels for 0%

commit v1 on v0

v1 whole, which is shorter than its diff:
```python
import functools

import jax
import jax.numpy as jnp
from jax import lax
from jax.experimental import pallas as pl
from jax.experimental.pallas import tpu as pltpu
from jax.sharding import PartitionSpec as P

Q = 8
EPS = 1e-06
BF = jnp.bfloat16
F32 = jnp.float32
ROWS, COLS, CH, LANES = 16, 48, 512, 128
CELLS = ROWS * COLS
BLOCKS = CH // LANES
RIM = 3
TAPS = 7
LEFT = 8
PAD_ROWS, PAD_COLS = ROWS + 2 * RIM, 64
HALF = 1024
PART = 256
GELU_A = 0.7978845608028654
GELU_B = 0.044715 * GELU_A


def shape(dims, dtype):
    return jax.ShapeDtypeStruct(dims, dtype)


def run(kernel, name, outs, *args, smem=0, scratch=(), flops=0, moved=1 << 20, views=None, room=4):
    views = views or {}
    in_specs = [
        pl.BlockSpec(memory_space=pltpu.SMEM)
        if at < smem
        else views.get(at, pl.BlockSpec(memory_space=pltpu.VMEM))
        for at in range(len(args))
    ]
    return pl.pallas_call(
        kernel,
        out_shape=outs,
        grid=(1,),
        in_specs=in_specs,
        out_specs=[pl.BlockSpec(memory_space=pltpu.VMEM)] * len(outs),
        scratch_shapes=list(scratch),
        compiler_params=pltpu.CompilerParams(vmem_limit_bytes=room << 20),
        cost_estimate=pl.CostEstimate(flops=flops, bytes_accessed=moved, transcendentals=0),
        name=name,
    )(*args)


def lon_is_even():
    return lax.rem(lax.axis_index("lon"), 2) == 0


def cols_into(packed, row, cells, first):
    packed[3 * row : 3 * row + 3, :] = cells[first : first + 3, :]


def by_parity(even, a, b):
    return jnp.where(even, a, b)


def export_kernel(state_ref, taps_ref, out_ref, top_ref, bottom_ref):
    top_ref[...] = state_ref[0:RIM]
    bottom_ref[...] = state_ref[ROWS - RIM :]
    cells = state_ref[:, :, 0:LANES].reshape(CELLS, LANES).astype(F32)
    out_ref[...] = jnp.concatenate(
        [cells[at * LANES : (at + 1) * LANES].T[:Q] for at in range(CELLS // LANES)], axis=0
    ).astype(BF)


def lon_pack_kernel(state_ref, fields_ref, one_ref, two_ref, left, right):
    for row in range(ROWS):
        cols_into(left, row, state_ref[row, 0:16, LANES:].astype(F32), 0)
        cols_into(right, row, state_ref[row, 32:48, LANES:].astype(F32), 13)
    even = lon_is_even()
    one_ref[:, LANES:] = by_parity(even, right[...], left[...]).astype(BF)
    two_ref[:, LANES:] = by_parity(even, left[...], right[...]).astype(BF)
    one_ref[:, :LANES] = fields_ref[...]
    two_ref[:, :LANES] = fields_ref[...]


def sides(one_ref, two_ref):
    even = lon_is_even()
    one, two = one_ref[...].astype(F32), two_ref[...].astype(F32)
    return by_parity(even, two, one), by_parity(even, one, two)


def lat_pack_kernel(fields_ref, one_ref, two_ref, top_ref, bottom_ref, up_ref, down_ref, hold):
    left, right = sides(one_ref, two_ref)
    hold[0:48, 0:128] = fields_ref[...].astype(F32)
    hold[0:48, 128:256] = left[:, :LANES]
    hold[0:48, 256:384] = right[:, :LANES]
    hold[64:80, :] = jnp.zeros((16, 384), F32)
    for out_ref, at in ((up_ref, 0), (down_ref, 39)):
        hold[48:57, :] = left[at : at + 9, LANES:]
        hold[57:66, :] = right[at : at + 9, LANES:]
        out_ref[...] = hold[...].astype(BF)


def import_kernel(
    source_ref, state_ref, weight_ref, fields_ref, one_ref, two_ref, above_ref, below_ref,
    forced_ref, send_one_ref, send_two_ref, tiles, cells, left, right, flat,
):
    lat, lon = lax.axis_index("lat"), lax.axis_index("lon")
    for row in range(ROWS):
        flat[0:4, row * COLS : (row + 1) * COLS] = weight_ref[row]
    places = []
    for pair in range(4):
        source = source_ref[pair]
        lat_step = source // 32 - lat + 1
        lon_step = lax.rem(lax.rem(source, 32) - lon + 33, 32)
        places.append(jnp.clip(lat_step * 3 + lon_step, 0, 8))
    lon_left, lon_right = sides(one_ref, two_ref)
    tiles[3] = lon_left[:, :LANES]
    tiles[4] = fields_ref[...].astype(F32)
    tiles[5] = lon_right[:, :LANES]
    for at, ref in ((0, above_ref), (6, below_ref)):
        tiles[at + 1] = ref[0:48, 0:128].astype(F32)
        tiles[at] = ref[0:48, 128:256].astype(F32)
        tiles[at + 2] = ref[0:48, 256:384].astype(F32)
    state = state_ref[:, :, 0:LANES].reshape(CELLS, LANES).astype(F32)
    for at in range(CELLS // LANES):
        running = jnp.zeros((Q, LANES), F32)
        for pair in range(4):
            weight = flat[pair : pair + 1, at * LANES : (at + 1) * LANES]
            running = running + weight * tiles[places[pair], at * Q : (at + 1) * Q, :]
        wide = jnp.concatenate(
            [jnp.zeros((Q, LANES), F32), running, jnp.zeros((LANES - 2 * Q, LANES), F32)], axis=0
        )
        cells[at * LANES : (at + 1) * LANES, :] = state[at * LANES : (at + 1) * LANES] + wide.T
    forced_ref[...] = cells[...].astype(BF)
    for row in range(ROWS):
        start = row * COLS
        left[3 * row : 3 * row + 3, :] = cells[start : start + 3, :]
        right[3 * row : 3 * row + 3, :] = cells[start + 45 : start + 48, :]
    even = lon_is_even()
    send_one_ref[...] = by_parity(even, right[...], left[...]).astype(BF)
    send_two_ref[...] = by_parity(even, left[...], right[...]).astype(BF)


def rim_pack_kernel(cells_ref, one_ref, two_ref, after_ref, up_ref, down_ref, hold):
    left, right = sides(one_ref, two_ref)
    width = hold.shape[1]
    hold[16:32, :] = jnp.zeros((16, width), F32)
    for out_ref, first, at in ((up_ref, 0, 0), (down_ref, CELLS - 144, 39)):
        out_ref[0:144, :] = cells_ref[first : first + 144, :]
        hold[0:9, :] = left[at : at + 9]
        hold[9:18, :] = right[at : at + 9]
        out_ref[144:176, :] = hold[...].astype(BF)


def spread_taps(spread, kernel_ref, lane_from, blocks, flipped):
    for at in range(blocks):
        for tap in range(TAPS * TAPS):
            from_tap = TAPS * TAPS - 1 - tap if flipped else tap
            spread[at, tap] = jnp.broadcast_to(kernel_ref[pl.ds(BLOCKS * from_tap + lane_from + at, 1), :], (8, LANES))


def fill_rows(pad, at, top, middle, bottom):
    pad[at, 0:RIM, LEFT : LEFT + COLS, :] = top
    pad[at, RIM : RIM + ROWS, LEFT : LEFT + COLS, :] = middle
    pad[at, RIM + ROWS :, LEFT : LEFT + COLS, :] = bottom


def fill_sides(pad, at, left, right, above, below):
    for row in range(PAD_ROWS):
        if row < RIM:
            one = above[3 * row : 3 * row + 3]
            two = above[9 + 3 * row : 12 + 3 * row]
        elif row < RIM + ROWS:
            one = left[3 * (row - RIM) : 3 * (row - RIM) + 3]
            two = right[3 * (row - RIM) : 3 * (row - RIM) + 3]
        else:
            low = row - RIM - ROWS
            one = below[3 * low : 3 * low + 3]
            two = below[9 + 3 * low : 12 + 3 * low]
        pad[at, row, LEFT - RIM : LEFT, :] = one
        pad[at, row, LEFT + COLS : LEFT + COLS + RIM, :] = two


def convolve(pad, spread, at, emit):
    for chunk in range(3):
        sums = {}
        for row in range(PAD_ROWS):
            first = chunk * 16 + LEFT - RIM
            window = [
                pad[at, row, first + shift : first + shift + 16, :].reshape(2, 8, LANES)
                for shift in range(TAPS)
            ]
            for off in range(TAPS):
                out_row = row - off
                if 0 <= out_row < ROWS:
                    part = window[0] * spread[at, off * TAPS][None]
                    for shift in range(1, TAPS):
                        part = part + window[shift] * spread[at, off * TAPS + shift][None]
                    sums[out_row] = part if off == 0 else sums[out_row] + part
            if row >= TAPS - 1:
                out_row = row - (TAPS - 1)
                emit(out_row, chunk * 16, sums.pop(out_row).reshape(16, LANES))


def conv_wide_kernel(
    state_ref, one_ref, two_ref, top_ref, bottom_ref, above_ref, below_ref, kernel_ref,
    upstream_ref, mask_ref, hidden_ref, update_ref, keep_ref, pad, spread,
):
    left, right = sides(one_ref, two_ref)
    above = above_ref[48:80, :].astype(F32)
    below = below_ref[48:80, :].astype(F32)
    spread_taps(spread, kernel_ref, 1, 3, False)
    for at in range(3):
        wide = slice((at + 1) * LANES, (at + 2) * LANES)
        thin = slice(at * LANES, (at + 1) * LANES)
        fill_rows(
            pad, at, top_ref[:, :, wide].astype(F32), state_ref[:, :, wide].astype(F32),
            bottom_ref[:, :, wide].astype(F32),
        )
        fill_sides(pad, at, left[:, wide], right[:, wide], above[:, thin], below[:, thin])

    def one_block(at, carry):
        def emit(row, col, value):
            hidden_ref[at, row, col : col + 16, :] = value

        convolve(pad, spread, at, emit)
        return carry

    lax.fori_loop(0, 3, one_block, 0)
    mask = jnp.where(lax.axis_index("group") == 1, mask_ref[...].astype(F32), 1.0).T
    for row in range(ROWS):
        rows = slice(row * COLS, (row + 1) * COLS)
        keep_ref[rows, :] = jnp.broadcast_to(mask[:, row : row + 1], (COLS, LANES))

    def one_lane_block(at, carry):
        lanes = pl.ds(pl.multiple_of(at * LANES, LANES), LANES)
        update_ref[:, lanes] = (keep_ref[...] * upstream_ref[:, lanes].astype(F32)).astype(BF)
        return carry

    lax.fori_loop(0, BLOCKS, one_lane_block, 0)


def conv_norm_kernel(
    forced_ref, one_ref, two_ref, above_ref, below_ref, kernel_ref, hidden_ref, gain_ref,
    normed_ref, hat_ref, inv_ref, pad, spread, first,
):
    left, right = sides(one_ref, two_ref)
    above, below = above_ref[...].astype(F32), below_ref[...].astype(F32)
    spread_taps(spread, kernel_ref, 0, 1, False)
    fill_rows(
        pad, 0, above[0:144].reshape(RIM, COLS, LANES),
        forced_ref[...].astype(F32).reshape(ROWS, COLS, LANES), below[0:144].reshape(RIM, COLS, LANES),
    )
    fill_sides(pad, 0, left, right, above[144:176], below[144:176])

    def emit(row, col, value):
        first[row, col : col + 16, :] = value

    convolve(pad, spread, 0, emit)

    def one_row(row, carry):
        parts = [first[row]] + [hidden_ref[at, row] for at in range(3)]
        centre = jnp.sum(sum(parts[1:], parts[0]), axis=-1, keepdims=True) * (1.0 / CH)
        parts = [part - centre for part in parts]
        squares = [part * part for part in parts]
        variance = jnp.sum(sum(squares[1:], squares[0]), axis=-1, keepdims=True) * (1.0 / CH)
        inv = lax.rsqrt(variance + EPS)
        inv_ref[row] = jnp.broadcast_to(inv, (COLS, LANES))
        for at in range(BLOCKS):
            lanes = slice(at * LANES, (at + 1) * LANES)
            hat = parts[at] * inv
            hat_ref[row, :, lanes] = hat
            normed_ref[row, :, lanes] = (hat * gain_ref[:, lanes]).astype(BF)
        return carry

    lax.fori_loop(0, ROWS, one_row, 0)


def dot(a, b, left, right):
    return lax.dot_general(a, b, (((left,), (right,)), ((), ())), preferred_element_type=F32)


def along(axis):
    lon = lax.axis_index("lon")
    if axis == "x":
        return lax.rem(lon, 4)
    if axis == "y":
        return lon // 8
    return lax.rem(lon // 4, 2) * 4 + lax.axis_index("lat")


def mlp_kernel(
    normed_ref, update_ref, w_in_ref, w_out_ref,
    grad0_ref, grad1_ref, grad2_ref, grad3_ref, act_ref, pre_ref, w_in_out_ref, w_out_out_ref,
    *, by_x,
):
    normed = normed_ref[...]
    update = update_ref[...]
    for step, grad_ref in enumerate((grad0_ref, grad1_ref, grad2_ref, grad3_ref)):
        chunk = lax.rem(along("x" if by_x else "y") + step, 4)
        first = w_in_ref[0, :, chunk].reshape(PART, CH)
        second = w_out_ref[0, :, chunk].reshape(PART, CH)
        mine = slice(step * PART, (step + 1) * PART)
        w_in_out_ref[mine, :] = first
        w_out_out_ref[mine, :] = second
        value = dot(normed, first, 1, 1)
        square = value * value
        bent = jnp.tanh(value * (GELU_A + GELU_B * square))
        cdf = 0.5 + 0.5 * bent
        act = (value * cdf).astype(BF)
        slope = cdf + (0.5 * value) * (1.0 - bent * bent) * (GELU_A + 3.0 * GELU_B * square)
        pre = (dot(update, second, 1, 1) * slope).astype(BF)
        act_ref[:, mine] = act
        pre_ref[:, mine] = pre
        grad_ref[:, :CH] = dot(pre, normed, 0, 0).astype(BF)
        grad_ref[:, CH:] = dot(act, update, 0, 0).astype(BF)


def finish_kernel(
    act_a_ref, act_b_ref, pre_a_ref, pre_b_ref, w_in_a_ref, w_in_b_ref, w_out_a_ref, w_out_b_ref,
    state_ref, keep_ref, gain_ref, hat_ref, inv_ref,
    advanced_ref, d_hidden_ref, one_ref, two_ref, wide, left, right,
):
    wide[...] = dot(act_a_ref[...], w_out_a_ref[...], 1, 0) + dot(act_b_ref[...], w_out_b_ref[...], 1, 0)
    for at in range(BLOCKS):
        lanes = slice(at * LANES, (at + 1) * LANES)
        advanced_ref[:, lanes] = (state_ref[:, lanes].astype(F32) + keep_ref[...] * wide[:, lanes]).astype(BF)
    wide[...] = dot(pre_a_ref[...], w_in_a_ref[...], 1, 0) + dot(pre_b_ref[...], w_in_b_ref[...], 1, 0)

    def one_row(row, carry):
        rows = pl.ds(pl.multiple_of(row * COLS, COLS), COLS)
        hat = hat_ref[rows, :]
        scaled = wide[rows, :] * gain_ref[...]
        plain = jnp.sum(scaled, axis=-1, keepdims=True) * (1.0 / CH)
        mixed = jnp.sum(scaled * hat, axis=-1, keepdims=True) * (1.0 / CH)
        back = inv_ref[rows, 0:1] * (scaled - plain - hat * mixed)
        wide[rows, :] = back
        d_hidden_ref[rows, :] = back.astype(BF)
        return carry

    lax.fori_loop(0, ROWS, one_row, 0)
    for row in range(ROWS):
        start = row * COLS
        left[3 * row : 3 * row + 3, :] = wide[start : start + 3, :]
        right[3 * row : 3 * row + 3, :] = wide[start + 45 : start + 48, :]
    even = lon_is_even()
    one_ref[...] = by_parity(even, right[...], left[...]).astype(BF)
    two_ref[...] = by_parity(even, left[...], right[...]).astype(BF)


def conv_back_kernel(
    d_hidden_ref, one_ref, two_ref, above_ref, below_ref, kernel_ref, upstream_ref,
    out_ref, pad, spread, held,
):
    left, right = sides(one_ref, two_ref)
    spread_taps(spread, kernel_ref, 0, BLOCKS, True)
    for at in range(BLOCKS):
        lanes = slice(at * LANES, (at + 1) * LANES)
        above, below = above_ref[:, lanes].astype(F32), below_ref[:, lanes].astype(F32)
        fill_rows(
            pad, at, above[0:144].reshape(RIM, COLS, LANES),
            d_hidden_ref[:, lanes].astype(F32).reshape(ROWS, COLS, LANES),
            below[0:144].reshape(RIM, COLS, LANES),
        )
        fill_sides(pad, at, left[:, lanes], right[:, lanes], above[144:176], below[144:176])

    def one_block(at, carry):
        def emit(row, col, value):
            held[at, row, col : col + 16, :] = value

        convolve(pad, spread, at, emit)
        return carry

    lax.fori_loop(0, BLOCKS, one_block, 0)
    for at in range(BLOCKS):
        lanes = slice(at * LANES, (at + 1) * LANES)
        out_ref[:, :, lanes] = (upstream_ref[:, :, lanes].astype(F32) + held[at]).astype(BF)


def sum_refs(refs):
    total = refs[0][...].astype(F32)
    for ref in refs[1:]:
        total = total + ref[...].astype(F32)
    return total


def sum_four_kernel(a, b, c, d, out0, out1, out2, out3, hold, *, by_x):
    hold[...] = sum_refs((a, b, c, d)).astype(BF).reshape(hold.shape)
    for step, out in enumerate((out0, out1, out2, out3)):
        chunk = lax.rem(along("y" if by_x else "x") + step, 4)
        if by_x:
            out[...] = hold[:, chunk].reshape(out.shape)
        else:
            out[...] = hold[:, :, chunk].reshape(out.shape)


def sum_eight_kernel(*refs):
    ins, outs, hold = refs[:8], refs[8:16], refs[16]
    hold[0:4] = sum_refs(ins[:4]).astype(BF).reshape(4, 16, 2 * CH)
    hold[4:8] = sum_refs(ins[4:]).astype(BF).reshape(4, 16, 2 * CH)
    for step, out in enumerate(outs):
        at = lax.rem(along("z") + step, 8)
        out[...] = hold[lax.rem(at, 4) * 2 + at // 4]


def sum_last_kernel(*refs):
    total = sum_refs(refs[:8])
    refs[8][...] = total[:, :CH]
    refs[9][...] = total[:, CH:]


def ring(axis):
    if axis == "x":
        lines = [[(i, a, b) for i in range(4)] for a in range(4) for b in range(8)]
    elif axis == "y":
        lines = [[(a, i, b) for i in range(4)] for a in range(4) for b in range(8)]
    else:
        lines = [[(a, b, i) for i in range(8)] for a in range(4) for b in range(4)]
    return [[(z % 4) * 32 + y * 8 + (z // 4) * 4 + x for x, y, z in line] for line in lines]


def around(pieces, axis):
    groups = ring(axis)
    count = len(groups[0])
    got = [pieces[0]]
    for step in range(1, count):
        pairs = [(g[i], g[(i + step) % count]) for g in groups for i in range(count)]
        got.append(lax.ppermute(pieces[step], ("lat", "lon"), pairs))
    return got


def swap_lon(one, two):
    pairs = [(i, i ^ 1) for i in range(32)]
    other = [(i, (i - 1) % 32 if i % 2 == 0 else (i + 1) % 32) for i in range(32)]
    return lax.ppermute(one, "lon", pairs), lax.ppermute(two, "lon", other)


def swap_lat(up, down):
    above = lax.ppermute(down, "lat", [(i, i + 1) for i in range(3)])
    below = lax.ppermute(up, "lat", [(i + 1, i) for i in range(3)])
    return above, below


def body(
    states, cotangent, depth_kernel, norm_gain, w_in, w_out, source_tiles, regrid_weights, land_mask
):
    vm = pltpu.VMEM
    state = states[0]
    upstream = cotangent[0]
    taps = depth_kernel[0].reshape(TAPS * TAPS * BLOCKS, LANES)
    sources = source_tiles.reshape(4)
    weights = regrid_weights[0].transpose(0, 2, 1)

    mine, top, bottom = run(
        export_kernel, "export", [shape((48, LANES), BF)] + [shape((RIM, COLS, CH), BF)] * 2, state, taps,
        views={1: pl.BlockSpec(memory_space=pl.ANY)},
    )
    fields = lax.ppermute(mine, "group", [(0, 1), (1, 0)])
    top, bottom = swap_lat(top, bottom)
    one, two = run(
        lon_pack_kernel, "lon_pack", [shape((48, CH), BF)] * 2, state, fields,
        scratch=[vm((48, 384), F32)] * 2,
    )
    one, two = swap_lon(one, two)
    up, down = run(
        lat_pack_kernel, "lat_pack", [shape((80, 384), BF)] * 2, fields, one, two, top, bottom,
        scratch=[vm((80, 384), F32)],
    )
    above, below = swap_lat(up, down)
    forced, f_one, f_two = run(
        import_kernel, "import", [shape((CELLS, LANES), BF)] + [shape((48, LANES), BF)] * 2,
        sources, state, weights, fields, one, two, above, below, smem=1,
        scratch=[vm((9, 48, LANES), F32), vm((CELLS, LANES), F32)] + [vm((48, LANES), F32)] * 2
        + [vm((8, CELLS), F32)],
    )
    f_one, f_two = swap_lon(f_one, f_two)
    hidden, update, keep = run(
        conv_wide_kernel, "conv_wide",
        [shape((3, ROWS, COLS, LANES), F32), shape((CELLS, CH), BF), shape((CELLS, LANES), F32)],
        state, one, two, top, bottom, above, below, taps, upstream.reshape(CELLS, CH), land_mask,
        scratch=[vm((3, PAD_ROWS, PAD_COLS, LANES), F32), vm((3, 49, 8, LANES), F32)], moved=8 << 20, room=8,
    )
    f_up, f_down = run(
        rim_pack_kernel, "rim_pack", [shape((176, LANES), BF)] * 2, forced, f_one, f_two, hidden,
        scratch=[vm((32, LANES), F32)], views={3: pl.BlockSpec(memory_space=pl.ANY)},
    )
    f_above, f_below = swap_lat(f_up, f_down)
    normed, hat, inv = run(
        conv_norm_kernel, "conv_norm",
        [shape((ROWS, COLS, CH), BF), shape((ROWS, COLS, CH), F32), shape((ROWS, COLS, LANES), F32)],
        forced, f_one, f_two, f_above, f_below, taps, hidden, norm_gain,
        scratch=[vm((1, PAD_ROWS, PAD_COLS, LANES), F32), vm((1, 49, 8, LANES), F32), vm((ROWS, COLS, LANES), F32)],
        moved=8 << 20, room=6,
    )
    normed = normed.reshape(CELLS, CH)
    hat = hat.reshape(CELLS, CH)
    inv = inv.reshape(CELLS, LANES)

    def half(by_x):
        if by_x:
            dims, block, at = (2, 16, 4, 16, CH), (1, 16, 4, 16, CH), lambda i: (0, 0, 0, 0, 0)
        else:
            dims, block, at = (2, 2, 4, 128, CH), (1, 2, 4, 128, CH), lambda i: (1, 0, 0, 0, 0)
        view = pl.BlockSpec(block, at)
        outs = run(
            functools.partial(mlp_kernel, by_x=by_x), "mlp_x" if by_x else "mlp_y",
            [shape((PART, 2 * CH), BF)] * 4 + [shape((CELLS, HALF), BF)] * 2 + [shape((HALF, CH), BF)] * 2,
            normed, update, w_in[0].reshape(dims), w_out[0].reshape(dims), views={2: view, 3: view}, flops=4 << 30, moved=10 << 20, room=12,
        )
        return outs[:4], outs[4:]

    grads_a, kept_a = half(True)
    grads_a = around(grads_a, "x")
    grads_b, kept_b = half(False)
    grads_b = around(grads_b, "y")
    advanced, d_hidden, d_one, d_two = run(
        finish_kernel, "finish", [shape((CELLS, CH), BF)] * 2 + [shape((48, CH), BF)] * 2,
        kept_a[0], kept_b[0], kept_a[1], kept_b[1], kept_a[2], kept_b[2], kept_a[3], kept_b[3],
        state.reshape(CELLS, CH), keep, norm_gain, hat, inv,
        scratch=[vm((CELLS, CH), F32)] + [vm((48, CH), F32)] * 2, flops=4 << 30, moved=10 << 20, room=12,
    )
    d_one, d_two = swap_lon(d_one, d_two)
    d_up, d_down = run(
        rim_pack_kernel, "rim_pack_back", [shape((176, CH), BF)] * 2, d_hidden, d_one, d_two, d_one,
        scratch=[vm((32, CH), F32)], views={3: pl.BlockSpec(memory_space=pl.ANY)},
    )
    d_above, d_below = swap_lat(d_up, d_down)
    (state_grad,) = run(
        conv_back_kernel, "conv_back", [shape((ROWS, COLS, CH), BF)],
        d_hidden, d_one, d_two, d_above, d_below, taps, upstream,
        scratch=[
            vm((BLOCKS, PAD_ROWS, PAD_COLS, LANES), F32), vm((BLOCKS, 49, 8, LANES), F32),
            vm((BLOCKS, ROWS, COLS, LANES), F32),
        ],
        moved=10 << 20, room=10,
    )
    grads_a = run(
        functools.partial(sum_four_kernel, by_x=True), "sum_x", [shape((64, 2 * CH), BF)] * 4,
        *grads_a, scratch=[vm((2, 4, 32, 2 * CH), BF)],
    )
    grads_a = around(grads_a, "y")
    grads_b = run(
        functools.partial(sum_four_kernel, by_x=False), "sum_y", [shape((64, 2 * CH), BF)] * 4,
        *grads_b, scratch=[vm((2, 2, 4, 16, 2 * CH), BF)],
    )
    grads_b = around(grads_b, "x")
    grads = run(
        sum_eight_kernel, "sum_xy", [shape((16, 2 * CH), BF)] * 8, *grads_a, *grads_b,
        scratch=[vm((8, 16, 2 * CH), BF)],
    )
    grads = around(grads, "z")
    grad_in, grad_out = run(sum_last_kernel, "sum_z", [shape((16, CH), F32)] * 2, *grads)
    return (
        advanced.reshape(1, ROWS, COLS, CH),
        state_grad[None],
        grad_in[None],
        grad_out[None],
    )


def solution(mesh):
    placed = (
        P("group", "lat", "lon", None),
        P("group", "lat", "lon", None),
        P("group", None, None, None),
        P("group", None),
        P("group", None, None),
        P("group", None, None),
        P("group", "lat", "lon", None),
        P("group", "lat", "lon", None),
        P("lat", "lon"),
    )
    return jax.shard_map(
        body,
        mesh=mesh,
        in_specs=placed,
        out_specs=(
            P("group", "lat", "lon", None),
            P("group", "lat", "lon", None),
            P("group", ("lat", "lon"), None),
            P("group", ("lat", "lon"), None),
        ),
        check_vma=False,
    )
```

time: 967 us -> 153 us (0.16)
  the two profiles are of different devices: /device:TPU:32 before, /device:TPU:6 now
where the time goes in v1:
time: 153 us; the launch traced here: 152 us
  starting transfers between devices  93.1 us (61%)
  Pallas kernels  38.5 us (25%)
  waiting for transfers between devices  17.4 us (11%)
    ppermute x19, starting transfers between devices, around(): got.append(lax.ppermute(pieces[step], ('lat', 'lon'), pairs))  50.7 us
    pallas_call x16, Pallas kernels, run(): pl.pallas_call(kernel, out_shape=outs, grid=(1,), in_specs=in_specs, out_...  38.5 us
    ppermute x6, starting transfers between devices, swap_lon(): return (lax.ppermute(one, 'lon', pairs), lax.ppermute(two, 'lon', other))  20.4 us
    ppermute x4, starting transfers between devices, swap_lat(): above = lax.ppermute(down, 'lat', [(i, i + 1) for i in range(3)])  16.5 us
    ppermute x4, starting transfers between devices, swap_lat(): below = lax.ppermute(up, 'lat', [(i + 1, i) for i in range(3)])  5.3 us
    ppermute x19, waiting for transfers between devices, around(): got.append(lax.ppermute(pieces[step], ('lat', 'lon'), pairs))  5.2 us
    ppermute x6, waiting for transfers between devices, swap_lon(): return (lax.ppermute(one, 'lon', pairs), lax.ppermute(two, 'lon', other))  4.47 us
    ppermute x4, waiting for transfers between devices, swap_lat(): below = lax.ppermute(up, 'lat', [(i + 1, i) for i in range(3)])  4.36 us
  transfers between devices with their start and end apart: 34, of which 9 were waited for; matrix products, arithmetic and copies ran while one was open for 0% of the time, Pallas kernels for 18%

profile of v1, /device:TPU:6, one launch (start us, length us, event | category | flops | bytes accessed | tf_op | source)
XLA Modules:
  0.0 152.2 jit_solution(14016794635957174064)
XLA Ops:
  3.0 4.0 %collective-permute-start.3 = (bf16[3,48,512]{2,1,0:T(8,128)(2,1)S(1)}, bf16[3,48,512]{2,1,0:T(8,128)(2,1)S(1)}, u32[]{:S(2)}, u32[]{:S(2)}) collective-permute-start(bf16[3,48,512]{2,1,0:T(8,128)(2,1)S(1)} %get-tuple-element.65), channel_id=1, source_target_pairs={{0,32},{32,64},{64,96},{1,33},{33,65},{65,97},{2,34},{34,66},{66,9... | collective-permute-start | bytes 442376 | tf_op jit(solution)/shard_map/ppermute | solution.py:438
  10.6 6.9 %collective-permute-start.2 = (bf16[48,512]{1,0:T(8,128)(2,1)S(1)}, bf16[48,512]{1,0:T(8,128)(2,1)S(1)}, u32[]{:S(2)}, u32[]{:S(2)}) collective-permute-start(bf16[48,512]{1,0:T(8,128)(2,1)S(1)} %get-tuple-element.64), channel_id=1, source_target_pairs={{0,31},{1,2},{2,1},{3,4},{4,3},{5,6},{6,5},{7,8},{8,7},{9,10},{10,... | collective-permute-start | bytes 147464 | tf_op jit(solution)/shard_map/ppermute | solution.py:434
  17.4 3.2 %collective-permute-done.2.two_ref = bf16[48,512]{1,0:T(8,128)(2,1)S(1)} collective-permute-done((bf16[48,512]{1,0:T(8,128)(2,1)S(1)}, bf16[48,512]{1,0:T(8,128)(2,1)S(1)}, u32[]{:S(2)}, u32[]{:S(2)}) %collective-permute-start.2) | collective-permute-done | bytes 49184 | tf_op jit(solution)/shard_map/ppermute | solution.py:434
  20.7 4.5 %collective-permute-start.5 = (bf16[80,384]{1,0:T(8,128)(2,1)S(1)}, bf16[80,384]{1,0:T(8,128)(2,1)S(1)}, u32[]{:S(2)}, u32[]{:S(2)}) collective-permute-start(bf16[80,384]{1,0:T(8,128)(2,1)S(1)} %get-tuple-element.67), channel_id=1, source_target_pairs={{0,32},{32,64},{64,96},{1,33},{33,65},{65,97},{2,34},{34,66},{66,9... | collective-permute-start | bytes 184328 | tf_op jit(solution)/shard_map/ppermute | solution.py:438
  27.1 4.3 %collective-permute-done.6.below_ref = bf16[80,384]{1,0:T(8,128)(2,1)S(1)} collective-permute-done((bf16[80,384]{1,0:T(8,128)(2,1)S(1)}, bf16[80,384]{1,0:T(8,128)(2,1)S(1)}, u32[]{:S(2)}, u32[]{:S(2)}) %collective-permute-start.6) | collective-permute-done | bytes 61472 | tf_op jit(solution)/shard_map/ppermute | solution.py:439
  32.3 7.1 %collective-permute-start.8 = (bf16[48,128]{1,0:T(8,128)(2,1)S(1)}, bf16[48,128]{1,0:T(8,128)(2,1)S(1)}, u32[]{:S(2)}, u32[]{:S(2)}) collective-permute-start(bf16[48,128]{1,0:T(8,128)(2,1)S(1)} %get-tuple-element.71), channel_id=1, source_target_pairs={{0,31},{1,2},{2,1},{3,4},{4,3},{5,6},{6,5},{7,8},{8,7},{9,10},{10,... | collective-permute-start | bytes 36872 | tf_op jit(solution)/shard_map/ppermute | solution.py:434
  39.5 6.0 %conv_wide.1 = (f32[3,16,48,128]{3,2,1,0:T(8,128)S(1)}, bf16[768,512]{1,0:T(8,128)(2,1)S(1)}, f32[768,128]{1,0:T(8,128)S(1)}) custom-call(bf16[16,48,512]{2,1,0:T(8,128)(2,1)S(1)} %bitcast.22, bf16[48,512]{1,0:T(8,128)(2,1)S(1)} %collective-permute-done.1.one_ref, bf16[48,512]{1,0:T(8,128)(2,1)S(1)} %collective-permute-done.2.two_ref, ...), custom_call_target="tpu_custom_call" | custom-call | bytes 8388608 | tf_op jit(solution)/shard_map/conv_wide/pallas_call | solution.py:39
  45.6 1.4 collective-permute-start.10
  47.0 4.5 %collective-permute-start.9 = (bf16[176,128]{1,0:T(8,128)(2,1)S(1)}, bf16[176,128]{1,0:T(8,128)(2,1)S(1)}, u32[]{:S(2)}, u32[]{:S(2)}) collective-permute-start(bf16[176,128]{1,0:T(8,128)(2,1)S(1)} %get-tuple-element.73), channel_id=1, source_target_pairs={{0,32},{32,64},{64,96},{1,33},{33,65},{65,97},{2,34},{34,66},{66,9... | collective-permute-start | bytes 135176 | tf_op jit(solution)/shard_map/ppermute | solution.py:438
  51.7 1.6 %collective-permute-done.9.above_ref = bf16[176,128]{1,0:T(8,128)(2,1)S(1)} collective-permute-done((bf16[176,128]{1,0:T(8,128)(2,1)S(1)}, bf16[176,128]{1,0:T(8,128)(2,1)S(1)}, u32[]{:S(2)}, u32[]{:S(2)}) %collective-permute-start.9) | collective-permute-done | bytes 45088 | tf_op jit(solution)/shard_map/ppermute | solution.py:438
  53.3 4.4 %conv_norm.1 = (bf16[16,48,512]{2,1,0:T(8,128)(2,1)S(1)}, f32[16,48,512]{2,1,0:T(8,128)S(1)}, f32[16,48,128]{2,1,0:T(8,128)S(1)}) custom-call(bf16[768,128]{1,0:T(8,128)(2,1)S(1)} %get-tuple-element.69.cells_ref.forced_ref, bf16[48,128]{1,0:T(8,128)(2,1)S(1)} %collective-permute-done.7.one_ref, bf16[48,128]{1,0:T(8,128)(2,1)S(1)} %collective-permute-done.8.two_ref, ...), custom_call_target="tpu_custom_call" | custom-call | bytes 8388608 | tf_op jit(solution)/shard_map/conv_norm/pallas_call | solution.py:39
  57.7 5.0 %mlp_y.1 = (bf16[256,1024]{1,0:T(8,128)(2,1)S(1)}, bf16[256,1024]{1,0:T(8,128)(2,1)S(1)}, bf16[256,1024]{1,0:T(8,128)(2,1)S(1)}, bf16[256,1024]{1,0:T(8,128)(2,1...) custom-call(bf16[768,512]{1,0:T(8,128)(2,1)S(1)} %bitcast.33, ...), custom_call_target="tpu_custom_call" | custom-call | flops 4294967296 | bytes 10485760 | tf_op jit(solution)/shard_map/mlp_y/pallas_call | solution.py:39
  62.8 1.8 %collective-permute-start.21 = (bf16[256,1024]{1,0:T(8,128)(2,1)S(1)}, bf16[256,1024]{1,0:T(8,128)(2,1)S(1)}, u32[]{:S(2)}, u32[]{:S(2)}) collective-permute-start(bf16[256,1024]{1,0:T(8,128)(2,1)S(1)} %get-tuple-element.103), channel_id=1, source_target_pairs={{0,8},{8,16},{16,24},{24,0},{32,40},{40,48},{48,56},{56,32},{64,72... | collective-permute-start | bytes 1572872 | tf_op jit(solution)/shard_map/ppermute | solution.py:427
  64.6 3.1 %collective-permute-start.22 = (bf16[256,1024]{1,0:T(8,128)(2,1)S(1)}, bf16[256,1024]{1,0:T(8,128)(2,1)S(1)}, u32[]{:S(2)}, u32[]{:S(2)}) collective-permute-start(bf16[256,1024]{1,0:T(8,128)(2,1)S(1)} %get-tuple-element.104), channel_id=1, source_target_pairs={{0,16},{8,24},{16,0},{24,8},{32,48},{40,56},{48,32},{56,40},{64,80... | collective-permute-start | bytes 1572872 | tf_op jit(solution)/shard_map/ppermute | solution.py:427
  67.7 2.0 %collective-permute-start.23 = (bf16[256,1024]{1,0:T(8,128)(2,1)S(1)}, bf16[256,1024]{1,0:T(8,128)(2,1)S(1)}, u32[]{:S(2)}, u32[]{:S(2)}) collective-permute-start(bf16[256,1024]{1,0:T(8,128)(2,1)S(1)} %get-tuple-element.105), channel_id=1, source_target_pairs={{0,24},{8,0},{16,8},{24,16},{32,56},{40,32},{48,40},{56,48},{64,88... | collective-permute-start | bytes 1572872 | tf_op jit(solution)/shard_map/ppermute | solution.py:427
  69.7 5.0 %mlp_x.1 = (bf16[256,1024]{1,0:T(8,128)(2,1)S(1)}, bf16[256,1024]{1,0:T(8,128)(2,1)S(1)}, bf16[256,1024]{1,0:T(8,128)(2,1)S(1)}, bf16[256,1024]{1,0:T(8,128)(2,1...) custom-call(bf16[768,512]{1,0:T(8,128)(2,1)S(1)} %bitcast.34, ...), custom_call_target="tpu_custom_call" | custom-call | flops 4294967296 | bytes 10485760 | tf_op jit(solution)/shard_map/mlp_x/pallas_call | solution.py:39
  74.7 3.5 %collective-permute-start.15 = (bf16[256,1024]{1,0:T(8,128)(2,1)S(1)}, bf16[256,1024]{1,0:T(8,128)(2,1)S(1)}, u32[]{:S(2)}, u32[]{:S(2)}) collective-permute-start(bf16[256,1024]{1,0:T(8,128)(2,1)S(1)} %get-tuple-element.95), channel_id=1, source_target_pairs={{0,1},{1,2},{2,3},{3,0},{32,33},{33,34},{34,35},{35,32},{64,65},{6... | collective-permute-start | bytes 1572872 | tf_op jit(solution)/shard_map/ppermute | solution.py:427
  78.2 5.2 %collective-permute-start.17 = (bf16[256,1024]{1,0:T(8,128)(2,1)S(1)}, bf16[256,1024]{1,0:T(8,128)(2,1)S(1)}, u32[]{:S(2)}, u32[]{:S(2)}) collective-permute-start(bf16[256,1024]{1,0:T(8,128)(2,1)S(1)} %get-tuple-element.97), channel_id=1, source_target_pairs={{0,3},{1,0},{2,1},{3,2},{32,35},{33,32},{34,33},{35,34},{64,67},{6... | collective-permute-start | bytes 1572872 | tf_op jit(solution)/shard_map/ppermute | solution.py:427
  83.4 6.2 %finish.1 = (bf16[768,512]{1,0:T(8,128)(2,1)}, bf16[768,512]{1,0:T(8,128)(2,1)S(1)}, bf16[48,512]{1,0:T(8,128)(2,1)S(1)}, bf16[48,512]{1,0:T(8,128)(2,1)S(1)}) custom-call(bf16[768,1024]{1,0:T(8,128)(2,1)S(1)} %get-tuple-element.77.act_a_ref, bf16[768,1024]{1,0:T(8,128)(2,1)S(1)} %get-tuple-element.78.act_b_ref, ...), custom_call_target="tpu_custom_call" | custom-call | flops 4294967296 | bytes 10485760 | tf_op jit(solution)/shard_map/finish/pallas_call | solution.py:39
  90.0 5.1 %collective-permute-start.12 = (bf16[48,512]{1,0:T(8,128)(2,1)S(1)}, bf16[48,512]{1,0:T(8,128)(2,1)S(1)}, u32[]{:S(2)}, u32[]{:S(2)}) collective-permute-start(bf16[48,512]{1,0:T(8,128)(2,1)S(1)} %get-tuple-element.91), channel_id=1, source_target_pairs={{0,31},{1,2},{2,1},{3,4},{4,3},{5,6},{6,5},{7,8},{8,7},{9,10},{10,... | collective-permute-start | bytes 147464 | tf_op jit(solution)/shard_map/ppermute | solution.py:434
  96.8 5.6 %collective-permute-start.24 = (bf16[64,1024]{1,0:T(8,128)(2,1)S(1)}, bf16[64,1024]{1,0:T(8,128)(2,1)S(1)}, u32[]{:S(2)}, u32[]{:S(2)}) collective-permute-start(bf16[64,1024]{1,0:T(8,128)(2,1)S(1)} %get-tuple-element.107), channel_id=1, source_target_pairs={{0,1},{1,2},{2,3},{3,0},{32,33},{33,34},{34,35},{35,32},{64,65},{6... | collective-permute-start | bytes 393224 | tf_op jit(solution)/shard_map/ppermute | solution.py:427
  102.5 1.9 %collective-permute-start.25 = (bf16[64,1024]{1,0:T(8,128)(2,1)S(1)}, bf16[64,1024]{1,0:T(8,128)(2,1)S(1)}, u32[]{:S(2)}, u32[]{:S(2)}) collective-permute-start(bf16[64,1024]{1,0:T(8,128)(2,1)S(1)} %get-tuple-element.108), channel_id=1, source_target_pairs={{0,2},{1,3},{2,0},{3,1},{32,34},{33,35},{34,32},{35,33},{64,66},{6... | collective-permute-start | bytes 393224 | tf_op jit(solution)/shard_map/ppermute | solution.py:427
  104.4 9.1 %collective-permute-start.26 = (bf16[64,1024]{1,0:T(8,128)(2,1)S(1)}, bf16[64,1024]{1,0:T(8,128)(2,1)S(1)}, u32[]{:S(2)}, u32[]{:S(2)}) collective-permute-start(bf16[64,1024]{1,0:T(8,128)(2,1)S(1)} %get-tuple-element.109), channel_id=1, source_target_pairs={{0,3},{1,0},{2,1},{3,2},{32,35},{33,32},{34,33},{35,34},{64,67},{6... | collective-permute-start | bytes 393224 | tf_op jit(solution)/shard_map/ppermute | solution.py:427
  113.5 3.5 %collective-permute-start.13 = (bf16[176,512]{1,0:T(8,128)(2,1)S(1)}, bf16[176,512]{1,0:T(8,128)(2,1)S(1)}, u32[]{:S(2)}, u32[]{:S(2)}) collective-permute-start(bf16[176,512]{1,0:T(8,128)(2,1)S(1)} %get-tuple-element.92), channel_id=1, source_target_pairs={{0,32},{32,64},{64,96},{1,33},{33,65},{65,97},{2,34},{34,66},{66,9... | collective-permute-start | bytes 540680 | tf_op jit(solution)/shard_map/ppermute | solution.py:438
  119.1 3.2 %collective-permute-start.20 = (bf16[64,1024]{1,0:T(8,128)(2,1)S(1)}, bf16[64,1024]{1,0:T(8,128)(2,1)S(1)}, u32[]{:S(2)}, u32[]{:S(2)}) collective-permute-start(bf16[64,1024]{1,0:T(8,128)(2,1)S(1)} %get-tuple-element.101), channel_id=1, source_target_pairs={{0,24},{8,0},{16,8},{24,16},{32,56},{40,32},{48,40},{56,48},{64,88... | collective-permute-start | bytes 393224 | tf_op jit(solution)/shard_map/ppermute | solution.py:427
  122.3 4.3 %collective-permute-done.18.refs_1_ = bf16[64,1024]{1,0:T(8,128)(2,1)S(1)} collective-permute-done((bf16[64,1024]{1,0:T(8,128)(2,1)S(1)}, bf16[64,1024]{1,0:T(8,128)(2,1)S(1)}, u32[]{:S(2)}, u32[]{:S(2)}) %collective-permute-start.18) | collective-permute-done | bytes 131104 | tf_op jit(solution)/shard_map/ppermute | solution.py:427
  127.7 3.0 %collective-permute-start.27 = (bf16[16,1024]{1,0:T(8,128)(2,1)S(1)}, bf16[16,1024]{1,0:T(8,128)(2,1)S(1)}, u32[]{:S(2)}, u32[]{:S(2)}) collective-permute-start(bf16[16,1024]{1,0:T(8,128)(2,1)S(1)} %get-tuple-element.111), channel_id=1, source_target_pairs={{0,32},{32,64},{64,96},{96,4},{4,36},{36,68},{68,100},{100,0},{8,4... | collective-permute-start | bytes 98312 | tf_op jit(solution)/shard_map/ppermute | solution.py:427
  130.7 1.5 %collective-permute-start.28 = (bf16[16,1024]{1,0:T(8,128)(2,1)S(1)}, bf16[16,1024]{1,0:T(8,128)(2,1)S(1)}, u32[]{:S(2)}, u32[]{:S(2)}) collective-permute-start(bf16[16,1024]{1,0:T(8,128)(2,1)S(1)} %get-tuple-element.112), channel_id=1, source_target_pairs={{0,64},{32,96},{64,4},{96,36},{4,68},{36,100},{68,0},{100,32},{8,7... | collective-permute-start | bytes 98312 | tf_op jit(solution)/shard_map/ppermute | solution.py:427
  132.2 6.4 %collective-permute-start.30 = (bf16[16,1024]{1,0:T(8,128)(2,1)S(1)}, bf16[16,1024]{1,0:T(8,128)(2,1)S(1)}, u32[]{:S(2)}, u32[]{:S(2)}) collective-permute-start(bf16[16,1024]{1,0:T(8,128)(2,1)S(1)} %get-tuple-element.114), channel_id=1, source_target_pairs={{0,4},{32,36},{64,68},{96,100},{4,0},{36,32},{68,64},{100,96},{8,1... | collective-permute-start | bytes 98312 | tf_op jit(solution)/shard_map/ppermute | solution.py:427
  138.6 2.7 %collective-permute-start.32 = (bf16[16,1024]{1,0:T(8,128)(2,1)S(1)}, bf16[16,1024]{1,0:T(8,128)(2,1)S(1)}, u32[]{:S(2)}, u32[]{:S(2)}) collective-permute-start(bf16[16,1024]{1,0:T(8,128)(2,1)S(1)} %get-tuple-element.116), channel_id=1, source_target_pairs={{0,68},{32,100},{64,0},{96,32},{4,64},{36,96},{68,4},{100,36},{8,7... | collective-permute-start | bytes 98312 | tf_op jit(solution)/shard_map/ppermute | solution.py:427
  141.3 1.5 collective-permute-start.33
  142.8 8.7 %conv_back.1 = bf16[16,48,512]{2,1,0:T(8,128)(2,1)} custom-call(bf16[768,512]{1,0:T(8,128)(2,1)S(1)} %get-tuple-element.89.cells_ref.d_hidden_ref, bf16[48,512]{1,0:T(8,128)(2,1)S(1)} %collective-permute-done.11.one_ref.after_ref, bf16[48,512]{1,0:T(8,128)(2,1)S(1)} %collective-permute-done.12.two_ref, ...), custom_call_target="tpu_custom_call" | custom-call | bytes 10485760 | tf_op jit(solution)/shard_map/conv_back/pallas_call | solution.py:39
  (72 shorter events, 14.8 us)
Async XLA Ops:
  3.0 17.6 %collective-permute-start.3 = (bf16[3,48,512]{2,1,0:T(8,128)(2,1)S(1)}, bf16[3,48,512]{2,1,0:T(8,128)(2,1)S(1)}, u32[]{:S(2)}, u32[]{:S(2)}) collective-permute-start(bf16[3,48,512]{2,1,0:T(8,128)(2,1)S(1)} %get-tuple-element.65), channel_id=1, source_target_pairs={{0,32},{32,64},{64,96},{1,33},{33,65},{65,97},{2,34},{34,66},{66,9... | collective-permute-start | bytes 442376 | tf_op jit(solution)/shard_map/ppermute | solution.py:438
  7.0 13.6 %collective-permute-start.4 = (bf16[3,48,512]{2,1,0:T(8,128)(2,1)S(1)}, bf16[3,48,512]{2,1,0:T(8,128)(2,1)S(1)}, u32[]{:S(2)}, u32[]{:S(2)}) collective-permute-start(bf16[3,48,512]{2,1,0:T(8,128)(2,1)S(1)} %get-tuple-element.66), channel_id=1, source_target_pairs={{32,0},{64,32},{96,64},{33,1},{65,33},{97,65},{34,2},{66,34},{98,6... | collective-permute-start | bytes 442376 | tf_op jit(solution)/shard_map/ppermute | solution.py:439
  9.6 7.8 %collective-permute-start.1 = (bf16[48,512]{1,0:T(8,128)(2,1)S(1)}, bf16[48,512]{1,0:T(8,128)(2,1)S(1)}, u32[]{:S(2)}, u32[]{:S(2)}) collective-permute-start(bf16[48,512]{1,0:T(8,128)(2,1)S(1)} %get-tuple-element.63), channel_id=1, source_target_pairs={{0,1},{1,0},{2,3},{3,2},{4,5},{5,4},{6,7},{7,6},{8,9},{9,8},{10,11... | collective-permute-start | bytes 147464 | tf_op jit(solution)/shard_map/ppermute | solution.py:434
  10.6 10.1 %collective-permute-start.2 = (bf16[48,512]{1,0:T(8,128)(2,1)S(1)}, bf16[48,512]{1,0:T(8,128)(2,1)S(1)}, u32[]{:S(2)}, u32[]{:S(2)}) collective-permute-start(bf16[48,512]{1,0:T(8,128)(2,1)S(1)} %get-tuple-element.64), channel_id=1, source_target_pairs={{0,31},{1,2},{2,1},{3,4},{4,3},{5,6},{6,5},{7,8},{8,7},{9,10},{10,... | collective-permute-start | bytes 147464 | tf_op jit(solution)/shard_map/ppermute | solution.py:434
  20.7 6.4 %collective-permute-start.5 = (bf16[80,384]{1,0:T(8,128)(2,1)S(1)}, bf16[80,384]{1,0:T(8,128)(2,1)S(1)}, u32[]{:S(2)}, u32[]{:S(2)}) collective-permute-start(bf16[80,384]{1,0:T(8,128)(2,1)S(1)} %get-tuple-element.67), channel_id=1, source_target_pairs={{0,32},{32,64},{64,96},{1,33},{33,65},{65,97},{2,34},{34,66},{66,9... | collective-permute-start | bytes 184328 | tf_op jit(solution)/shard_map/ppermute | solution.py:438
  25.3 6.1 %collective-permute-start.6 = (bf16[80,384]{1,0:T(8,128)(2,1)S(1)}, bf16[80,384]{1,0:T(8,128)(2,1)S(1)}, u32[]{:S(2)}, u32[]{:S(2)}) collective-permute-start(bf16[80,384]{1,0:T(8,128)(2,1)S(1)} %get-tuple-element.68), channel_id=1, source_target_pairs={{32,0},{64,32},{96,64},{33,1},{65,33},{97,65},{34,2},{66,34},{98,6... | collective-permute-start | bytes 184328 | tf_op jit(solution)/shard_map/ppermute | solution.py:439
  32.2 13.3 %collective-permute-start.7 = (bf16[48,128]{1,0:T(8,128)(2,1)S(1)}, bf16[48,128]{1,0:T(8,128)(2,1)S(1)}, u32[]{:S(2)}, u32[]{:S(2)}) collective-permute-start(bf16[48,128]{1,0:T(8,128)(2,1)S(1)} %get-tuple-element.70), channel_id=1, source_target_pairs={{0,1},{1,0},{2,3},{3,2},{4,5},{5,4},{6,7},{7,6},{8,9},{9,8},{10,11... | collective-permute-start | bytes 36872 | tf_op jit(solution)/shard_map/ppermute | solution.py:434
  32.3 13.2 %collective-permute-start.8 = (bf16[48,128]{1,0:T(8,128)(2,1)S(1)}, bf16[48,128]{1,0:T(8,128)(2,1)S(1)}, u32[]{:S(2)}, u32[]{:S(2)}) collective-permute-start(bf16[48,128]{1,0:T(8,128)(2,1)S(1)} %get-tuple-element.71), channel_id=1, source_target_pairs={{0,31},{1,2},{2,1},{3,4},{4,3},{5,6},{6,5},{7,8},{8,7},{9,10},{10,... | collective-permute-start | bytes 36872 | tf_op jit(solution)/shard_map/ppermute | solution.py:434
  47.0 6.2 %collective-permute-start.9 = (bf16[176,128]{1,0:T(8,128)(2,1)S(1)}, bf16[176,128]{1,0:T(8,128)(2,1)S(1)}, u32[]{:S(2)}, u32[]{:S(2)}) collective-permute-start(bf16[176,128]{1,0:T(8,128)(2,1)S(1)} %get-tuple-element.73), channel_id=1, source_target_pairs={{0,32},{32,64},{64,96},{1,33},{33,65},{65,97},{2,34},{34,66},{66,9... | collective-permute-start | bytes 135176 | tf_op jit(solution)/shard_map/ppermute | solution.py:438
  62.8 15.4 %collective-permute-start.21 = (bf16[256,1024]{1,0:T(8,128)(2,1)S(1)}, bf16[256,1024]{1,0:T(8,128)(2,1)S(1)}, u32[]{:S(2)}, u32[]{:S(2)}) collective-permute-start(bf16[256,1024]{1,0:T(8,128)(2,1)S(1)} %get-tuple-element.103), channel_id=1, source_target_pairs={{0,8},{8,16},{16,24},{24,0},{32,40},{40,48},{48,56},{56,32},{64,72... | collective-permute-start | bytes 1572872 | tf_op jit(solution)/shard_map/ppermute | solution.py:427
  64.6 25.1 %collective-permute-start.22 = (bf16[256,1024]{1,0:T(8,128)(2,1)S(1)}, bf16[256,1024]{1,0:T(8,128)(2,1)S(1)}, u32[]{:S(2)}, u32[]{:S(2)}) collective-permute-start(bf16[256,1024]{1,0:T(8,128)(2,1)S(1)} %get-tuple-element.104), channel_id=1, source_target_pairs={{0,16},{8,24},{16,0},{24,8},{32,48},{40,56},{48,32},{56,40},{64,80... | collective-permute-start | bytes 1572872 | tf_op jit(solution)/shard_map/ppermute | solution.py:427
  67.7 22.3 %collective-permute-start.23 = (bf16[256,1024]{1,0:T(8,128)(2,1)S(1)}, bf16[256,1024]{1,0:T(8,128)(2,1)S(1)}, u32[]{:S(2)}, u32[]{:S(2)}) collective-permute-start(bf16[256,1024]{1,0:T(8,128)(2,1)S(1)} %get-tuple-element.105), channel_id=1, source_target_pairs={{0,24},{8,0},{16,8},{24,16},{32,56},{40,32},{48,40},{56,48},{64,88... | collective-permute-start | bytes 1572872 | tf_op jit(solution)/shard_map/ppermute | solution.py:427
  74.7 29.7 %collective-permute-start.15 = (bf16[256,1024]{1,0:T(8,128)(2,1)S(1)}, bf16[256,1024]{1,0:T(8,128)(2,1)S(1)}, u32[]{:S(2)}, u32[]{:S(2)}) collective-permute-start(bf16[256,1024]{1,0:T(8,128)(2,1)S(1)} %get-tuple-element.95), channel_id=1, source_target_pairs={{0,1},{1,2},{2,3},{3,0},{32,33},{33,34},{34,35},{35,32},{64,65},{6... | collective-permute-start | bytes 1572872 | tf_op jit(solution)/shard_map/ppermute | solution.py:427
  78.2 35.3 %collective-permute-start.16 = (bf16[256,1024]{1,0:T(8,128)(2,1)S(1)}, bf16[256,1024]{1,0:T(8,128)(2,1)S(1)}, u32[]{:S(2)}, u32[]{:S(2)}) collective-permute-start(bf16[256,1024]{1,0:T(8,128)(2,1)S(1)} %get-tuple-element.96), channel_id=1, source_target_pairs={{0,2},{1,3},{2,0},{3,1},{32,34},{33,35},{34,32},{35,33},{64,66},{6... | collective-permute-start | bytes 1572872 | tf_op jit(solution)/shard_map/ppermute | solution.py:427
  78.2 38.8 %collective-permute-start.17 = (bf16[256,1024]{1,0:T(8,128)(2,1)S(1)}, bf16[256,1024]{1,0:T(8,128)(2,1)S(1)}, u32[]{:S(2)}, u32[]{:S(2)}) collective-permute-start(bf16[256,1024]{1,0:T(8,128)(2,1)S(1)} %get-tuple-element.97), channel_id=1, source_target_pairs={{0,3},{1,0},{2,1},{3,2},{32,35},{33,32},{34,33},{35,34},{64,67},{6... | collective-permute-start | bytes 1572872 | tf_op jit(solution)/shard_map/ppermute | solution.py:427
  89.7 7.2 %collective-permute-start.11 = (bf16[48,512]{1,0:T(8,128)(2,1)S(1)}, bf16[48,512]{1,0:T(8,128)(2,1)S(1)}, u32[]{:S(2)}, u32[]{:S(2)}) collective-permute-start(bf16[48,512]{1,0:T(8,128)(2,1)S(1)} %get-tuple-element.90), channel_id=1, source_target_pairs={{0,1},{1,0},{2,3},{3,2},{4,5},{5,4},{6,7},{7,6},{8,9},{9,8},{10,11... | collective-permute-start | bytes 147464 | tf_op jit(solution)/shard_map/ppermute | solution.py:434
  90.0 12.5 %collective-permute-start.12 = (bf16[48,512]{1,0:T(8,128)(2,1)S(1)}, bf16[48,512]{1,0:T(8,128)(2,1)S(1)}, u32[]{:S(2)}, u32[]{:S(2)}) collective-permute-start(bf16[48,512]{1,0:T(8,128)(2,1)S(1)} %get-tuple-element.91), channel_id=1, source_target_pairs={{0,31},{1,2},{2,1},{3,4},{4,3},{5,6},{6,5},{7,8},{8,7},{9,10},{10,... | collective-permute-start | bytes 147464 | tf_op jit(solution)/shard_map/ppermute | solution.py:434
  96.8 22.0 %collective-permute-start.24 = (bf16[64,1024]{1,0:T(8,128)(2,1)S(1)}, bf16[64,1024]{1,0:T(8,128)(2,1)S(1)}, u32[]{:S(2)}, u32[]{:S(2)}) collective-permute-start(bf16[64,1024]{1,0:T(8,128)(2,1)S(1)} %get-tuple-element.107), channel_id=1, source_target_pairs={{0,1},{1,2},{2,3},{3,0},{32,33},{33,34},{34,35},{35,32},{64,65},{6... | collective-permute-start | bytes 393224 | tf_op jit(solution)/shard_map/ppermute | solution.py:427
  102.5 16.5 %collective-permute-start.25 = (bf16[64,1024]{1,0:T(8,128)(2,1)S(1)}, bf16[64,1024]{1,0:T(8,128)(2,1)S(1)}, u32[]{:S(2)}, u32[]{:S(2)}) collective-permute-start(bf16[64,1024]{1,0:T(8,128)(2,1)S(1)} %get-tuple-element.108), channel_id=1, source_target_pairs={{0,2},{1,3},{2,0},{3,1},{32,34},{33,35},{34,32},{35,33},{64,66},{6... | collective-permute-start | bytes 393224 | tf_op jit(solution)/shard_map/ppermute | solution.py:427
  104.4 14.7 %collective-permute-start.26 = (bf16[64,1024]{1,0:T(8,128)(2,1)S(1)}, bf16[64,1024]{1,0:T(8,128)(2,1)S(1)}, u32[]{:S(2)}, u32[]{:S(2)}) collective-permute-start(bf16[64,1024]{1,0:T(8,128)(2,1)S(1)} %get-tuple-element.109), channel_id=1, source_target_pairs={{0,3},{1,0},{2,1},{3,2},{32,35},{33,32},{34,33},{35,34},{64,67},{6... | collective-permute-start | bytes 393224 | tf_op jit(solution)/shard_map/ppermute | solution.py:427
  113.5 18.7 %collective-permute-start.13 = (bf16[176,512]{1,0:T(8,128)(2,1)S(1)}, bf16[176,512]{1,0:T(8,128)(2,1)S(1)}, u32[]{:S(2)}, u32[]{:S(2)}) collective-permute-start(bf16[176,512]{1,0:T(8,128)(2,1)S(1)} %get-tuple-element.92), channel_id=1, source_target_pairs={{0,32},{32,64},{64,96},{1,33},{33,65},{65,97},{2,34},{34,66},{66,9... | collective-permute-start | bytes 540680 | tf_op jit(solution)/shard_map/ppermute | solution.py:438
  117.0 21.6 %collective-permute-start.14 = (bf16[176,512]{1,0:T(8,128)(2,1)S(1)}, bf16[176,512]{1,0:T(8,128)(2,1)S(1)}, u32[]{:S(2)}, u32[]{:S(2)}) collective-permute-start(bf16[176,512]{1,0:T(8,128)(2,1)S(1)} %get-tuple-element.93), channel_id=1, source_target_pairs={{32,0},{64,32},{96,64},{33,1},{65,33},{97,65},{34,2},{66,34},{98,6... | collective-permute-start | bytes 540680 | tf_op jit(solution)/shard_map/ppermute | solution.py:439
  118.9 7.7 %collective-permute-start.18 = (bf16[64,1024]{1,0:T(8,128)(2,1)S(1)}, bf16[64,1024]{1,0:T(8,128)(2,1)S(1)}, u32[]{:S(2)}, u32[]{:S(2)}) collective-permute-start(bf16[64,1024]{1,0:T(8,128)(2,1)S(1)} %get-tuple-element.99), channel_id=1, source_target_pairs={{0,8},{8,16},{16,24},{24,0},{32,40},{40,48},{48,56},{56,32},{64,72... | collective-permute-start | bytes 393224 | tf_op jit(solution)/shard_map/ppermute | solution.py:427
  119.0 7.6 %collective-permute-start.19 = (bf16[64,1024]{1,0:T(8,128)(2,1)S(1)}, bf16[64,1024]{1,0:T(8,128)(2,1)S(1)}, u32[]{:S(2)}, u32[]{:S(2)}) collective-permute-start(bf16[64,1024]{1,0:T(8,128)(2,1)S(1)} %get-tuple-element.100), channel_id=1, source_target_pairs={{0,16},{8,24},{16,0},{24,8},{32,48},{40,56},{48,32},{56,40},{64,80... | collective-permute-start | bytes 393224 | tf_op jit(solution)/shard_map/ppermute | solution.py:427
  119.1 8.4 %collective-permute-start.20 = (bf16[64,1024]{1,0:T(8,128)(2,1)S(1)}, bf16[64,1024]{1,0:T(8,128)(2,1)S(1)}, u32[]{:S(2)}, u32[]{:S(2)}) collective-permute-start(bf16[64,1024]{1,0:T(8,128)(2,1)S(1)} %get-tuple-element.101), channel_id=1, source_target_pairs={{0,24},{8,0},{16,8},{24,16},{32,56},{40,32},{48,40},{56,48},{64,88... | collective-permute-start | bytes 393224 | tf_op jit(solution)/shard_map/ppermute | solution.py:427
  127.7 11.0 %collective-permute-start.27 = (bf16[16,1024]{1,0:T(8,128)(2,1)S(1)}, bf16[16,1024]{1,0:T(8,128)(2,1)S(1)}, u32[]{:S(2)}, u32[]{:S(2)}) collective-permute-start(bf16[16,1024]{1,0:T(8,128)(2,1)S(1)} %get-tuple-element.111), channel_id=1, source_target_pairs={{0,32},{32,64},{64,96},{96,4},{4,36},{36,68},{68,100},{100,0},{8,4... | collective-permute-start | bytes 98312 | tf_op jit(solution)/shard_map/ppermute | solution.py:427
  130.7 10.6 %collective-permute-start.28 = (bf16[16,1024]{1,0:T(8,128)(2,1)S(1)}, bf16[16,1024]{1,0:T(8,128)(2,1)S(1)}, u32[]{:S(2)}, u32[]{:S(2)}) collective-permute-start(bf16[16,1024]{1,0:T(8,128)(2,1)S(1)} %get-tuple-element.112), channel_id=1, source_target_pairs={{0,64},{32,96},{64,4},{96,36},{4,68},{36,100},{68,0},{100,32},{8,7... | collective-permute-start | bytes 98312 | tf_op jit(solution)/shard_map/ppermute | solution.py:427
  132.2 19.3 %collective-permute-start.29 = (bf16[16,1024]{1,0:T(8,128)(2,1)S(1)}, bf16[16,1024]{1,0:T(8,128)(2,1)S(1)}, u32[]{:S(2)}, u32[]{:S(2)}) collective-permute-start(bf16[16,1024]{1,0:T(8,128)(2,1)S(1)} %get-tuple-element.113), channel_id=1, source_target_pairs={{0,96},{32,4},{64,36},{96,68},{4,100},{36,0},{68,32},{100,64},{8,1... | collective-permute-start | bytes 98312 | tf_op jit(solution)/shard_map/ppermute | solution.py:427
  132.2 19.3 %collective-permute-start.30 = (bf16[16,1024]{1,0:T(8,128)(2,1)S(1)}, bf16[16,1024]{1,0:T(8,128)(2,1)S(1)}, u32[]{:S(2)}, u32[]{:S(2)}) collective-permute-start(bf16[16,1024]{1,0:T(8,128)(2,1)S(1)} %get-tuple-element.114), channel_id=1, source_target_pairs={{0,4},{32,36},{64,68},{96,100},{4,0},{36,32},{68,64},{100,96},{8,1... | collective-permute-start | bytes 98312 | tf_op jit(solution)/shard_map/ppermute | solution.py:427
  138.6 12.9 %collective-permute-start.31 = (bf16[16,1024]{1,0:T(8,128)(2,1)S(1)}, bf16[16,1024]{1,0:T(8,128)(2,1)S(1)}, u32[]{:S(2)}, u32[]{:S(2)}) collective-permute-start(bf16[16,1024]{1,0:T(8,128)(2,1)S(1)} %get-tuple-element.115), channel_id=1, source_target_pairs={{0,36},{32,68},{64,100},{96,0},{4,32},{36,64},{68,96},{100,4},{8,4... | collective-permute-start | bytes 98312 | tf_op jit(solution)/shard_map/ppermute | solution.py:427
  138.6 12.9 %collective-permute-start.32 = (bf16[16,1024]{1,0:T(8,128)(2,1)S(1)}, bf16[16,1024]{1,0:T(8,128)(2,1)S(1)}, u32[]{:S(2)}, u32[]{:S(2)}) collective-permute-start(bf16[16,1024]{1,0:T(8,128)(2,1)S(1)} %get-tuple-element.116), channel_id=1, source_target_pairs={{0,68},{32,100},{64,0},{96,32},{4,64},{36,96},{68,4},{100,36},{8,7... | collective-permute-start | bytes 98312 | tf_op jit(solution)/shard_map/ppermute | solution.py:427
  141.3 10.2 %collective-permute-start.33 = (bf16[16,1024]{1,0:T(8,128)(2,1)S(1)}, bf16[16,1024]{1,0:T(8,128)(2,1)S(1)}, u32[]{:S(2)}, u32[]{:S(2)}) collective-permute-start(bf16[16,1024]{1,0:T(8,128)(2,1)S(1)} %get-tuple-element.117), channel_id=1, source_target_pairs={{0,100},{32,0},{64,32},{96,64},{4,96},{36,4},{68,36},{100,68},{8,1... | collective-permute-start | bytes 98312 | tf_op jit(solution)/shard_map/ppermute | solution.py:427
  (11 other events, 215.6 us)

commit v2 on v1

--- a/solution.py
+++ b/solution.py
@@ -28,7 +28,7 @@
     return jax.ShapeDtypeStruct(dims, dtype)
 
 
-def run(kernel, name, outs, *args, smem=0, scratch=(), flops=0, moved=1 << 20, views=None, room=4):
+def run(kernel, name, outs, *args, smem=0, scratch=(), views=None, room=4, same=None):
     views = views or {}
     in_specs = [
         pl.BlockSpec(memory_space=pltpu.SMEM)
@@ -43,8 +43,9 @@
         in_specs=in_specs,
         out_specs=[pl.BlockSpec(memory_space=pltpu.VMEM)] * len(outs),
         scratch_shapes=list(scratch),
+        input_output_aliases=same or {},
         compiler_params=pltpu.CompilerParams(vmem_limit_bytes=room << 20),
-        cost_estimate=pl.CostEstimate(flops=flops, bytes_accessed=moved, transcendentals=0),
+        cost_estimate=pl.CostEstimate(flops=0, bytes_accessed=1024, transcendentals=0),
         name=name,
     )(*args)
 
@@ -61,9 +62,7 @@
     return jnp.where(even, a, b)
 
 
-def export_kernel(state_ref, taps_ref, out_ref, top_ref, bottom_ref):
-    top_ref[...] = state_ref[0:RIM]
-    bottom_ref[...] = state_ref[ROWS - RIM :]
+def export_kernel(state_ref, taps_ref, out_ref):
     cells = state_ref[:, :, 0:LANES].reshape(CELLS, LANES).astype(F32)
     out_ref[...] = jnp.concatenate(
         [cells[at * LANES : (at + 1) * LANES].T[:Q] for at in range(CELLS // LANES)], axis=0
@@ -87,7 +86,9 @@
     return by_parity(even, two, one), by_parity(even, one, two)
 
 
-def lat_pack_kernel(fields_ref, one_ref, two_ref, top_ref, bottom_ref, up_ref, down_ref, hold):
+def lat_pack_kernel(fields_ref, one_ref, two_ref, state_ref, up_ref, down_ref, hold):
+    up_ref[80:224, :] = state_ref[0:RIM, :, LANES:].reshape(144, 384)
+    down_ref[80:224, :] = state_ref[ROWS - RIM :, :, LANES:].reshape(144, 384)
     left, right = sides(one_ref, two_ref)
     hold[0:48, 0:128] = fields_ref[...].astype(F32)
     hold[0:48, 128:256] = left[:, :LANES]
@@ -96,7 +97,7 @@
     for out_ref, at in ((up_ref, 0), (down_ref, 39)):
         hold[48:57, :] = left[at : at + 9, LANES:]
         hold[57:66, :] = right[at : at + 9, LANES:]
-        out_ref[...] = hold[...].astype(BF)
+        out_ref[0:80, :] = hold[...].astype(BF)
 
 
 def import_kernel(
@@ -202,7 +203,7 @@
 
 
 def conv_wide_kernel(
-    state_ref, one_ref, two_ref, top_ref, bottom_ref, above_ref, below_ref, kernel_ref,
+    state_ref, one_ref, two_ref, above_ref, below_ref, kernel_ref,
     upstream_ref, mask_ref, hidden_ref, update_ref, keep_ref, pad, spread,
 ):
     left, right = sides(one_ref, two_ref)
@@ -213,8 +214,8 @@
         wide = slice((at + 1) * LANES, (at + 2) * LANES)
         thin = slice(at * LANES, (at + 1) * LANES)
         fill_rows(
-            pad, at, top_ref[:, :, wide].astype(F32), state_ref[:, :, wide].astype(F32),
-            bottom_ref[:, :, wide].astype(F32),
+            pad, at, above_ref[80:224, thin].astype(F32).reshape(RIM, COLS, LANES),
+            state_ref[:, :, wide].astype(F32), below_ref[80:224, thin].astype(F32).reshape(RIM, COLS, LANES),
         )
         fill_sides(pad, at, left[:, wide], right[:, wide], above[:, thin], below[:, thin])
 
@@ -285,7 +286,7 @@
         return lax.rem(lon, 4)
     if axis == "y":
         return lon // 8
-    return lax.rem(lon // 4, 2) * 4 + lax.axis_index("lat")
+    return lax.rem(lon // 4, 2)
 
 
 def mlp_kernel(
@@ -315,15 +316,19 @@
         grad_ref[:, CH:] = dot(act, update, 0, 0).astype(BF)
 
 
-def finish_kernel(
-    act_a_ref, act_b_ref, pre_a_ref, pre_b_ref, w_in_a_ref, w_in_b_ref, w_out_a_ref, w_out_b_ref,
-    state_ref, keep_ref, gain_ref, hat_ref, inv_ref,
-    advanced_ref, d_hidden_ref, one_ref, two_ref, wide, left, right,
+def advance_kernel(
+    act_a_ref, act_b_ref, w_out_a_ref, w_out_b_ref, state_ref, keep_ref, after_ref, advanced_ref, wide
 ):
     wide[...] = dot(act_a_ref[...], w_out_a_ref[...], 1, 0) + dot(act_b_ref[...], w_out_b_ref[...], 1, 0)
     for at in range(BLOCKS):
         lanes = slice(at * LANES, (at + 1) * LANES)
         advanced_ref[:, lanes] = (state_ref[:, lanes].astype(F32) + keep_ref[...] * wide[:, lanes]).astype(BF)
+
+
+def finish_kernel(
+    pre_a_ref, pre_b_ref, w_in_a_ref, w_in_b_ref, gain_ref, hat_ref, inv_ref, passed_ref,
+    d_hidden_ref, one_ref, two_ref, passed_out_ref, wide, left, right,
+):
     wide[...] = dot(pre_a_ref[...], w_in_a_ref[...], 1, 0) + dot(pre_b_ref[...], w_in_b_ref[...], 1, 0)
 
     def one_row(row, carry):
@@ -348,7 +353,7 @@
 
 
 def conv_back_kernel(
-    d_hidden_ref, one_ref, two_ref, above_ref, below_ref, kernel_ref, upstream_ref,
+    d_hidden_ref, one_ref, two_ref, above_ref, below_ref, kernel_ref, upstream_ref, after_ref,
     out_ref, pad, spread, held,
 ):
     left, right = sides(one_ref, two_ref)
@@ -383,7 +388,7 @@
     return total
 
 
-def sum_four_kernel(a, b, c, d, out0, out1, out2, out3, hold, *, by_x):
+def sum_four_kernel(a, b, c, d, after, out0, out1, out2, out3, hold, *, by_x):
     hold[...] = sum_refs((a, b, c, d)).astype(BF).reshape(hold.shape)
     for step, out in enumerate((out0, out1, out2, out3)):
         chunk = lax.rem(along("y" if by_x else "x") + step, 4)
@@ -394,18 +399,24 @@
 
 
 def sum_eight_kernel(*refs):
-    ins, outs, hold = refs[:8], refs[8:16], refs[16]
-    hold[0:4] = sum_refs(ins[:4]).astype(BF).reshape(4, 16, 2 * CH)
-    hold[4:8] = sum_refs(ins[4:]).astype(BF).reshape(4, 16, 2 * CH)
-    for step, out in enumerate(outs):
-        at = lax.rem(along("z") + step, 8)
-        out[...] = hold[lax.rem(at, 4) * 2 + at // 4]
+    ins, (mine, other), hold = refs[:8], refs[8:10], refs[10]
+    hold[0:2] = sum_refs(ins[:4]).astype(BF).reshape(2, 2, 16, 2 * CH)
+    hold[2:4] = sum_refs(ins[4:]).astype(BF).reshape(2, 2, 16, 2 * CH)
+    at = along("z_hi")
+    mine[...] = hold[:, at].reshape(64, 2 * CH)
+    other[...] = hold[:, 1 - at].reshape(64, 2 * CH)
+
+
+def sum_two_kernel(a, b, after, out0, out1, out2, out3, hold):
+    hold[...] = sum_refs((a, b)).astype(BF).reshape(4, 16, 2 * CH)
+    for step, out in enumerate((out0, out1, out2, out3)):
+        out[...] = hold[lax.rem(lax.axis_index("lat") + step, 4)]
 
 
 def sum_last_kernel(*refs):
-    total = sum_refs(refs[:8])
-    refs[8][...] = total[:, :CH]
-    refs[9][...] = total[:, CH:]
+    total = sum_refs(refs[:4])
+    refs[4][...] = total[:, :CH]
+    refs[5][...] = total[:, CH:]
 
 
 def ring(axis):
@@ -413,25 +424,29 @@
         lines = [[(i, a, b) for i in range(4)] for a in range(4) for b in range(8)]
     elif axis == "y":
         lines = [[(a, i, b) for i in range(4)] for a in range(4) for b in range(8)]
+    elif axis == "z_hi":
+        lines = [[(a, b, i + 4 * j) for j in range(2)] for a in range(4) for b in range(4) for i in range(4)]
     else:
-        lines = [[(a, b, i) for i in range(8)] for a in range(4) for b in range(4)]
+        lines = [[(a, b, i + 4 * j) for i in range(4)] for a in range(4) for b in range(4) for j in range(2)]
     return [[(z % 4) * 32 + y * 8 + (z // 4) * 4 + x for x, y, z in line] for line in lines]
 
 
-def around(pieces, axis):
+def send(piece, axis, step):
     groups = ring(axis)
     count = len(groups[0])
-    got = [pieces[0]]
-    for step in range(1, count):
-        pairs = [(g[i], g[(i + step) % count]) for g in groups for i in range(count)]
-        got.append(lax.ppermute(pieces[step], ("lat", "lon"), pairs))
-    return got
+    pairs = [(g[i], g[(i + step) % count]) for g in groups for i in range(count)]
+    return lax.ppermute(piece, ("lat", "lon"), pairs)
+
+
+def around(pieces, axis):
+    return [pieces[0]] + [send(piece, axis, step) for step, piece in enumerate(pieces) if step]
 
 
 def swap_lon(one, two):
     pairs = [(i, i ^ 1) for i in range(32)]
     other = [(i, (i - 1) % 32 if i % 2 == 0 else (i + 1) % 32) for i in range(32)]
-    return lax.ppermute(one, "lon", pairs), lax.ppermute(two, "lon", other)
+    two = lax.ppermute(two, "lon", other)
+    return lax.ppermute(one, "lon", pairs), two
 
 
 def swap_lat(up, down):
@@ -450,19 +465,18 @@
     sources = source_tiles.reshape(4)
     weights = regrid_weights[0].transpose(0, 2, 1)
 
-    mine, top, bottom = run(
-        export_kernel, "export", [shape((48, LANES), BF)] + [shape((RIM, COLS, CH), BF)] * 2, state, taps,
+    (mine,) = run(
+        export_kernel, "export", [shape((48, LANES), BF)], state, taps,
         views={1: pl.BlockSpec(memory_space=pl.ANY)},
     )
     fields = lax.ppermute(mine, "group", [(0, 1), (1, 0)])
-    top, bottom = swap_lat(top, bottom)
     one, two = run(
         lon_pack_kernel, "lon_pack", [shape((48, CH), BF)] * 2, state, fields,
         scratch=[vm((48, 384), F32)] * 2,
     )
     one, two = swap_lon(one, two)
     up, down = run(
-        lat_pack_kernel, "lat_pack", [shape((80, 384), BF)] * 2, fields, one, two, top, bottom,
+        lat_pack_kernel, "lat_pack", [shape((224, 384), BF)] * 2, fields, one, two, state,
         scratch=[vm((80, 384), F32)],
     )
     above, below = swap_lat(up, down)
@@ -476,8 +490,8 @@
     hidden, update, keep = run(
         conv_wide_kernel, "conv_wide",
         [shape((3, ROWS, COLS, LANES), F32), shape((CELLS, CH), BF), shape((CELLS, LANES), F32)],
-        state, one, two, top, bottom, above, below, taps, upstream.reshape(CELLS, CH), land_mask,
-        scratch=[vm((3, PAD_ROWS, PAD_COLS, LANES), F32), vm((3, 49, 8, LANES), F32)], moved=8 << 20, room=8,
+        state, one, two, above, below, taps, upstream.reshape(CELLS, CH), land_mask,
+        scratch=[vm((3, PAD_ROWS, PAD_COLS, LANES), F32), vm((3, 49, 8, LANES), F32)], room=8,
     )
     f_up, f_down = run(
         rim_pack_kernel, "rim_pack", [shape((176, LANES), BF)] * 2, forced, f_one, f_two, hidden,
@@ -489,7 +503,7 @@
         [shape((ROWS, COLS, CH), BF), shape((ROWS, COLS, CH), F32), shape((ROWS, COLS, LANES), F32)],
         forced, f_one, f_two, f_above, f_below, taps, hidden, norm_gain,
         scratch=[vm((1, PAD_ROWS, PAD_COLS, LANES), F32), vm((1, 49, 8, LANES), F32), vm((ROWS, COLS, LANES), F32)],
-        moved=8 << 20, room=6,
+        room=6,
     )
     normed = normed.reshape(CELLS, CH)
     hat = hat.reshape(CELLS, CH)
@@ -504,50 +518,62 @@
         outs = run(
             functools.partial(mlp_kernel, by_x=by_x), "mlp_x" if by_x else "mlp_y",
             [shape((PART, 2 * CH), BF)] * 4 + [shape((CELLS, HALF), BF)] * 2 + [shape((HALF, CH), BF)] * 2,
-            normed, update, w_in[0].reshape(dims), w_out[0].reshape(dims), views={2: view, 3: view}, flops=4 << 30, moved=10 << 20, room=12,
+            normed, update, w_in[0].reshape(dims), w_out[0].reshape(dims), views={2: view, 3: view}, room=12,
         )
         return outs[:4], outs[4:]
 
-    grads_a, kept_a = half(True)
-    grads_a = around(grads_a, "x")
     grads_b, kept_b = half(False)
     grads_b = around(grads_b, "y")
-    advanced, d_hidden, d_one, d_two = run(
-        finish_kernel, "finish", [shape((CELLS, CH), BF)] * 2 + [shape((48, CH), BF)] * 2,
-        kept_a[0], kept_b[0], kept_a[1], kept_b[1], kept_a[2], kept_b[2], kept_a[3], kept_b[3],
-        state.reshape(CELLS, CH), keep, norm_gain, hat, inv,
-        scratch=[vm((CELLS, CH), F32)] + [vm((48, CH), F32)] * 2, flops=4 << 30, moved=10 << 20, room=12,
+    grads_a, kept_a = half(True)
+    a_one, a_two = send(grads_a[1], "x", 1), send(grads_a[2], "x", 2)
+    anywhere = pl.BlockSpec(memory_space=pl.ANY)
+    d_hidden, d_one, d_two, a_three = run(
+        finish_kernel, "finish",
+        [shape((CELLS, CH), BF)] + [shape((48, CH), BF)] * 2 + [shape((PART, 2 * CH), BF)],
+        kept_a[1], kept_b[1], kept_a[2], kept_b[2], norm_gain, hat, inv, grads_a[3], same={7: 3},
+        scratch=[vm((CELLS, CH), F32)] + [vm((48, CH), F32)] * 2, room=12,
+    )
+    (advanced,) = run(
+        advance_kernel, "advance", [shape((CELLS, CH), BF)],
+        kept_a[0], kept_b[0], kept_a[3], kept_b[3], state.reshape(CELLS, CH), keep, d_hidden,
+        views={6: anywhere}, scratch=[vm((CELLS, CH), F32)], room=12,
+    )
+    grads_b = run(
+        functools.partial(sum_four_kernel, by_x=False), "sum_y", [shape((64, 2 * CH), BF)] * 4,
+        *grads_b, advanced, views={4: anywhere}, scratch=[vm((2, 2, 4, 16, 2 * CH), BF)],
     )
     d_one, d_two = swap_lon(d_one, d_two)
+    grads_a = [grads_a[0], a_one, a_two, send(a_three, "x", 3)]
+    grads_b = around(grads_b, "x")
+    grads_a = run(
+        functools.partial(sum_four_kernel, by_x=True), "sum_x", [shape((64, 2 * CH), BF)] * 4,
+        *grads_a, d_hidden, views={4: anywhere}, scratch=[vm((2, 4, 32, 2 * CH), BF)],
+    )
     d_up, d_down = run(
         rim_pack_kernel, "rim_pack_back", [shape((176, CH), BF)] * 2, d_hidden, d_one, d_two, d_one,
-        scratch=[vm((32, CH), F32)], views={3: pl.BlockSpec(memory_space=pl.ANY)},
+        scratch=[vm((32, CH), F32)], views={3: anywhere},
     )
     d_above, d_below = swap_lat(d_up, d_down)
+    grads_a = around(grads_a, "y")
+    mine, other = run(
+        sum_eight_kernel, "sum_xy", [shape((64, 2 * CH), BF)] * 2, *grads_a, *grads_b,
+        scratch=[vm((4, 2, 16, 2 * CH), BF)],
+    )
+    other = send(other, "z_hi", 1)
     (state_grad,) = run(
         conv_back_kernel, "conv_back", [shape((ROWS, COLS, CH), BF)],
-        d_hidden, d_one, d_two, d_above, d_below, taps, upstream,
+        d_hidden, d_one, d_two, d_above, d_below, taps, upstream, mine, views={7: anywhere},
         scratch=[
             vm((BLOCKS, PAD_ROWS, PAD_COLS, LANES), F32), vm((BLOCKS, 49, 8, LANES), F32),
             vm((BLOCKS, ROWS, COLS, LANES), F32),
         ],
-        moved=10 << 20, room=10,
-    )
-    grads_a = run(
-        functools.partial(sum_four_kernel, by_x=True), "sum_x", [shape((64, 2 * CH), BF)] * 4,
-        *grads_a, scratch=[vm((2, 4, 32, 2 * CH), BF)],
-    )
-    grads_a = around(grads_a, "y")
-    grads_b = run(
-        functools.partial(sum_four_kernel, by_x=False), "sum_y", [shape((64, 2 * CH), BF)] * 4,
-        *grads_b, scratch=[vm((2, 2, 4, 16, 2 * CH), BF)],
-    )
-    grads_b = around(grads_b, "x")
+        room=10,
+    )
     grads = run(
-        sum_eight_kernel, "sum_xy", [shape((16, 2 * CH), BF)] * 8, *grads_a, *grads_b,
-        scratch=[vm((8, 16, 2 * CH), BF)],
-    )
-    grads = around(grads, "z")
+        sum_two_kernel, "sum_z_hi", [shape((16, 2 * CH), BF)] * 4, mine, other, state_grad, views={2: anywhere},
+        scratch=[vm((4, 16, 2 * CH), BF)],
+    )
+    grads = around(grads, "z_lo")
     grad_in, grad_out = run(sum_last_kernel, "sum_z", [shape((16, CH), F32)] * 2, *grads)
     return (
         advanced.reshape(1, ROWS, COLS, CH),

time: 153 us -> 143 us (0.935)
  starting transfers between devices: 93.1 us -> 80.9 us
  local copies, waits for them, and re-layouts: 1.18 us -> 3.45 us
    ppermute x4 -> x3, starting transfers between devices: 16.5 us -> 9.84 us  [swap_lat(): above = lax.ppermute(down, 'lat', [(i, i + 1) for i in range(3)])]
    ppermute x25 -> x22, waiting for transfers between devices: 9.68 us -> 4.92 us  [the longest x16 2.48 us: send(): return lax.ppermute(piece, ('lat', 'lon'), pairs)]
    ppermute x4 -> x3, waiting for transfers between devices: 4.36 us -> 8.92 us  [swap_lat(): below = lax.ppermute(up, 'lat', [(i + 1, i) for i in range(3)])]
    ppermute x25 -> x22, starting transfers between devices: 71.1 us -> 67.1 us  [the longest x16 41 us: send(): return lax.ppermute(piece, ('lat', 'lon'), pairs)]
    unnamed x18 -> x22, local copies, waits for them, and re-layouts: 1.16 us -> 3.43 us
    ppermute x4 -> x3, starting transfers between devices: 5.3 us -> 3.88 us  [swap_lat(): below = lax.ppermute(up, 'lat', [(i + 1, i) for i in range(3)])]
    pallas_call x16 -> x18, Pallas kernels: 38.5 us -> 38.6 us  [run(): pl.pallas_call(kernel, out_shape=outs, grid=(1,), in_specs=in_specs, out_...]
  transfers between devices with their start and end apart: 34 -> 29, of which waited for: 9 -> 10; matrix products, arithmetic and copies ran while one was open for 0% -> 0% of each run, Pallas kernels for 18% -> 19%
where the time goes in v2:
time: 143 us; the launch traced here: 142 us
  starting transfers between devices  80.9 us (57%)
  Pallas kernels  38.6 us (27%)
  waiting for transfers between devices  17 us (12%)
  local copies, waits for them, and re-layouts  3.45 us (2%)
    ppermute x16, starting transfers between devices, send(): return lax.ppermute(piece, ('lat', 'lon'), pairs)  41 us
    pallas_call x18, Pallas kernels, run(): pl.pallas_call(kernel, out_shape=outs, grid=(1,), in_specs=in_specs, out_...  38.6 us
    ppermute x3, starting transfers between devices, swap_lon(): two = lax.ppermute(two, 'lon', other)  24.1 us
    ppermute x3, starting transfers between devices, swap_lat(): above = lax.ppermute(down, 'lat', [(i, i + 1) for i in range(3)])  9.84 us
    ppermute x3, waiting for transfers between devices, swap_lat(): below = lax.ppermute(up, 'lat', [(i + 1, i) for i in range(3)])  8.92 us
    ppermute x3, starting transfers between devices, swap_lat(): below = lax.ppermute(up, 'lat', [(i + 1, i) for i in range(3)])  3.88 us
    unnamed x22, local copies, waits for them, and re-layouts  3.43 us
  transfers between devices with their start and end apart: 29, of which 10 were waited for; matrix products, arithmetic and copies ran while one was open for 0% of the time, Pallas kernels for 19%

profile of v2, /device:TPU:6, one launch (start us, length us, event | category | flops | bytes accessed | tf_op | source)
XLA Modules:
  0.0 142.0 jit_solution(6932946895293588366)
XLA Ops:
  5.3 7.8 %collective-permute-start.2 = (bf16[48,512]{1,0:T(8,128)(2,1)S(1)}, bf16[48,512]{1,0:T(8,128)(2,1)S(1)}, u32[]{:S(2)}, u32[]{:S(2)}) collective-permute-start(bf16[48,512]{1,0:T(8,128)(2,1)S(1)} %get-tuple-element.58), channel_id=1, source_target_pairs={{0,31},{1,2},{2,1},{3,4},{4,3},{5,6},{6,5},{7,8},{8,7},{9,10},{10,... | collective-permute-start | bytes 147464 | tf_op jit(solution)/shard_map/ppermute | solution.py:448
  13.1 2.4 %collective-permute-done.2.two_ref = bf16[48,512]{1,0:T(8,128)(2,1)S(1)} collective-permute-done((bf16[48,512]{1,0:T(8,128)(2,1)S(1)}, bf16[48,512]{1,0:T(8,128)(2,1)S(1)}, u32[]{:S(2)}, u32[]{:S(2)}) %collective-permute-start.2) | collective-permute-done | bytes 49184 | tf_op jit(solution)/shard_map/ppermute | solution.py:448
  15.6 3.7 %collective-permute-start.3 = (bf16[224,384]{1,0:T(8,128)(2,1)S(1)}, bf16[224,384]{1,0:T(8,128)(2,1)S(1)}, u32[]{:S(2)}, u32[]{:S(2)}) collective-permute-start(bf16[224,384]{1,0:T(8,128)(2,1)S(1)} %get-tuple-element.59), channel_id=1, source_target_pairs={{0,32},{32,64},{64,96},{1,33},{33,65},{65,97},{2,34},{34,66},{66,9... | collective-permute-start | bytes 516104 | tf_op jit(solution)/shard_map/ppermute | solution.py:453
  19.3 1.3 collective-permute-start.4
  20.6 1.6 %collective-permute-done.3.above_ref = bf16[224,384]{1,0:T(8,128)(2,1)S(1)} collective-permute-done((bf16[224,384]{1,0:T(8,128)(2,1)S(1)}, bf16[224,384]{1,0:T(8,128)(2,1)S(1)}, u32[]{:S(2)}, u32[]{:S(2)}) %collective-permute-start.3) | collective-permute-done | bytes 172064 | tf_op jit(solution)/shard_map/ppermute | solution.py:453
  22.2 4.4 %collective-permute-done.4.below_ref = bf16[224,384]{1,0:T(8,128)(2,1)S(1)} collective-permute-done((bf16[224,384]{1,0:T(8,128)(2,1)S(1)}, bf16[224,384]{1,0:T(8,128)(2,1)S(1)}, u32[]{:S(2)}, u32[]{:S(2)}) %collective-permute-start.4) | collective-permute-done | bytes 172064 | tf_op jit(solution)/shard_map/ppermute | solution.py:454
  27.6 7.1 %collective-permute-start.6 = (bf16[48,128]{1,0:T(8,128)(2,1)S(1)}, bf16[48,128]{1,0:T(8,128)(2,1)S(1)}, u32[]{:S(2)}, u32[]{:S(2)}) collective-permute-start(bf16[48,128]{1,0:T(8,128)(2,1)S(1)} %get-tuple-element.63), channel_id=1, source_target_pairs={{0,31},{1,2},{2,1},{3,4},{4,3},{5,6},{6,5},{7,8},{8,7},{9,10},{10,... | collective-permute-start | bytes 36872 | tf_op jit(solution)/shard_map/ppermute | solution.py:448
  34.7 6.0 %conv_wide.1 = (f32[3,16,48,128]{3,2,1,0:T(8,128)S(1)}, bf16[768,512]{1,0:T(8,128)(2,1)S(1)}, f32[768,128]{1,0:T(8,128)S(1)}) custom-call(bf16[16,48,512]{2,1,0:T(8,128)(2,1)S(1)} %bitcast.23, bf16[48,512]{1,0:T(8,128)(2,1)S(1)} %collective-permute-done.1.one_ref, bf16[48,512]{1,0:T(8,128)(2,1)S(1)} %collective-permute-done.2.two_ref, ...), custom_call_target="tpu_custom_call" | custom-call | bytes 1024 | tf_op jit(solution)/shard_map/conv_wide/pallas_call | solution.py:39
  40.8 3.2 %collective-permute-start.7 = (bf16[176,128]{1,0:T(8,128)(2,1)S(1)}, bf16[176,128]{1,0:T(8,128)(2,1)S(1)}, u32[]{:S(2)}, u32[]{:S(2)}) collective-permute-start(bf16[176,128]{1,0:T(8,128)(2,1)S(1)} %get-tuple-element.65), channel_id=1, source_target_pairs={{0,32},{32,64},{64,96},{1,33},{33,65},{65,97},{2,34},{34,66},{66,9... | collective-permute-start | bytes 135176 | tf_op jit(solution)/shard_map/ppermute | solution.py:453
  45.7 4.2 %collective-permute-done.8.below_ref = bf16[176,128]{1,0:T(8,128)(2,1)S(1)} collective-permute-done((bf16[176,128]{1,0:T(8,128)(2,1)S(1)}, bf16[176,128]{1,0:T(8,128)(2,1)S(1)}, u32[]{:S(2)}, u32[]{:S(2)}) %collective-permute-start.8) | collective-permute-done | bytes 45088 | tf_op jit(solution)/shard_map/ppermute | solution.py:454
  50.0 4.4 %conv_norm.1 = (bf16[16,48,512]{2,1,0:T(8,128)(2,1)S(1)}, f32[16,48,512]{2,1,0:T(8,128)S(1)}, f32[16,48,128]{2,1,0:T(8,128)S(1)}) custom-call(bf16[768,128]{1,0:T(8,128)(2,1)S(1)} %get-tuple-element.61.cells_ref.forced_ref, bf16[48,128]{1,0:T(8,128)(2,1)S(1)} %collective-permute-done.5.one_ref, bf16[48,128]{1,0:T(8,128)(2,1)S(1)} %collective-permute-done.6.two_ref, ...), custom_call_target="tpu_custom_call" | custom-call | bytes 1024 | tf_op jit(solution)/shard_map/conv_norm/pallas_call | solution.py:39
  54.4 5.0 %mlp_y.1 = (bf16[256,1024]{1,0:T(8,128)(2,1)S(1)}, bf16[256,1024]{1,0:T(8,128)(2,1)S(1)}, bf16[256,1024]{1,0:T(8,128)(2,1)S(1)}, bf16[256,1024]{1,0:T(8,128)(2,1...) custom-call(bf16[768,512]{1,0:T(8,128)(2,1)S(1)} %bitcast.32, ...), custom_call_target="tpu_custom_call" | custom-call | bytes 1024 | tf_op jit(solution)/shard_map/mlp_y/pallas_call | solution.py:39
  59.4 1.8 %collective-permute-start.19 = (bf16[256,1024]{1,0:T(8,128)(2,1)S(1)}, bf16[256,1024]{1,0:T(8,128)(2,1)S(1)}, u32[]{:S(2)}, u32[]{:S(2)}) collective-permute-start(bf16[256,1024]{1,0:T(8,128)(2,1)S(1)} %get-tuple-element.95), channel_id=1, source_target_pairs={{0,8},{8,16},{16,24},{24,0},{32,40},{40,48},{48,56},{56,32},{64,72... | collective-permute-start | bytes 1572872 | tf_op jit(solution)/shard_map/ppermute | solution.py:438
  61.2 2.9 %collective-permute-start.20 = (bf16[256,1024]{1,0:T(8,128)(2,1)S(1)}, bf16[256,1024]{1,0:T(8,128)(2,1)S(1)}, u32[]{:S(2)}, u32[]{:S(2)}) collective-permute-start(bf16[256,1024]{1,0:T(8,128)(2,1)S(1)} %get-tuple-element.96), channel_id=1, source_target_pairs={{0,16},{8,24},{16,0},{24,8},{32,48},{40,56},{48,32},{56,40},{64,80... | collective-permute-start | bytes 1572872 | tf_op jit(solution)/shard_map/ppermute | solution.py:438
  64.1 1.4 %collective-permute-start.21 = (bf16[256,1024]{1,0:T(8,128)(2,1)S(1)}, bf16[256,1024]{1,0:T(8,128)(2,1)S(1)}, u32[]{:S(2)}, u32[]{:S(2)}) collective-permute-start(bf16[256,1024]{1,0:T(8,128)(2,1)S(1)} %get-tuple-element.97), channel_id=1, source_target_pairs={{0,24},{8,0},{16,8},{24,16},{32,56},{40,32},{48,40},{56,48},{64,88... | collective-permute-start | bytes 1572872 | tf_op jit(solution)/shard_map/ppermute | solution.py:438
  65.6 5.0 %mlp_x.1 = (bf16[256,1024]{1,0:T(8,128)(2,1)S(1)}, bf16[256,1024]{1,0:T(8,128)(2,1)S(1)}, bf16[256,1024]{1,0:T(8,128)(2,1)S(1)}, bf16[256,1024]{1,0:T(8,128)(2,1...) custom-call(bf16[768,512]{1,0:T(8,128)(2,1)S(1)} %bitcast.33, ...), custom_call_target="tpu_custom_call" | custom-call | bytes 1024 | tf_op jit(solution)/shard_map/mlp_x/pallas_call | solution.py:39
  70.6 3.8 %finish.1 = (bf16[768,512]{1,0:T(8,128)(2,1)S(1)}, bf16[48,512]{1,0:T(8,128)(2,1)S(1)}, bf16[48,512]{1,0:T(8,128)(2,1)S(1)}, bf16[256,1024]{1,0:T(8,128)(2,1)S(1)}) custom-call(bf16[768,1024]{1,0:T(8,128)(2,1)S(1)} %get-tuple-element.74.pre_a_ref, bf16[768,1024]{1,0:T(8,128)(2,1)S(1)} %get-tuple-element.75.pre_b_ref, ...), custom_call_target="tpu_custom_call", output_to_operand_aliasing={{3}: (7, {})} | custom-call | bytes 1024 | tf_op jit(solution)/shard_map/finish/pallas_call | solution.py:39
  74.4 4.1 %collective-permute-start.13 = (bf16[256,1024]{1,0:T(8,128)(2,1)S(1)}, bf16[256,1024]{1,0:T(8,128)(2,1)S(1)}, u32[]{:S(2)}, u32[]{:S(2)}) collective-permute-start(bf16[256,1024]{1,0:T(8,128)(2,1)S(1)} %get-tuple-element.87), channel_id=1, source_target_pairs={{0,1},{1,2},{2,3},{3,0},{32,33},{33,34},{34,35},{35,32},{64,65},{6... | collective-permute-start | bytes 1572872 | tf_op jit(solution)/shard_map/ppermute | solution.py:438
  78.5 1.4 collective-permute-start.14
  79.9 2.7 %advance.1.after = bf16[768,512]{1,0:T(8,128)(2,1)} custom-call(bf16[768,1024]{1,0:T(8,128)(2,1)S(1)} %get-tuple-element.69.act_a_ref, bf16[768,1024]{1,0:T(8,128)(2,1)S(1)} %get-tuple-element.70.act_b_ref, bf16[1024,512]{1,0:T(8,128)(2,1)S(1)} %get-tuple-element.71.w_out_a_ref, bf16[1024,512]{1,0:T(8,128)(2,1)S(1)} %get-tuple-element.72.w_out_b_ref, ...), custom_call_target="tpu_custom_call" | custom-call | bytes 1024 | tf_op jit(solution)/shard_map/advance/pallas_call | solution.py:39
  84.3 8.2 %collective-permute-start.22 = (bf16[64,1024]{1,0:T(8,128)(2,1)S(1)}, bf16[64,1024]{1,0:T(8,128)(2,1)S(1)}, u32[]{:S(2)}, u32[]{:S(2)}) collective-permute-start(bf16[64,1024]{1,0:T(8,128)(2,1)S(1)} %get-tuple-element.99), channel_id=1, source_target_pairs={{0,1},{1,2},{2,3},{3,0},{32,33},{33,34},{34,35},{35,32},{64,65},{6... | collective-permute-start | bytes 393224 | tf_op jit(solution)/shard_map/ppermute | solution.py:438
  93.5 9.3 %collective-permute-start.10 = (bf16[48,512]{1,0:T(8,128)(2,1)S(1)}, bf16[48,512]{1,0:T(8,128)(2,1)S(1)}, u32[]{:S(2)}, u32[]{:S(2)}) collective-permute-start(bf16[48,512]{1,0:T(8,128)(2,1)S(1)} %get-tuple-element.83), channel_id=1, source_target_pairs={{0,31},{1,2},{2,1},{3,4},{4,3},{5,6},{6,5},{7,8},{8,7},{9,10},{10,... | collective-permute-start | bytes 147464 | tf_op jit(solution)/shard_map/ppermute | solution.py:448
  102.7 3.6 %collective-permute-start.24 = (bf16[64,1024]{1,0:T(8,128)(2,1)S(1)}, bf16[64,1024]{1,0:T(8,128)(2,1)S(1)}, u32[]{:S(2)}, u32[]{:S(2)}) collective-permute-start(bf16[64,1024]{1,0:T(8,128)(2,1)S(1)} %get-tuple-element.101), channel_id=1, source_target_pairs={{0,3},{1,0},{2,1},{3,2},{32,35},{33,32},{34,33},{35,34},{64,67},{6... | collective-permute-start | bytes 393224 | tf_op jit(solution)/shard_map/ppermute | solution.py:438
  106.9 2.4 %collective-permute-start.16 = (bf16[64,1024]{1,0:T(8,128)(2,1)S(1)}, bf16[64,1024]{1,0:T(8,128)(2,1)S(1)}, u32[]{:S(2)}, u32[]{:S(2)}) collective-permute-start(bf16[64,1024]{1,0:T(8,128)(2,1)S(1)} %get-tuple-element.91), channel_id=1, source_target_pairs={{0,8},{8,16},{16,24},{24,0},{32,40},{40,48},{48,56},{56,32},{64,72... | collective-permute-start | bytes 393224 | tf_op jit(solution)/shard_map/ppermute | solution.py:438
  109.4 1.9 %collective-permute-start.17 = (bf16[64,1024]{1,0:T(8,128)(2,1)S(1)}, bf16[64,1024]{1,0:T(8,128)(2,1)S(1)}, u32[]{:S(2)}, u32[]{:S(2)}) collective-permute-start(bf16[64,1024]{1,0:T(8,128)(2,1)S(1)} %get-tuple-element.92), channel_id=1, source_target_pairs={{0,16},{8,24},{16,0},{24,8},{32,48},{40,56},{48,32},{56,40},{64,80... | collective-permute-start | bytes 393224 | tf_op jit(solution)/shard_map/ppermute | solution.py:438
  111.3 2.5 %collective-permute-start.18 = (bf16[64,1024]{1,0:T(8,128)(2,1)S(1)}, bf16[64,1024]{1,0:T(8,128)(2,1)S(1)}, u32[]{:S(2)}, u32[]{:S(2)}) collective-permute-start(bf16[64,1024]{1,0:T(8,128)(2,1)S(1)} %get-tuple-element.93), channel_id=1, source_target_pairs={{0,24},{8,0},{16,8},{24,16},{32,56},{40,32},{48,40},{56,48},{64,88... | collective-permute-start | bytes 393224 | tf_op jit(solution)/shard_map/ppermute | solution.py:438
  113.9 2.9 %collective-permute-start.11 = (bf16[176,512]{1,0:T(8,128)(2,1)S(1)}, bf16[176,512]{1,0:T(8,128)(2,1)S(1)}, u32[]{:S(2)}, u32[]{:S(2)}) collective-permute-start(bf16[176,512]{1,0:T(8,128)(2,1)S(1)} %get-tuple-element.84), channel_id=1, source_target_pairs={{0,32},{32,64},{64,96},{1,33},{33,65},{65,97},{2,34},{34,66},{66,9... | collective-permute-start | bytes 540680 | tf_op jit(solution)/shard_map/ppermute | solution.py:453
  118.3 5.6 %collective-permute-start.25 = (bf16[64,1024]{1,0:T(8,128)(2,1)S(1)}, bf16[64,1024]{1,0:T(8,128)(2,1)S(1)}, u32[]{:S(2)}, u32[]{:S(2)}) collective-permute-start(bf16[64,1024]{1,0:T(8,128)(2,1)S(1)} %get-tuple-element.103), channel_id=1, source_target_pairs={{0,4},{4,0},{32,36},{36,32},{64,68},{68,64},{96,100},{100,96},{8,1... | collective-permute-start | bytes 393224 | tf_op jit(solution)/shard_map/ppermute | solution.py:438
  124.2 8.7 %conv_back.1.after = bf16[16,48,512]{2,1,0:T(8,128)(2,1)} custom-call(bf16[768,512]{1,0:T(8,128)(2,1)S(1)} %get-tuple-element.81.after_ref.cells_ref.after.d_hidden_ref, bf16[48,512]{1,0:T(8,128)(2,1)S(1)} %collective-permute-done.9.one_ref.after_ref, bf16[48,512]{1,0:T(8,128)(2,1)S(1)} %collective-permute-done.10.two_ref, ...), custom_call_target="tpu_custom_call" | custom-call | bytes 1024 | tf_op jit(solution)/shard_map/conv_back/pallas_call | solution.py:39
  134.0 2.5 %collective-permute-start.26 = (bf16[16,1024]{1,0:T(8,128)(2,1)S(1)}, bf16[16,1024]{1,0:T(8,128)(2,1)S(1)}, u32[]{:S(2)}, u32[]{:S(2)}) collective-permute-start(bf16[16,1024]{1,0:T(8,128)(2,1)S(1)} %get-tuple-element.105), channel_id=1, source_target_pairs={{0,32},{32,64},{64,96},{96,0},{4,36},{36,68},{68,100},{100,4},{8,4... | collective-permute-start | bytes 98312 | tf_op jit(solution)/shard_map/ppermute | solution.py:438
  136.5 2.5 %collective-permute-start.28 = (bf16[16,1024]{1,0:T(8,128)(2,1)S(1)}, bf16[16,1024]{1,0:T(8,128)(2,1)S(1)}, u32[]{:S(2)}, u32[]{:S(2)}) collective-permute-start(bf16[16,1024]{1,0:T(8,128)(2,1)S(1)} %get-tuple-element.107), channel_id=1, source_target_pairs={{0,96},{32,0},{64,32},{96,64},{4,100},{36,4},{68,36},{100,68},{8,1... | collective-permute-start | bytes 98312 | tf_op jit(solution)/shard_map/ppermute | solution.py:438
  139.8 1.5 %collective-permute-done.27.refs_2_ = bf16[16,1024]{1,0:T(8,128)(2,1)S(1)} collective-permute-done((bf16[16,1024]{1,0:T(8,128)(2,1)S(1)}, bf16[16,1024]{1,0:T(8,128)(2,1)S(1)}, u32[]{:S(2)}, u32[]{:S(2)}) %collective-permute-start.27) | collective-permute-done | bytes 32800 | tf_op jit(solution)/shard_map/ppermute | solution.py:438
  (68 shorter events, 15.2 us)
Async XLA Ops:
  3.0 31.7 %copy-start.1 = (bf16[1,16,48,512]{3,2,1,0:T(8,128)(2,1)S(1)}, bf16[1,16,48,512]{3,2,1,0:T(8,128)(2,1)}, u32[]{:S(2)}) copy-start(bf16[1,16,48,512]{3,2,1,0:T(8,128)(2,1)} %param.9) | copy-start | bytes 2359300
  3.0 31.7 %copy-start.4 = (bf16[1,16,48,512]{3,2,1,0:T(8,128)(2,1)S(1)}, bf16[1,16,48,512]{3,2,1,0:T(8,128)(2,1)}, u32[]{:S(2)}) copy-start(bf16[1,16,48,512]{3,2,1,0:T(8,128)(2,1)} %param.10) | copy-start | bytes 2359300
  3.0 31.6 %copy-start.8 = (s32[16,48]{1,0:T(8,128)S(1)}, s32[16,48]{1,0:T(8,128)}, u32[]{:S(2)}) copy-start(s32[16,48]{1,0:T(8,128)} %mask_ref.1) | copy-start | bytes 9220
  3.1 1.3 collective-permute-start
  4.4 8.7 %collective-permute-start.1 = (bf16[48,512]{1,0:T(8,128)(2,1)S(1)}, bf16[48,512]{1,0:T(8,128)(2,1)S(1)}, u32[]{:S(2)}, u32[]{:S(2)}) collective-permute-start(bf16[48,512]{1,0:T(8,128)(2,1)S(1)} %get-tuple-element.57), channel_id=1, source_target_pairs={{0,1},{1,0},{2,3},{3,2},{4,5},{5,4},{6,7},{7,6},{8,9},{9,8},{10,11... | collective-permute-start | bytes 147464 | tf_op jit(solution)/shard_map/ppermute | solution.py:449
  5.3 10.2 %collective-permute-start.2 = (bf16[48,512]{1,0:T(8,128)(2,1)S(1)}, bf16[48,512]{1,0:T(8,128)(2,1)S(1)}, u32[]{:S(2)}, u32[]{:S(2)}) collective-permute-start(bf16[48,512]{1,0:T(8,128)(2,1)S(1)} %get-tuple-element.58), channel_id=1, source_target_pairs={{0,31},{1,2},{2,1},{3,4},{4,3},{5,6},{6,5},{7,8},{8,7},{9,10},{10,... | collective-permute-start | bytes 147464 | tf_op jit(solution)/shard_map/ppermute | solution.py:448
  15.6 6.6 %collective-permute-start.3 = (bf16[224,384]{1,0:T(8,128)(2,1)S(1)}, bf16[224,384]{1,0:T(8,128)(2,1)S(1)}, u32[]{:S(2)}, u32[]{:S(2)}) collective-permute-start(bf16[224,384]{1,0:T(8,128)(2,1)S(1)} %get-tuple-element.59), channel_id=1, source_target_pairs={{0,32},{32,64},{64,96},{1,33},{33,65},{65,97},{2,34},{34,66},{66,9... | collective-permute-start | bytes 516104 | tf_op jit(solution)/shard_map/ppermute | solution.py:453
  19.3 7.3 %collective-permute-start.4 = (bf16[224,384]{1,0:T(8,128)(2,1)S(1)}, bf16[224,384]{1,0:T(8,128)(2,1)S(1)}, u32[]{:S(2)}, u32[]{:S(2)}) collective-permute-start(bf16[224,384]{1,0:T(8,128)(2,1)S(1)} %get-tuple-element.60), channel_id=1, source_target_pairs={{32,0},{64,32},{96,64},{33,1},{65,33},{97,65},{34,2},{66,34},{98,6... | collective-permute-start | bytes 516104 | tf_op jit(solution)/shard_map/ppermute | solution.py:454
  27.5 13.3 %collective-permute-start.5 = (bf16[48,128]{1,0:T(8,128)(2,1)S(1)}, bf16[48,128]{1,0:T(8,128)(2,1)S(1)}, u32[]{:S(2)}, u32[]{:S(2)}) collective-permute-start(bf16[48,128]{1,0:T(8,128)(2,1)S(1)} %get-tuple-element.62), channel_id=1, source_target_pairs={{0,1},{1,0},{2,3},{3,2},{4,5},{5,4},{6,7},{7,6},{8,9},{9,8},{10,11... | collective-permute-start | bytes 36872 | tf_op jit(solution)/shard_map/ppermute | solution.py:449
  27.6 13.2 %collective-permute-start.6 = (bf16[48,128]{1,0:T(8,128)(2,1)S(1)}, bf16[48,128]{1,0:T(8,128)(2,1)S(1)}, u32[]{:S(2)}, u32[]{:S(2)}) collective-permute-start(bf16[48,128]{1,0:T(8,128)(2,1)S(1)} %get-tuple-element.63), channel_id=1, source_target_pairs={{0,31},{1,2},{2,1},{3,4},{4,3},{5,6},{6,5},{7,8},{8,7},{9,10},{10,... | collective-permute-start | bytes 36872 | tf_op jit(solution)/shard_map/ppermute | solution.py:448
  40.8 4.9 %collective-permute-start.7 = (bf16[176,128]{1,0:T(8,128)(2,1)S(1)}, bf16[176,128]{1,0:T(8,128)(2,1)S(1)}, u32[]{:S(2)}, u32[]{:S(2)}) collective-permute-start(bf16[176,128]{1,0:T(8,128)(2,1)S(1)} %get-tuple-element.65), channel_id=1, source_target_pairs={{0,32},{32,64},{64,96},{1,33},{33,65},{65,97},{2,34},{34,66},{66,9... | collective-permute-start | bytes 135176 | tf_op jit(solution)/shard_map/ppermute | solution.py:453
  44.0 5.9 %collective-permute-start.8 = (bf16[176,128]{1,0:T(8,128)(2,1)S(1)}, bf16[176,128]{1,0:T(8,128)(2,1)S(1)}, u32[]{:S(2)}, u32[]{:S(2)}) collective-permute-start(bf16[176,128]{1,0:T(8,128)(2,1)S(1)} %get-tuple-element.66), channel_id=1, source_target_pairs={{32,0},{64,32},{96,64},{33,1},{65,33},{97,65},{34,2},{66,34},{98,6... | collective-permute-start | bytes 135176 | tf_op jit(solution)/shard_map/ppermute | solution.py:454
  59.4 19.1 %collective-permute-start.19 = (bf16[256,1024]{1,0:T(8,128)(2,1)S(1)}, bf16[256,1024]{1,0:T(8,128)(2,1)S(1)}, u32[]{:S(2)}, u32[]{:S(2)}) collective-permute-start(bf16[256,1024]{1,0:T(8,128)(2,1)S(1)} %get-tuple-element.95), channel_id=1, source_target_pairs={{0,8},{8,16},{16,24},{24,0},{32,40},{40,48},{48,56},{56,32},{64,72... | collective-permute-start | bytes 1572872 | tf_op jit(solution)/shard_map/ppermute | solution.py:438
  61.2 21.4 %collective-permute-start.20 = (bf16[256,1024]{1,0:T(8,128)(2,1)S(1)}, bf16[256,1024]{1,0:T(8,128)(2,1)S(1)}, u32[]{:S(2)}, u32[]{:S(2)}) collective-permute-start(bf16[256,1024]{1,0:T(8,128)(2,1)S(1)} %get-tuple-element.96), channel_id=1, source_target_pairs={{0,16},{8,24},{16,0},{24,8},{32,48},{40,56},{48,32},{56,40},{64,80... | collective-permute-start | bytes 1572872 | tf_op jit(solution)/shard_map/ppermute | solution.py:438
  64.1 18.5 %collective-permute-start.21 = (bf16[256,1024]{1,0:T(8,128)(2,1)S(1)}, bf16[256,1024]{1,0:T(8,128)(2,1)S(1)}, u32[]{:S(2)}, u32[]{:S(2)}) collective-permute-start(bf16[256,1024]{1,0:T(8,128)(2,1)S(1)} %get-tuple-element.97), channel_id=1, source_target_pairs={{0,24},{8,0},{16,8},{24,16},{32,56},{40,32},{48,40},{56,48},{64,88... | collective-permute-start | bytes 1572872 | tf_op jit(solution)/shard_map/ppermute | solution.py:438
  74.3 19.1 %collective-permute-start.15 = (bf16[256,1024]{1,0:T(8,128)(2,1)S(1)}, bf16[256,1024]{1,0:T(8,128)(2,1)S(1)}, u32[]{:S(2)}, u32[]{:S(2)}) collective-permute-start(bf16[256,1024]{1,0:T(8,128)(2,1)S(1)} %get-tuple-element.89), channel_id=1, source_target_pairs={{0,3},{1,0},{2,1},{3,2},{32,35},{33,32},{34,33},{35,34},{64,67},{6... | collective-permute-start | bytes 1572872 | tf_op jit(solution)/shard_map/ppermute | solution.py:438
  74.4 28.3 %collective-permute-start.13 = (bf16[256,1024]{1,0:T(8,128)(2,1)S(1)}, bf16[256,1024]{1,0:T(8,128)(2,1)S(1)}, u32[]{:S(2)}, u32[]{:S(2)}) collective-permute-start(bf16[256,1024]{1,0:T(8,128)(2,1)S(1)} %get-tuple-element.87), channel_id=1, source_target_pairs={{0,1},{1,2},{2,3},{3,0},{32,33},{33,34},{34,35},{35,32},{64,65},{6... | collective-permute-start | bytes 1572872 | tf_op jit(solution)/shard_map/ppermute | solution.py:438
  78.5 24.2 %collective-permute-start.14 = (bf16[256,1024]{1,0:T(8,128)(2,1)S(1)}, bf16[256,1024]{1,0:T(8,128)(2,1)S(1)}, u32[]{:S(2)}, u32[]{:S(2)}) collective-permute-start(bf16[256,1024]{1,0:T(8,128)(2,1)S(1)} %get-tuple-element.88), channel_id=1, source_target_pairs={{0,2},{1,3},{2,0},{3,1},{32,34},{33,35},{34,32},{35,33},{64,66},{6... | collective-permute-start | bytes 1572872 | tf_op jit(solution)/shard_map/ppermute | solution.py:438
  84.3 26.9 %collective-permute-start.22 = (bf16[64,1024]{1,0:T(8,128)(2,1)S(1)}, bf16[64,1024]{1,0:T(8,128)(2,1)S(1)}, u32[]{:S(2)}, u32[]{:S(2)}) collective-permute-start(bf16[64,1024]{1,0:T(8,128)(2,1)S(1)} %get-tuple-element.99), channel_id=1, source_target_pairs={{0,1},{1,2},{2,3},{3,0},{32,33},{33,34},{34,35},{35,32},{64,65},{6... | collective-permute-start | bytes 393224 | tf_op jit(solution)/shard_map/ppermute | solution.py:438
  92.5 14.4 %collective-permute-start.9 = (bf16[48,512]{1,0:T(8,128)(2,1)S(1)}, bf16[48,512]{1,0:T(8,128)(2,1)S(1)}, u32[]{:S(2)}, u32[]{:S(2)}) collective-permute-start(bf16[48,512]{1,0:T(8,128)(2,1)S(1)} %get-tuple-element.82), channel_id=1, source_target_pairs={{0,1},{1,0},{2,3},{3,2},{4,5},{5,4},{6,7},{7,6},{8,9},{9,8},{10,11... | collective-permute-start | bytes 147464 | tf_op jit(solution)/shard_map/ppermute | solution.py:449
  93.5 15.9 %collective-permute-start.10 = (bf16[48,512]{1,0:T(8,128)(2,1)S(1)}, bf16[48,512]{1,0:T(8,128)(2,1)S(1)}, u32[]{:S(2)}, u32[]{:S(2)}) collective-permute-start(bf16[48,512]{1,0:T(8,128)(2,1)S(1)} %get-tuple-element.83), channel_id=1, source_target_pairs={{0,31},{1,2},{2,1},{3,4},{4,3},{5,6},{6,5},{7,8},{8,7},{9,10},{10,... | collective-permute-start | bytes 147464 | tf_op jit(solution)/shard_map/ppermute | solution.py:448
  102.7 11.1 %collective-permute-start.23 = (bf16[64,1024]{1,0:T(8,128)(2,1)S(1)}, bf16[64,1024]{1,0:T(8,128)(2,1)S(1)}, u32[]{:S(2)}, u32[]{:S(2)}) collective-permute-start(bf16[64,1024]{1,0:T(8,128)(2,1)S(1)} %get-tuple-element.100), channel_id=1, source_target_pairs={{0,2},{1,3},{2,0},{3,1},{32,34},{33,35},{34,32},{35,33},{64,66},{6... | collective-permute-start | bytes 393224 | tf_op jit(solution)/shard_map/ppermute | solution.py:438
  102.7 14.0 %collective-permute-start.24 = (bf16[64,1024]{1,0:T(8,128)(2,1)S(1)}, bf16[64,1024]{1,0:T(8,128)(2,1)S(1)}, u32[]{:S(2)}, u32[]{:S(2)}) collective-permute-start(bf16[64,1024]{1,0:T(8,128)(2,1)S(1)} %get-tuple-element.101), channel_id=1, source_target_pairs={{0,3},{1,0},{2,1},{3,2},{32,35},{33,32},{34,33},{35,34},{64,67},{6... | collective-permute-start | bytes 393224 | tf_op jit(solution)/shard_map/ppermute | solution.py:438
  106.9 11.2 %collective-permute-start.16 = (bf16[64,1024]{1,0:T(8,128)(2,1)S(1)}, bf16[64,1024]{1,0:T(8,128)(2,1)S(1)}, u32[]{:S(2)}, u32[]{:S(2)}) collective-permute-start(bf16[64,1024]{1,0:T(8,128)(2,1)S(1)} %get-tuple-element.91), channel_id=1, source_target_pairs={{0,8},{8,16},{16,24},{24,0},{32,40},{40,48},{48,56},{56,32},{64,72... | collective-permute-start | bytes 393224 | tf_op jit(solution)/shard_map/ppermute | solution.py:438
  109.4 8.7 %collective-permute-start.17 = (bf16[64,1024]{1,0:T(8,128)(2,1)S(1)}, bf16[64,1024]{1,0:T(8,128)(2,1)S(1)}, u32[]{:S(2)}, u32[]{:S(2)}) collective-permute-start(bf16[64,1024]{1,0:T(8,128)(2,1)S(1)} %get-tuple-element.92), channel_id=1, source_target_pairs={{0,16},{8,24},{16,0},{24,8},{32,48},{40,56},{48,32},{56,40},{64,80... | collective-permute-start | bytes 393224 | tf_op jit(solution)/shard_map/ppermute | solution.py:438
  111.3 6.8 %collective-permute-start.18 = (bf16[64,1024]{1,0:T(8,128)(2,1)S(1)}, bf16[64,1024]{1,0:T(8,128)(2,1)S(1)}, u32[]{:S(2)}, u32[]{:S(2)}) collective-permute-start(bf16[64,1024]{1,0:T(8,128)(2,1)S(1)} %get-tuple-element.93), channel_id=1, source_target_pairs={{0,24},{8,0},{16,8},{24,16},{32,56},{40,32},{48,40},{56,48},{64,88... | collective-permute-start | bytes 393224 | tf_op jit(solution)/shard_map/ppermute | solution.py:438
  113.9 10.1 %collective-permute-start.11 = (bf16[176,512]{1,0:T(8,128)(2,1)S(1)}, bf16[176,512]{1,0:T(8,128)(2,1)S(1)}, u32[]{:S(2)}, u32[]{:S(2)}) collective-permute-start(bf16[176,512]{1,0:T(8,128)(2,1)S(1)} %get-tuple-element.84), channel_id=1, source_target_pairs={{0,32},{32,64},{64,96},{1,33},{33,65},{65,97},{2,34},{34,66},{66,9... | collective-permute-start | bytes 540680 | tf_op jit(solution)/shard_map/ppermute | solution.py:453
  116.8 7.4 %collective-permute-start.12 = (bf16[176,512]{1,0:T(8,128)(2,1)S(1)}, bf16[176,512]{1,0:T(8,128)(2,1)S(1)}, u32[]{:S(2)}, u32[]{:S(2)}) collective-permute-start(bf16[176,512]{1,0:T(8,128)(2,1)S(1)} %get-tuple-element.85), channel_id=1, source_target_pairs={{32,0},{64,32},{96,64},{33,1},{65,33},{97,65},{34,2},{66,34},{98,6... | collective-permute-start | bytes 540680 | tf_op jit(solution)/shard_map/ppermute | solution.py:454
  118.3 14.5 %collective-permute-start.25 = (bf16[64,1024]{1,0:T(8,128)(2,1)S(1)}, bf16[64,1024]{1,0:T(8,128)(2,1)S(1)}, u32[]{:S(2)}, u32[]{:S(2)}) collective-permute-start(bf16[64,1024]{1,0:T(8,128)(2,1)S(1)} %get-tuple-element.103), channel_id=1, source_target_pairs={{0,4},{4,0},{32,36},{36,32},{64,68},{68,64},{96,100},{100,96},{8,1... | collective-permute-start | bytes 393224 | tf_op jit(solution)/shard_map/ppermute | solution.py:438
  134.0 5.8 %collective-permute-start.26 = (bf16[16,1024]{1,0:T(8,128)(2,1)S(1)}, bf16[16,1024]{1,0:T(8,128)(2,1)S(1)}, u32[]{:S(2)}, u32[]{:S(2)}) collective-permute-start(bf16[16,1024]{1,0:T(8,128)(2,1)S(1)} %get-tuple-element.105), channel_id=1, source_target_pairs={{0,32},{32,64},{64,96},{96,0},{4,36},{36,68},{68,100},{100,4},{8,4... | collective-permute-start | bytes 98312 | tf_op jit(solution)/shard_map/ppermute | solution.py:438
  136.5 4.8 %collective-permute-start.27 = (bf16[16,1024]{1,0:T(8,128)(2,1)S(1)}, bf16[16,1024]{1,0:T(8,128)(2,1)S(1)}, u32[]{:S(2)}, u32[]{:S(2)}) collective-permute-start(bf16[16,1024]{1,0:T(8,128)(2,1)S(1)} %get-tuple-element.106), channel_id=1, source_target_pairs={{0,64},{32,96},{64,0},{96,32},{4,68},{36,100},{68,4},{100,36},{8,7... | collective-permute-start | bytes 98312 | tf_op jit(solution)/shard_map/ppermute | solution.py:438
  136.5 4.8 %collective-permute-start.28 = (bf16[16,1024]{1,0:T(8,128)(2,1)S(1)}, bf16[16,1024]{1,0:T(8,128)(2,1)S(1)}, u32[]{:S(2)}, u32[]{:S(2)}) collective-permute-start(bf16[16,1024]{1,0:T(8,128)(2,1)S(1)} %get-tuple-element.107), channel_id=1, source_target_pairs={{0,96},{32,0},{64,32},{96,64},{4,100},{36,4},{68,36},{100,68},{8,1... | collective-permute-start | bytes 98312 | tf_op jit(solution)/shard_map/ppermute | solution.py:438
  (8 other events, 104.0 us)

commit v3 on v2

--- a/solution.py
+++ b/solution.py
@@ -62,7 +62,7 @@
     return jnp.where(even, a, b)
 
 
-def export_kernel(state_ref, taps_ref, out_ref):
+def export_kernel(state_ref, out_ref):
     cells = state_ref[:, :, 0:LANES].reshape(CELLS, LANES).astype(F32)
     out_ref[...] = jnp.concatenate(
         [cells[at * LANES : (at + 1) * LANES].T[:Q] for at in range(CELLS // LANES)], axis=0
@@ -101,7 +101,7 @@
 
 
 def import_kernel(
-    source_ref, state_ref, weight_ref, fields_ref, one_ref, two_ref, above_ref, below_ref,
+    source_ref, state_ref, weight_ref, fields_ref, one_ref, two_ref, above_ref, below_ref, after_ref,
     forced_ref, send_one_ref, send_two_ref, tiles, cells, left, right, flat,
 ):
     lat, lon = lax.axis_index("lat"), lax.axis_index("lon")
@@ -156,7 +156,7 @@
     for at in range(blocks):
         for tap in range(TAPS * TAPS):
             from_tap = TAPS * TAPS - 1 - tap if flipped else tap
-            spread[at, tap] = jnp.broadcast_to(kernel_ref[pl.ds(BLOCKS * from_tap + lane_from + at, 1), :], (8, LANES))
+            spread[at, tap] = jnp.broadcast_to(kernel_ref[from_tap, lane_from + at : lane_from + at + 1, :], (8, LANES))
 
 
 def fill_rows(pad, at, top, middle, bottom):
@@ -181,38 +181,49 @@
         pad[at, row, LEFT + COLS : LEFT + COLS + RIM, :] = two
 
 
-def convolve(pad, spread, at, emit):
-    for chunk in range(3):
-        sums = {}
-        for row in range(PAD_ROWS):
-            first = chunk * 16 + LEFT - RIM
-            window = [
-                pad[at, row, first + shift : first + shift + 16, :].reshape(2, 8, LANES)
-                for shift in range(TAPS)
-            ]
-            for off in range(TAPS):
-                out_row = row - off
-                if 0 <= out_row < ROWS:
-                    part = window[0] * spread[at, off * TAPS][None]
-                    for shift in range(1, TAPS):
-                        part = part + window[shift] * spread[at, off * TAPS + shift][None]
-                    sums[out_row] = part if off == 0 else sums[out_row] + part
-            if row >= TAPS - 1:
-                out_row = row - (TAPS - 1)
-                emit(out_row, chunk * 16, sums.pop(out_row).reshape(16, LANES))
+PASSES = ((0, 1, 2), (3, 4), (5, 6))
+
+
+def convolve(pad, spread, at, out):
+    for first in (0, 24):
+        cols = slice(first, first + 24)
+        for shifts in PASSES:
+            taps = {
+                (off, shift): spread[at, off * TAPS + shift][None] for off in range(TAPS) for shift in shifts
+            }
+            sums = {}
+            for row in range(PAD_ROWS):
+                start = first + LEFT - RIM
+                window = {
+                    shift: pad[at, row, start + shift : start + shift + 24, :].reshape(3, 8, LANES)
+                    for shift in shifts
+                }
+                for off in range(TAPS):
+                    out_row = row - off
+                    if 0 <= out_row < ROWS:
+                        part = window[shifts[0]] * taps[off, shifts[0]]
+                        for shift in shifts[1:]:
+                            part = part + window[shift] * taps[off, shift]
+                        if off > 0:
+                            part = part + sums[out_row]
+                        elif shifts[0] > 0:
+                            part = part + out[at, out_row, cols, :].reshape(3, 8, LANES)
+                        sums[out_row] = part
+                if row >= TAPS - 1:
+                    out_row = row - (TAPS - 1)
+                    out[at, out_row, cols, :] = sums.pop(out_row).reshape(24, LANES)
 
 
 def conv_wide_kernel(
-    state_ref, one_ref, two_ref, above_ref, below_ref, kernel_ref,
-    upstream_ref, mask_ref, hidden_ref, update_ref, keep_ref, pad, spread,
+    state_ref, one_ref, two_ref, above_ref, below_ref, kernel_ref, after_ref, hidden_ref, pad, spread, *, blocks
 ):
     left, right = sides(one_ref, two_ref)
     above = above_ref[48:80, :].astype(F32)
     below = below_ref[48:80, :].astype(F32)
-    spread_taps(spread, kernel_ref, 1, 3, False)
-    for at in range(3):
-        wide = slice((at + 1) * LANES, (at + 2) * LANES)
-        thin = slice(at * LANES, (at + 1) * LANES)
+    spread_taps(spread, kernel_ref, blocks[0] + 1, len(blocks), False)
+    for at, block in enumerate(blocks):
+        wide = slice((block + 1) * LANES, (block + 2) * LANES)
+        thin = slice(block * LANES, (block + 1) * LANES)
         fill_rows(
             pad, at, above_ref[80:224, thin].astype(F32).reshape(RIM, COLS, LANES),
             state_ref[:, :, wide].astype(F32), below_ref[80:224, thin].astype(F32).reshape(RIM, COLS, LANES),
@@ -220,28 +231,37 @@
         fill_sides(pad, at, left[:, wide], right[:, wide], above[:, thin], below[:, thin])
 
     def one_block(at, carry):
-        def emit(row, col, value):
-            hidden_ref[at, row, col : col + 16, :] = value
-
-        convolve(pad, spread, at, emit)
+        convolve(pad, spread, at, hidden_ref)
         return carry
 
-    lax.fori_loop(0, 3, one_block, 0)
+    lax.fori_loop(0, len(blocks), one_block, 0)
+
+
+def d_active_kernel(
+    upstream_ref, mask_ref, w_out_ref, after_ref, update_ref, keep_ref, by_x_ref, by_y_ref, token_ref
+):
+    token_ref[...] = jnp.zeros((8, LANES), F32)
     mask = jnp.where(lax.axis_index("group") == 1, mask_ref[...].astype(F32), 1.0).T
     for row in range(ROWS):
         rows = slice(row * COLS, (row + 1) * COLS)
         keep_ref[rows, :] = jnp.broadcast_to(mask[:, row : row + 1], (COLS, LANES))
-
-    def one_lane_block(at, carry):
-        lanes = pl.ds(pl.multiple_of(at * LANES, LANES), LANES)
+    for at in range(BLOCKS):
+        lanes = slice(at * LANES, (at + 1) * LANES)
         update_ref[:, lanes] = (keep_ref[...] * upstream_ref[:, lanes].astype(F32)).astype(BF)
-        return carry
-
-    lax.fori_loop(0, BLOCKS, one_lane_block, 0)
+    update = update_ref[...]
+    for step in range(4):
+        mine = slice(step * PART, (step + 1) * PART)
+        chunk = lax.rem(along("x") + step, 4)
+        by_x_ref[:, mine] = dot(update, w_out_ref[0:16, chunk].reshape(PART, CH), 1, 1)
+        chunk = lax.rem(along("y") + step, 4)
+        for part in range(2):
+            rows = w_out_ref[pl.ds(16 + 8 * part + 2 * chunk, 2)].reshape(LANES, CH)
+            spot = slice(step * PART + part * LANES, step * PART + (part + 1) * LANES)
+            by_y_ref[:, spot] = dot(update, rows, 1, 1)
 
 
 def conv_norm_kernel(
-    forced_ref, one_ref, two_ref, above_ref, below_ref, kernel_ref, hidden_ref, gain_ref,
+    forced_ref, one_ref, two_ref, above_ref, below_ref, kernel_ref, hidden_ref, more_ref, gain_ref,
     normed_ref, hat_ref, inv_ref, pad, spread, first,
 ):
     left, right = sides(one_ref, two_ref)
@@ -253,13 +273,10 @@
     )
     fill_sides(pad, 0, left, right, above[144:176], below[144:176])
 
-    def emit(row, col, value):
-        first[row, col : col + 16, :] = value
-
-    convolve(pad, spread, 0, emit)
+    convolve(pad, spread, 0, first)
 
     def one_row(row, carry):
-        parts = [first[row]] + [hidden_ref[at, row] for at in range(3)]
+        parts = [first[0, row], hidden_ref[0, row], more_ref[0, row], more_ref[1, row]]
         centre = jnp.sum(sum(parts[1:], parts[0]), axis=-1, keepdims=True) * (1.0 / CH)
         parts = [part - centre for part in parts]
         squares = [part * part for part in parts]
@@ -290,7 +307,7 @@
 
 
 def mlp_kernel(
-    normed_ref, update_ref, w_in_ref, w_out_ref,
+    normed_ref, update_ref, d_active_ref, w_in_ref, w_out_ref,
     grad0_ref, grad1_ref, grad2_ref, grad3_ref, act_ref, pre_ref, w_in_out_ref, w_out_out_ref,
     *, by_x,
 ):
@@ -309,7 +326,7 @@
         cdf = 0.5 + 0.5 * bent
         act = (value * cdf).astype(BF)
         slope = cdf + (0.5 * value) * (1.0 - bent * bent) * (GELU_A + 3.0 * GELU_B * square)
-        pre = (dot(update, second, 1, 1) * slope).astype(BF)
+        pre = (d_active_ref[:, mine] * slope).astype(BF)
         act_ref[:, mine] = act
         pre_ref[:, mine] = pre
         grad_ref[:, :CH] = dot(pre, normed, 0, 0).astype(BF)
@@ -317,8 +334,9 @@
 
 
 def advance_kernel(
-    act_a_ref, act_b_ref, w_out_a_ref, w_out_b_ref, state_ref, keep_ref, after_ref, advanced_ref, wide
-):
+    act_a_ref, act_b_ref, w_out_a_ref, w_out_b_ref, state_ref, keep_ref, after_ref, advanced_ref, token_ref, wide
+):
+    token_ref[...] = jnp.zeros((8, LANES), F32)
     wide[...] = dot(act_a_ref[...], w_out_a_ref[...], 1, 0) + dot(act_b_ref[...], w_out_b_ref[...], 1, 0)
     for at in range(BLOCKS):
         lanes = slice(at * LANES, (at + 1) * LANES)
@@ -354,7 +372,7 @@
 
 def conv_back_kernel(
     d_hidden_ref, one_ref, two_ref, above_ref, below_ref, kernel_ref, upstream_ref, after_ref,
-    out_ref, pad, spread, held,
+    out_ref, token_ref, pad, spread, held,
 ):
     left, right = sides(one_ref, two_ref)
     spread_taps(spread, kernel_ref, 0, BLOCKS, True)
@@ -368,11 +386,10 @@
         )
         fill_sides(pad, at, left[:, lanes], right[:, lanes], above[144:176], below[144:176])
 
+    token_ref[...] = jnp.zeros((8, LANES), F32)
+
     def one_block(at, carry):
-        def emit(row, col, value):
-            held[at, row, col : col + 16, :] = value
-
-        convolve(pad, spread, at, emit)
+        convolve(pad, spread, at, held)
         return carry
 
     lax.fori_loop(0, BLOCKS, one_block, 0)
@@ -461,13 +478,12 @@
     vm = pltpu.VMEM
     state = states[0]
     upstream = cotangent[0]
-    taps = depth_kernel[0].reshape(TAPS * TAPS * BLOCKS, LANES)
+    taps = depth_kernel[0].reshape(TAPS * TAPS, BLOCKS, LANES)
     sources = source_tiles.reshape(4)
     weights = regrid_weights[0].transpose(0, 2, 1)
 
     (mine,) = run(
-        export_kernel, "export", [shape((48, LANES), BF)], state, taps,
-        views={1: pl.BlockSpec(memory_space=pl.ANY)},
+        export_kernel, "export", [shape((48, LANES), BF)], state,
     )
     fields = lax.ppermute(mine, "group", [(0, 1), (1, 0)])
     one, two = run(
@@ -480,36 +496,47 @@
         scratch=[vm((80, 384), F32)],
     )
     above, below = swap_lat(up, down)
+    anywhere = pl.BlockSpec(memory_space=pl.ANY)
+    update, keep, by_x, by_y, token = run(
+        d_active_kernel, "d_active",
+        [shape((CELLS, CH), BF), shape((CELLS, LANES), F32)] + [shape((CELLS, HALF), F32)] * 2
+        + [shape((8, LANES), F32)],
+        upstream.reshape(CELLS, CH), land_mask, w_out[0].reshape(32, 4, 16, CH), up, views={3: anywhere}, room=12,
+    )
     forced, f_one, f_two = run(
         import_kernel, "import", [shape((CELLS, LANES), BF)] + [shape((48, LANES), BF)] * 2,
-        sources, state, weights, fields, one, two, above, below, smem=1,
+        sources, state, weights, fields, one, two, above, below, token, smem=1, views={8: anywhere},
         scratch=[vm((9, 48, LANES), F32), vm((CELLS, LANES), F32)] + [vm((48, LANES), F32)] * 2
         + [vm((8, CELLS), F32)],
     )
     f_one, f_two = swap_lon(f_one, f_two)
-    hidden, update, keep = run(
-        conv_wide_kernel, "conv_wide",
-        [shape((3, ROWS, COLS, LANES), F32), shape((CELLS, CH), BF), shape((CELLS, LANES), F32)],
-        state, one, two, above, below, taps, upstream.reshape(CELLS, CH), land_mask,
-        scratch=[vm((3, PAD_ROWS, PAD_COLS, LANES), F32), vm((3, 49, 8, LANES), F32)], room=8,
+    (hidden,) = run(
+        functools.partial(conv_wide_kernel, blocks=(0,)), "conv_one", [shape((1, ROWS, COLS, LANES), F32)],
+        state, one, two, above, below, taps, forced, views={6: anywhere},
+        scratch=[vm((1, PAD_ROWS, PAD_COLS, LANES), F32), vm((1, 49, 8, LANES), F32)], room=6,
     )
     f_up, f_down = run(
         rim_pack_kernel, "rim_pack", [shape((176, LANES), BF)] * 2, forced, f_one, f_two, hidden,
         scratch=[vm((32, LANES), F32)], views={3: pl.BlockSpec(memory_space=pl.ANY)},
     )
     f_above, f_below = swap_lat(f_up, f_down)
+    (more,) = run(
+        functools.partial(conv_wide_kernel, blocks=(1, 2)), "conv_two", [shape((2, ROWS, COLS, LANES), F32)],
+        state, one, two, above, below, taps, f_up, views={6: anywhere},
+        scratch=[vm((2, PAD_ROWS, PAD_COLS, LANES), F32), vm((2, 49, 8, LANES), F32)], room=6,
+    )
     normed, hat, inv = run(
         conv_norm_kernel, "conv_norm",
         [shape((ROWS, COLS, CH), BF), shape((ROWS, COLS, CH), F32), shape((ROWS, COLS, LANES), F32)],
-        forced, f_one, f_two, f_above, f_below, taps, hidden, norm_gain,
-        scratch=[vm((1, PAD_ROWS, PAD_COLS, LANES), F32), vm((1, 49, 8, LANES), F32), vm((ROWS, COLS, LANES), F32)],
+        forced, f_one, f_two, f_above, f_below, taps, hidden, more, norm_gain,
+        scratch=[vm((1, PAD_ROWS, PAD_COLS, LANES), F32), vm((1, 49, 8, LANES), F32), vm((1, ROWS, COLS, LANES), F32)],
         room=6,
     )
     normed = normed.reshape(CELLS, CH)
     hat = hat.reshape(CELLS, CH)
     inv = inv.reshape(CELLS, LANES)
 
-    def half(by_x):
+    def half(by_x, d_active):
         if by_x:
             dims, block, at = (2, 16, 4, 16, CH), (1, 16, 4, 16, CH), lambda i: (0, 0, 0, 0, 0)
         else:
@@ -518,29 +545,28 @@
         outs = run(
             functools.partial(mlp_kernel, by_x=by_x), "mlp_x" if by_x else "mlp_y",
             [shape((PART, 2 * CH), BF)] * 4 + [shape((CELLS, HALF), BF)] * 2 + [shape((HALF, CH), BF)] * 2,
-            normed, update, w_in[0].reshape(dims), w_out[0].reshape(dims), views={2: view, 3: view}, room=12,
+            normed, update, d_active, w_in[0].reshape(dims), w_out[0].reshape(dims), views={3: view, 4: view}, room=12,
         )
         return outs[:4], outs[4:]
 
-    grads_b, kept_b = half(False)
+    grads_b, kept_b = half(False, by_y)
     grads_b = around(grads_b, "y")
-    grads_a, kept_a = half(True)
+    grads_a, kept_a = half(True, by_x)
     a_one, a_two = send(grads_a[1], "x", 1), send(grads_a[2], "x", 2)
-    anywhere = pl.BlockSpec(memory_space=pl.ANY)
     d_hidden, d_one, d_two, a_three = run(
         finish_kernel, "finish",
         [shape((CELLS, CH), BF)] + [shape((48, CH), BF)] * 2 + [shape((PART, 2 * CH), BF)],
         kept_a[1], kept_b[1], kept_a[2], kept_b[2], norm_gain, hat, inv, grads_a[3], same={7: 3},
         scratch=[vm((CELLS, CH), F32)] + [vm((48, CH), F32)] * 2, room=12,
     )
-    (advanced,) = run(
-        advance_kernel, "advance", [shape((CELLS, CH), BF)],
+    advanced, token = run(
+        advance_kernel, "advance", [shape((CELLS, CH), BF), shape((8, LANES), F32)],
         kept_a[0], kept_b[0], kept_a[3], kept_b[3], state.reshape(CELLS, CH), keep, d_hidden,
         views={6: anywhere}, scratch=[vm((CELLS, CH), F32)], room=12,
     )
     grads_b = run(
         functools.partial(sum_four_kernel, by_x=False), "sum_y", [shape((64, 2 * CH), BF)] * 4,
-        *grads_b, advanced, views={4: anywhere}, scratch=[vm((2, 2, 4, 16, 2 * CH), BF)],
+        *grads_b, token, views={4: anywhere}, scratch=[vm((2, 2, 4, 16, 2 * CH), BF)],
     )
     d_one, d_two = swap_lon(d_one, d_two)
     grads_a = [grads_a[0], a_one, a_two, send(a_three, "x", 3)]
@@ -560,8 +586,8 @@
         scratch=[vm((4, 2, 16, 2 * CH), BF)],
     )
     other = send(other, "z_hi", 1)
-    (state_grad,) = run(
-        conv_back_kernel, "conv_back", [shape((ROWS, COLS, CH), BF)],
+    state_grad, token = run(
+        conv_back_kernel, "conv_back", [shape((ROWS, COLS, CH), BF), shape((8, LANES), F32)],
         d_hidden, d_one, d_two, d_above, d_below, taps, upstream, mine, views={7: anywhere},
         scratch=[
             vm((BLOCKS, PAD_ROWS, PAD_COLS, LANES), F32), vm((BLOCKS, 49, 8, LANES), F32),
@@ -570,7 +596,7 @@
         room=10,
     )
     grads = run(
-        sum_two_kernel, "sum_z_hi", [shape((16, 2 * CH), BF)] * 4, mine, other, state_grad, views={2: anywhere},
+        sum_two_kernel, "sum_z_hi", [shape((16, 2 * CH), BF)] * 4, mine, other, token, views={2: anywhere},
         scratch=[vm((4, 16, 2 * CH), BF)],
     )
     grads = around(grads, "z_lo")

time: 143 us -> 140 us (0.979)
  starting transfers between devices: 80.9 us -> 88.3 us
  waiting for transfers between devices: 17 us -> 11.2 us
  Pallas kernels: 38.6 us -> 36.4 us
    ppermute x3, starting transfers between devices: 24.1 us -> 29.6 us  [swap_lon(): two = lax.ppermute(two, 'lon', other)]
    ppermute x3, waiting for transfers between devices: 8.92 us -> 4.67 us  [swap_lat(): below = lax.ppermute(up, 'lat', [(i + 1, i) for i in range(3)])]
    pallas_call x18 -> x20, Pallas kernels: 38.6 us -> 36.4 us  [run(): pl.pallas_call(kernel, out_shape=outs, grid=(1,), in_specs=in_specs, out_...]
    ppermute x3, waiting for transfers between devices: 1.99 us -> 0.01 us  [swap_lat(): above = lax.ppermute(down, 'lat', [(i, i + 1) for i in range(3)])]
    ppermute x3, starting transfers between devices: 9.84 us -> 11.3 us  [swap_lat(): above = lax.ppermute(down, 'lat', [(i, i + 1) for i in range(3)])]
  transfers between devices with their start and end apart: 29 -> 29, of which waited for: 10 -> 8; matrix products, arithmetic and copies ran while one was open for 0% -> 0% of each run, Pallas kernels for 19% -> 18%
where the time goes in v3:
time: 140 us; the launch traced here: 139 us
  starting transfers between devices  88.3 us (63%)
  Pallas kernels  36.4 us (26%)
  waiting for transfers between devices  11.2 us (8%)
  local copies, waits for them, and re-layouts  2.3 us (2%)
    ppermute x16, starting transfers between devices, send(): return lax.ppermute(piece, ('lat', 'lon'), pairs)  41.1 us
    pallas_call x20, Pallas kernels, run(): pl.pallas_call(kernel, out_shape=outs, grid=(1,), in_specs=in_specs, out_...  36.4 us
    ppermute x3, starting transfers between devices, swap_lon(): two = lax.ppermute(two, 'lon', other)  29.6 us
    ppermute x3, starting transfers between devices, swap_lat(): above = lax.ppermute(down, 'lat', [(i, i + 1) for i in range(3)])  11.3 us
    ppermute x3, waiting for transfers between devices, swap_lat(): below = lax.ppermute(up, 'lat', [(i + 1, i) for i in range(3)])  4.67 us
    ppermute x3, starting transfers between devices, swap_lat(): below = lax.ppermute(up, 'lat', [(i + 1, i) for i in range(3)])  4.19 us
    ppermute x3, waiting for transfers between devices, swap_lon(): two = lax.ppermute(two, 'lon', other)  3.76 us
  transfers between devices with their start and end apart: 29, of which 8 were waited for; matrix products, arithmetic and copies ran while one was open for 0% of the time, Pallas kernels for 18%

profile of v3, /device:TPU:6, one launch (start us, length us, event | category | flops | bytes accessed | tf_op | source)
XLA Modules:
  0.0 139.2 jit_solution(17708554768361137480)
XLA Ops:
  4.1 7.8 %collective-permute-start.2 = (bf16[48,512]{1,0:T(8,128)(2,1)S(1)}, bf16[48,512]{1,0:T(8,128)(2,1)S(1)}, u32[]{:S(2)}, u32[]{:S(2)}) collective-permute-start(bf16[48,512]{1,0:T(8,128)(2,1)S(1)} %get-tuple-element.64), channel_id=1, source_target_pairs={{0,31},{1,2},{2,1},{3,4},{4,3},{5,6},{6,5},{7,8},{8,7},{9,10},{10,... | collective-permute-start | bytes 147464 | tf_op jit(solution)/shard_map/ppermute | solution.py:465
  11.8 2.4 %collective-permute-done.2.two_ref = bf16[48,512]{1,0:T(8,128)(2,1)S(1)} collective-permute-done((bf16[48,512]{1,0:T(8,128)(2,1)S(1)}, bf16[48,512]{1,0:T(8,128)(2,1)S(1)}, u32[]{:S(2)}, u32[]{:S(2)}) %collective-permute-start.2) | collective-permute-done | bytes 49184 | tf_op jit(solution)/shard_map/ppermute | solution.py:465
  14.4 3.9 %collective-permute-start.3 = (bf16[224,384]{1,0:T(8,128)(2,1)S(1)}, bf16[224,384]{1,0:T(8,128)(2,1)S(1)}, u32[]{:S(2)}, u32[]{:S(2)}) collective-permute-start(bf16[224,384]{1,0:T(8,128)(2,1)S(1)} %get-tuple-element.65), channel_id=1, source_target_pairs={{0,32},{32,64},{64,96},{1,33},{33,65},{65,97},{2,34},{34,66},{66,9... | collective-permute-start | bytes 516104 | tf_op jit(solution)/shard_map/ppermute | solution.py:470
  20.7 2.8 %d_active.1 = (bf16[768,512]{1,0:T(8,128)(2,1)S(1)}, f32[768,128]{1,0:T(8,128)S(1)}, f32[768,1024]{1,0:T(8,128)S(1)}, f32[768,1024]{1,0:T(8,128)S(1)}, f32[8,128]{1,0:T(8,128)S(1)}) custom-call(bf16[768,512]{1,0:T(8,128)(2,1)S(1)} %bitcast.35, s32[16,48]{1,0:T(8,128)S(1)} %copy-done.8, bf16[32,4,16,512]{3,2,1,0:T(8,128)(2,1)S(1)} %bitcast.28, ...), custom_call_target="tpu_custom_call" | custom-call | bytes 1024 | tf_op jit(solution)/shard_map/d_active/pallas_call | solution.py:39
  23.5 2.1 %collective-permute-done.4.below_ref = bf16[224,384]{1,0:T(8,128)(2,1)S(1)} collective-permute-done((bf16[224,384]{1,0:T(8,128)(2,1)S(1)}, bf16[224,384]{1,0:T(8,128)(2,1)S(1)}, u32[]{:S(2)}, u32[]{:S(2)}) %collective-permute-start.4) | collective-permute-done | bytes 172064 | tf_op jit(solution)/shard_map/ppermute | solution.py:471
  26.5 7.1 %collective-permute-start.6 = (bf16[48,128]{1,0:T(8,128)(2,1)S(1)}, bf16[48,128]{1,0:T(8,128)(2,1)S(1)}, u32[]{:S(2)}, u32[]{:S(2)}) collective-permute-start(bf16[48,128]{1,0:T(8,128)(2,1)S(1)} %get-tuple-element.70), channel_id=1, source_target_pairs={{0,31},{1,2},{2,1},{3,4},{4,3},{5,6},{6,5},{7,8},{8,7},{9,10},{10,... | collective-permute-start | bytes 36872 | tf_op jit(solution)/shard_map/ppermute | solution.py:465
  36.3 3.8 %collective-permute-start.7 = (bf16[176,128]{1,0:T(8,128)(2,1)S(1)}, bf16[176,128]{1,0:T(8,128)(2,1)S(1)}, u32[]{:S(2)}, u32[]{:S(2)}) collective-permute-start(bf16[176,128]{1,0:T(8,128)(2,1)S(1)} %get-tuple-element.71), channel_id=1, source_target_pairs={{0,32},{32,64},{64,96},{1,33},{33,65},{65,97},{2,34},{34,66},{66,9... | collective-permute-start | bytes 135176 | tf_op jit(solution)/shard_map/ppermute | solution.py:470
  40.1 1.6 %collective-permute-start.8 = (bf16[176,128]{1,0:T(8,128)(2,1)S(1)}, bf16[176,128]{1,0:T(8,128)(2,1)S(1)}, u32[]{:S(2)}, u32[]{:S(2)}) collective-permute-start(bf16[176,128]{1,0:T(8,128)(2,1)S(1)} %get-tuple-element.72.after_ref), channel_id=1, source_target_pairs={{32,0},{64,32},{96,64},{33,1},{65,33},{97,65},{34,2},{66,34},{98,6... | collective-permute-start | bytes 135176 | tf_op jit(solution)/shard_map/ppermute | solution.py:471
  41.7 2.7 %conv_two.1.more_ref = f32[2,16,48,128]{3,2,1,0:T(8,128)S(1)} custom-call(bf16[16,48,512]{2,1,0:T(8,128)(2,1)S(1)} %bitcast.26, bf16[48,512]{1,0:T(8,128)(2,1)S(1)} %collective-permute-done.1.one_ref, bf16[48,512]{1,0:T(8,128)(2,1)S(1)} %collective-permute-done.2.two_ref, bf16[224,384]{1,0:T(8,128)(2,1)S(1)} %collective-permute-done.3.above_ref, ...), custom_call_target="tpu_custom_call" | custom-call | bytes 1024 | tf_op jit(solution)/shard_map/conv_two/pallas_call | solution.py:39
  44.4 1.8 %collective-permute-done.8.below_ref = bf16[176,128]{1,0:T(8,128)(2,1)S(1)} collective-permute-done((bf16[176,128]{1,0:T(8,128)(2,1)S(1)}, bf16[176,128]{1,0:T(8,128)(2,1)S(1)}, u32[]{:S(2)}, u32[]{:S(2)}) %collective-permute-start.8) | collective-permute-done | bytes 45088 | tf_op jit(solution)/shard_map/ppermute | solution.py:471
  46.2 4.3 %conv_norm.1 = (bf16[16,48,512]{2,1,0:T(8,128)(2,1)S(1)}, f32[16,48,512]{2,1,0:T(8,128)S(1)}, f32[16,48,128]{2,1,0:T(8,128)S(1)}) custom-call(bf16[768,128]{1,0:T(8,128)(2,1)S(1)} %get-tuple-element.68.after_ref.cells_ref.forced_ref, bf16[48,128]{1,0:T(8,128)(2,1)S(1)} %collective-permute-done.5.one_ref, bf16[48,128]{1,0:T(8,128)(2,1)S(1)} %collective-permute-done.6.two_ref, ...), custom_call_target="tpu_custom_call" | custom-call | bytes 1024 | tf_op jit(solution)/shard_map/conv_norm/pallas_call | solution.py:39
  50.5 4.8 %mlp_y.1 = (bf16[256,1024]{1,0:T(8,128)(2,1)S(1)}, bf16[256,1024]{1,0:T(8,128)(2,1)S(1)}, bf16[256,1024]{1,0:T(8,128)(2,1)S(1)}, bf16[256,1024]{1,0:T(8,128)(2,1...) custom-call(bf16[768,512]{1,0:T(8,128)(2,1)S(1)} %bitcast.33, ...), custom_call_target="tpu_custom_call" | custom-call | bytes 1024 | tf_op jit(solution)/shard_map/mlp_y/pallas_call | solution.py:39
  55.3 1.7 %collective-permute-start.19 = (bf16[256,1024]{1,0:T(8,128)(2,1)S(1)}, bf16[256,1024]{1,0:T(8,128)(2,1)S(1)}, u32[]{:S(2)}, u32[]{:S(2)}) collective-permute-start(bf16[256,1024]{1,0:T(8,128)(2,1)S(1)} %get-tuple-element.104), channel_id=1, source_target_pairs={{0,8},{8,16},{16,24},{24,0},{32,40},{40,48},{48,56},{56,32},{64,72... | collective-permute-start | bytes 1572872 | tf_op jit(solution)/shard_map/ppermute | solution.py:455
  57.0 2.9 %collective-permute-start.20 = (bf16[256,1024]{1,0:T(8,128)(2,1)S(1)}, bf16[256,1024]{1,0:T(8,128)(2,1)S(1)}, u32[]{:S(2)}, u32[]{:S(2)}) collective-permute-start(bf16[256,1024]{1,0:T(8,128)(2,1)S(1)} %get-tuple-element.105), channel_id=1, source_target_pairs={{0,16},{8,24},{16,0},{24,8},{32,48},{40,56},{48,32},{56,40},{64,80... | collective-permute-start | bytes 1572872 | tf_op jit(solution)/shard_map/ppermute | solution.py:455
  59.9 1.4 collective-permute-start.21
  61.3 4.7 %mlp_x.1 = (bf16[256,1024]{1,0:T(8,128)(2,1)S(1)}, bf16[256,1024]{1,0:T(8,128)(2,1)S(1)}, bf16[256,1024]{1,0:T(8,128)(2,1)S(1)}, bf16[256,1024]{1,0:T(8,128)(2,1...) custom-call(bf16[768,512]{1,0:T(8,128)(2,1)S(1)} %bitcast.34, ...), custom_call_target="tpu_custom_call" | custom-call | bytes 1024 | tf_op jit(solution)/shard_map/mlp_x/pallas_call | solution.py:39
  66.0 3.8 %finish.1 = (bf16[768,512]{1,0:T(8,128)(2,1)S(1)}, bf16[48,512]{1,0:T(8,128)(2,1)S(1)}, bf16[48,512]{1,0:T(8,128)(2,1)S(1)}, bf16[256,1024]{1,0:T(8,128)(2,1)S(1)}) custom-call(bf16[768,1024]{1,0:T(8,128)(2,1)S(1)} %get-tuple-element.82.pre_a_ref, bf16[768,1024]{1,0:T(8,128)(2,1)S(1)} %get-tuple-element.83.pre_b_ref, ...), custom_call_target="tpu_custom_call", output_to_operand_aliasing={{3}: (7, {})} | custom-call | bytes 1024 | tf_op jit(solution)/shard_map/finish/pallas_call | solution.py:39
  69.9 3.4 %collective-permute-start.13 = (bf16[256,1024]{1,0:T(8,128)(2,1)S(1)}, bf16[256,1024]{1,0:T(8,128)(2,1)S(1)}, u32[]{:S(2)}, u32[]{:S(2)}) collective-permute-start(bf16[256,1024]{1,0:T(8,128)(2,1)S(1)} %get-tuple-element.96), channel_id=1, source_target_pairs={{0,1},{1,2},{2,3},{3,0},{32,33},{33,34},{34,35},{35,32},{64,65},{6... | collective-permute-start | bytes 1572872 | tf_op jit(solution)/shard_map/ppermute | solution.py:455
  73.2 2.2 %collective-permute-start.14 = (bf16[256,1024]{1,0:T(8,128)(2,1)S(1)}, bf16[256,1024]{1,0:T(8,128)(2,1)S(1)}, u32[]{:S(2)}, u32[]{:S(2)}) collective-permute-start(bf16[256,1024]{1,0:T(8,128)(2,1)S(1)} %get-tuple-element.97), channel_id=1, source_target_pairs={{0,2},{1,3},{2,0},{3,1},{32,34},{33,35},{34,32},{35,33},{64,66},{6... | collective-permute-start | bytes 1572872 | tf_op jit(solution)/shard_map/ppermute | solution.py:455
  75.5 2.7 %advance.1 = (bf16[768,512]{1,0:T(8,128)(2,1)}, f32[8,128]{1,0:T(8,128)S(1)}) custom-call(bf16[768,1024]{1,0:T(8,128)(2,1)S(1)} %get-tuple-element.76.act_a_ref, bf16[768,1024]{1,0:T(8,128)(2,1)S(1)} %get-tuple-element.78.act_b_ref, bf16[1024,512]{1,0:T(8,128)(2,1)S(1)} %get-tuple-element.79.w_out_a_ref, ...), custom_call_target="tpu_custom_call" | custom-call | bytes 1024 | tf_op jit(solution)/shard_map/advance/pallas_call | solution.py:39
  78.7 6.9 %collective-permute-start.22 = (bf16[64,1024]{1,0:T(8,128)(2,1)S(1)}, bf16[64,1024]{1,0:T(8,128)(2,1)S(1)}, u32[]{:S(2)}, u32[]{:S(2)}) collective-permute-start(bf16[64,1024]{1,0:T(8,128)(2,1)S(1)} %get-tuple-element.109), channel_id=1, source_target_pairs={{0,1},{1,2},{2,3},{3,0},{32,33},{33,34},{34,35},{35,32},{64,65},{6... | collective-permute-start | bytes 393224 | tf_op jit(solution)/shard_map/ppermute | solution.py:455
  86.5 14.8 %collective-permute-start.10 = (bf16[48,512]{1,0:T(8,128)(2,1)S(1)}, bf16[48,512]{1,0:T(8,128)(2,1)S(1)}, u32[]{:S(2)}, u32[]{:S(2)}) collective-permute-start(bf16[48,512]{1,0:T(8,128)(2,1)S(1)} %get-tuple-element.92), channel_id=1, source_target_pairs={{0,31},{1,2},{2,1},{3,4},{4,3},{5,6},{6,5},{7,8},{8,7},{9,10},{10,... | collective-permute-start | bytes 147464 | tf_op jit(solution)/shard_map/ppermute | solution.py:465
  101.3 4.5 %collective-permute-start.24 = (bf16[64,1024]{1,0:T(8,128)(2,1)S(1)}, bf16[64,1024]{1,0:T(8,128)(2,1)S(1)}, u32[]{:S(2)}, u32[]{:S(2)}) collective-permute-start(bf16[64,1024]{1,0:T(8,128)(2,1)S(1)} %get-tuple-element.111), channel_id=1, source_target_pairs={{0,3},{1,0},{2,1},{3,2},{32,35},{33,32},{34,33},{35,34},{64,67},{6... | collective-permute-start | bytes 393224 | tf_op jit(solution)/shard_map/ppermute | solution.py:455
  106.4 1.5 %collective-permute-start.16 = (bf16[64,1024]{1,0:T(8,128)(2,1)S(1)}, bf16[64,1024]{1,0:T(8,128)(2,1)S(1)}, u32[]{:S(2)}, u32[]{:S(2)}) collective-permute-start(bf16[64,1024]{1,0:T(8,128)(2,1)S(1)} %get-tuple-element.100), channel_id=1, source_target_pairs={{0,8},{8,16},{16,24},{24,0},{32,40},{40,48},{48,56},{56,32},{64,72... | collective-permute-start | bytes 393224 | tf_op jit(solution)/shard_map/ppermute | solution.py:455
  108.0 1.9 %collective-permute-start.17 = (bf16[64,1024]{1,0:T(8,128)(2,1)S(1)}, bf16[64,1024]{1,0:T(8,128)(2,1)S(1)}, u32[]{:S(2)}, u32[]{:S(2)}) collective-permute-start(bf16[64,1024]{1,0:T(8,128)(2,1)S(1)} %get-tuple-element.101), channel_id=1, source_target_pairs={{0,16},{8,24},{16,0},{24,8},{32,48},{40,56},{48,32},{56,40},{64,80... | collective-permute-start | bytes 393224 | tf_op jit(solution)/shard_map/ppermute | solution.py:455
  109.9 2.5 %collective-permute-start.18 = (bf16[64,1024]{1,0:T(8,128)(2,1)S(1)}, bf16[64,1024]{1,0:T(8,128)(2,1)S(1)}, u32[]{:S(2)}, u32[]{:S(2)}) collective-permute-start(bf16[64,1024]{1,0:T(8,128)(2,1)S(1)} %get-tuple-element.102), channel_id=1, source_target_pairs={{0,24},{8,0},{16,8},{24,16},{32,56},{40,32},{48,40},{56,48},{64,88... | collective-permute-start | bytes 393224 | tf_op jit(solution)/shard_map/ppermute | solution.py:455
  112.4 3.7 %collective-permute-start.11 = (bf16[176,512]{1,0:T(8,128)(2,1)S(1)}, bf16[176,512]{1,0:T(8,128)(2,1)S(1)}, u32[]{:S(2)}, u32[]{:S(2)}) collective-permute-start(bf16[176,512]{1,0:T(8,128)(2,1)S(1)} %get-tuple-element.93), channel_id=1, source_target_pairs={{0,32},{32,64},{64,96},{1,33},{33,65},{65,97},{2,34},{34,66},{66,9... | collective-permute-start | bytes 540680 | tf_op jit(solution)/shard_map/ppermute | solution.py:470
  117.7 6.0 %collective-permute-start.25 = (bf16[64,1024]{1,0:T(8,128)(2,1)S(1)}, bf16[64,1024]{1,0:T(8,128)(2,1)S(1)}, u32[]{:S(2)}, u32[]{:S(2)}) collective-permute-start(bf16[64,1024]{1,0:T(8,128)(2,1)S(1)} %get-tuple-element.114), channel_id=1, source_target_pairs={{0,4},{4,0},{32,36},{36,32},{64,68},{68,64},{96,100},{100,96},{8,1... | collective-permute-start | bytes 393224 | tf_op jit(solution)/shard_map/ppermute | solution.py:455
  124.5 6.3 %conv_back.1 = (bf16[16,48,512]{2,1,0:T(8,128)(2,1)}, f32[8,128]{1,0:T(8,128)S(1)}) custom-call(bf16[768,512]{1,0:T(8,128)(2,1)S(1)} %get-tuple-element.89.after_ref.cells_ref.after.d_hidden_ref, bf16[48,512]{1,0:T(8,128)(2,1)S(1)} %collective-permute-done.9.one_ref.after_ref, bf16[48,512]{1,0:T(8,128)(2,1)S(1)} %collective-permute-done.10.two_ref, ...), custom_call_target="tpu_custom_call" | custom-call | bytes 1024 | tf_op jit(solution)/shard_map/conv_back/pallas_call | solution.py:39
  130.9 1.9 %collective-permute-start.26 = (bf16[16,1024]{1,0:T(8,128)(2,1)S(1)}, bf16[16,1024]{1,0:T(8,128)(2,1)S(1)}, u32[]{:S(2)}, u32[]{:S(2)}) collective-permute-start(bf16[16,1024]{1,0:T(8,128)(2,1)S(1)} %get-tuple-element.117), channel_id=1, source_target_pairs={{0,32},{32,64},{64,96},{96,0},{4,36},{36,68},{68,100},{100,4},{8,4... | collective-permute-start | bytes 98312 | tf_op jit(solution)/shard_map/ppermute | solution.py:455
  132.8 1.4 %collective-permute-start.27 = (bf16[16,1024]{1,0:T(8,128)(2,1)S(1)}, bf16[16,1024]{1,0:T(8,128)(2,1)S(1)}, u32[]{:S(2)}, u32[]{:S(2)}) collective-permute-start(bf16[16,1024]{1,0:T(8,128)(2,1)S(1)} %get-tuple-element.118), channel_id=1, source_target_pairs={{0,64},{32,96},{64,0},{96,32},{4,68},{36,100},{68,4},{100,36},{8,7... | collective-permute-start | bytes 98312 | tf_op jit(solution)/shard_map/ppermute | solution.py:455
  134.2 2.8 %collective-permute-start.28 = (bf16[16,1024]{1,0:T(8,128)(2,1)S(1)}, bf16[16,1024]{1,0:T(8,128)(2,1)S(1)}, u32[]{:S(2)}, u32[]{:S(2)}) collective-permute-start(bf16[16,1024]{1,0:T(8,128)(2,1)S(1)} %get-tuple-element.119), channel_id=1, source_target_pairs={{0,96},{32,0},{64,32},{96,64},{4,100},{36,4},{68,36},{100,68},{8,1... | collective-permute-start | bytes 98312 | tf_op jit(solution)/shard_map/ppermute | solution.py:455
  (68 shorter events, 16.4 us)
Async XLA Ops:
  1.8 17.8 %copy-start.2 = (bf16[1,2048,512]{2,1,0:T(8,128)(2,1)S(1)}, bf16[1,2048,512]{2,1,0:T(8,128)(2,1)}, u32[]{:S(2)}) copy-start(bf16[1,2048,512]{2,1,0:T(8,128)(2,1)} %param.14) | copy-start | bytes 6291460
  1.8 17.8 %copy-start.8 = (s32[16,48]{1,0:T(8,128)S(1)}, s32[16,48]{1,0:T(8,128)}, u32[]{:S(2)}) copy-start(s32[16,48]{1,0:T(8,128)} %mask_ref.1) | copy-start | bytes 9220
  1.9 1.2 collective-permute-start
  3.2 8.7 %collective-permute-start.1 = (bf16[48,512]{1,0:T(8,128)(2,1)S(1)}, bf16[48,512]{1,0:T(8,128)(2,1)S(1)}, u32[]{:S(2)}, u32[]{:S(2)}) collective-permute-start(bf16[48,512]{1,0:T(8,128)(2,1)S(1)} %get-tuple-element.63), channel_id=1, source_target_pairs={{0,1},{1,0},{2,3},{3,2},{4,5},{5,4},{6,7},{7,6},{8,9},{9,8},{10,11... | collective-permute-start | bytes 147464 | tf_op jit(solution)/shard_map/ppermute | solution.py:466
  4.1 10.2 %collective-permute-start.2 = (bf16[48,512]{1,0:T(8,128)(2,1)S(1)}, bf16[48,512]{1,0:T(8,128)(2,1)S(1)}, u32[]{:S(2)}, u32[]{:S(2)}) collective-permute-start(bf16[48,512]{1,0:T(8,128)(2,1)S(1)} %get-tuple-element.64), channel_id=1, source_target_pairs={{0,31},{1,2},{2,1},{3,4},{4,3},{5,6},{6,5},{7,8},{8,7},{9,10},{10,... | collective-permute-start | bytes 147464 | tf_op jit(solution)/shard_map/ppermute | solution.py:465
  14.4 9.1 %collective-permute-start.3 = (bf16[224,384]{1,0:T(8,128)(2,1)S(1)}, bf16[224,384]{1,0:T(8,128)(2,1)S(1)}, u32[]{:S(2)}, u32[]{:S(2)}) collective-permute-start(bf16[224,384]{1,0:T(8,128)(2,1)S(1)} %get-tuple-element.65), channel_id=1, source_target_pairs={{0,32},{32,64},{64,96},{1,33},{33,65},{65,97},{2,34},{34,66},{66,9... | collective-permute-start | bytes 516104 | tf_op jit(solution)/shard_map/ppermute | solution.py:470
  18.2 7.3 %collective-permute-start.4 = (bf16[224,384]{1,0:T(8,128)(2,1)S(1)}, bf16[224,384]{1,0:T(8,128)(2,1)S(1)}, u32[]{:S(2)}, u32[]{:S(2)}) collective-permute-start(bf16[224,384]{1,0:T(8,128)(2,1)S(1)} %get-tuple-element.66.after_ref), channel_id=1, source_target_pairs={{32,0},{64,32},{96,64},{33,1},{65,33},{97,65},{34,2},{66,34},{98,6... | collective-permute-start | bytes 516104 | tf_op jit(solution)/shard_map/ppermute | solution.py:471
  26.4 8.6 %collective-permute-start.5 = (bf16[48,128]{1,0:T(8,128)(2,1)S(1)}, bf16[48,128]{1,0:T(8,128)(2,1)S(1)}, u32[]{:S(2)}, u32[]{:S(2)}) collective-permute-start(bf16[48,128]{1,0:T(8,128)(2,1)S(1)} %get-tuple-element.69), channel_id=1, source_target_pairs={{0,1},{1,0},{2,3},{3,2},{4,5},{5,4},{6,7},{7,6},{8,9},{9,8},{10,11... | collective-permute-start | bytes 36872 | tf_op jit(solution)/shard_map/ppermute | solution.py:466
  26.5 9.8 %collective-permute-start.6 = (bf16[48,128]{1,0:T(8,128)(2,1)S(1)}, bf16[48,128]{1,0:T(8,128)(2,1)S(1)}, u32[]{:S(2)}, u32[]{:S(2)}) collective-permute-start(bf16[48,128]{1,0:T(8,128)(2,1)S(1)} %get-tuple-element.70), channel_id=1, source_target_pairs={{0,31},{1,2},{2,1},{3,4},{4,3},{5,6},{6,5},{7,8},{8,7},{9,10},{10,... | collective-permute-start | bytes 36872 | tf_op jit(solution)/shard_map/ppermute | solution.py:465
  36.3 8.1 %collective-permute-start.7 = (bf16[176,128]{1,0:T(8,128)(2,1)S(1)}, bf16[176,128]{1,0:T(8,128)(2,1)S(1)}, u32[]{:S(2)}, u32[]{:S(2)}) collective-permute-start(bf16[176,128]{1,0:T(8,128)(2,1)S(1)} %get-tuple-element.71), channel_id=1, source_target_pairs={{0,32},{32,64},{64,96},{1,33},{33,65},{65,97},{2,34},{34,66},{66,9... | collective-permute-start | bytes 135176 | tf_op jit(solution)/shard_map/ppermute | solution.py:470
  40.1 6.1 %collective-permute-start.8 = (bf16[176,128]{1,0:T(8,128)(2,1)S(1)}, bf16[176,128]{1,0:T(8,128)(2,1)S(1)}, u32[]{:S(2)}, u32[]{:S(2)}) collective-permute-start(bf16[176,128]{1,0:T(8,128)(2,1)S(1)} %get-tuple-element.72.after_ref), channel_id=1, source_target_pairs={{32,0},{64,32},{96,64},{33,1},{65,33},{97,65},{34,2},{66,34},{98,6... | collective-permute-start | bytes 135176 | tf_op jit(solution)/shard_map/ppermute | solution.py:471
  55.3 17.9 %collective-permute-start.19 = (bf16[256,1024]{1,0:T(8,128)(2,1)S(1)}, bf16[256,1024]{1,0:T(8,128)(2,1)S(1)}, u32[]{:S(2)}, u32[]{:S(2)}) collective-permute-start(bf16[256,1024]{1,0:T(8,128)(2,1)S(1)} %get-tuple-element.104), channel_id=1, source_target_pairs={{0,8},{8,16},{16,24},{24,0},{32,40},{40,48},{48,56},{56,32},{64,72... | collective-permute-start | bytes 1572872 | tf_op jit(solution)/shard_map/ppermute | solution.py:455
  57.0 21.1 %collective-permute-start.20 = (bf16[256,1024]{1,0:T(8,128)(2,1)S(1)}, bf16[256,1024]{1,0:T(8,128)(2,1)S(1)}, u32[]{:S(2)}, u32[]{:S(2)}) collective-permute-start(bf16[256,1024]{1,0:T(8,128)(2,1)S(1)} %get-tuple-element.105), channel_id=1, source_target_pairs={{0,16},{8,24},{16,0},{24,8},{32,48},{40,56},{48,32},{56,40},{64,80... | collective-permute-start | bytes 1572872 | tf_op jit(solution)/shard_map/ppermute | solution.py:455
  59.9 18.2 %collective-permute-start.21 = (bf16[256,1024]{1,0:T(8,128)(2,1)S(1)}, bf16[256,1024]{1,0:T(8,128)(2,1)S(1)}, u32[]{:S(2)}, u32[]{:S(2)}) collective-permute-start(bf16[256,1024]{1,0:T(8,128)(2,1)S(1)} %get-tuple-element.106), channel_id=1, source_target_pairs={{0,24},{8,0},{16,8},{24,16},{32,56},{40,32},{48,40},{56,48},{64,88... | collective-permute-start | bytes 1572872 | tf_op jit(solution)/shard_map/ppermute | solution.py:455
  69.8 16.7 %collective-permute-start.15 = (bf16[256,1024]{1,0:T(8,128)(2,1)S(1)}, bf16[256,1024]{1,0:T(8,128)(2,1)S(1)}, u32[]{:S(2)}, u32[]{:S(2)}) collective-permute-start(bf16[256,1024]{1,0:T(8,128)(2,1)S(1)} %get-tuple-element.98), channel_id=1, source_target_pairs={{0,3},{1,0},{2,1},{3,2},{32,35},{33,32},{34,33},{35,34},{64,67},{6... | collective-permute-start | bytes 1572872 | tf_op jit(solution)/shard_map/ppermute | solution.py:455
  69.9 31.4 %collective-permute-start.13 = (bf16[256,1024]{1,0:T(8,128)(2,1)S(1)}, bf16[256,1024]{1,0:T(8,128)(2,1)S(1)}, u32[]{:S(2)}, u32[]{:S(2)}) collective-permute-start(bf16[256,1024]{1,0:T(8,128)(2,1)S(1)} %get-tuple-element.96), channel_id=1, source_target_pairs={{0,1},{1,2},{2,3},{3,0},{32,33},{33,34},{34,35},{35,32},{64,65},{6... | collective-permute-start | bytes 1572872 | tf_op jit(solution)/shard_map/ppermute | solution.py:455
  73.2 28.1 %collective-permute-start.14 = (bf16[256,1024]{1,0:T(8,128)(2,1)S(1)}, bf16[256,1024]{1,0:T(8,128)(2,1)S(1)}, u32[]{:S(2)}, u32[]{:S(2)}) collective-permute-start(bf16[256,1024]{1,0:T(8,128)(2,1)S(1)} %get-tuple-element.97), channel_id=1, source_target_pairs={{0,2},{1,3},{2,0},{3,1},{32,34},{33,35},{34,32},{35,33},{64,66},{6... | collective-permute-start | bytes 1572872 | tf_op jit(solution)/shard_map/ppermute | solution.py:455
  78.7 31.2 %collective-permute-start.22 = (bf16[64,1024]{1,0:T(8,128)(2,1)S(1)}, bf16[64,1024]{1,0:T(8,128)(2,1)S(1)}, u32[]{:S(2)}, u32[]{:S(2)}) collective-permute-start(bf16[64,1024]{1,0:T(8,128)(2,1)S(1)} %get-tuple-element.109), channel_id=1, source_target_pairs={{0,1},{1,2},{2,3},{3,0},{32,33},{33,34},{34,35},{35,32},{64,65},{6... | collective-permute-start | bytes 393224 | tf_op jit(solution)/shard_map/ppermute | solution.py:455
  85.6 20.9 %collective-permute-start.9 = (bf16[48,512]{1,0:T(8,128)(2,1)S(1)}, bf16[48,512]{1,0:T(8,128)(2,1)S(1)}, u32[]{:S(2)}, u32[]{:S(2)}) collective-permute-start(bf16[48,512]{1,0:T(8,128)(2,1)S(1)} %get-tuple-element.91), channel_id=1, source_target_pairs={{0,1},{1,0},{2,3},{3,2},{4,5},{5,4},{6,7},{7,6},{8,9},{9,8},{10,11... | collective-permute-start | bytes 147464 | tf_op jit(solution)/shard_map/ppermute | solution.py:466
  86.5 21.5 %collective-permute-start.10 = (bf16[48,512]{1,0:T(8,128)(2,1)S(1)}, bf16[48,512]{1,0:T(8,128)(2,1)S(1)}, u32[]{:S(2)}, u32[]{:S(2)}) collective-permute-start(bf16[48,512]{1,0:T(8,128)(2,1)S(1)} %get-tuple-element.92), channel_id=1, source_target_pairs={{0,31},{1,2},{2,1},{3,4},{4,3},{5,6},{6,5},{7,8},{8,7},{9,10},{10,... | collective-permute-start | bytes 147464 | tf_op jit(solution)/shard_map/ppermute | solution.py:465
  101.3 11.1 %collective-permute-start.23 = (bf16[64,1024]{1,0:T(8,128)(2,1)S(1)}, bf16[64,1024]{1,0:T(8,128)(2,1)S(1)}, u32[]{:S(2)}, u32[]{:S(2)}) collective-permute-start(bf16[64,1024]{1,0:T(8,128)(2,1)S(1)} %get-tuple-element.110), channel_id=1, source_target_pairs={{0,2},{1,3},{2,0},{3,1},{32,34},{33,35},{34,32},{35,33},{64,66},{6... | collective-permute-start | bytes 393224 | tf_op jit(solution)/shard_map/ppermute | solution.py:455
  101.3 14.8 %collective-permute-start.24 = (bf16[64,1024]{1,0:T(8,128)(2,1)S(1)}, bf16[64,1024]{1,0:T(8,128)(2,1)S(1)}, u32[]{:S(2)}, u32[]{:S(2)}) collective-permute-start(bf16[64,1024]{1,0:T(8,128)(2,1)S(1)} %get-tuple-element.111), channel_id=1, source_target_pairs={{0,3},{1,0},{2,1},{3,2},{32,35},{33,32},{34,33},{35,34},{64,67},{6... | collective-permute-start | bytes 393224 | tf_op jit(solution)/shard_map/ppermute | solution.py:455
  106.4 18.1 %copy-start.5 = (bf16[1,16,48,512]{3,2,1,0:T(8,128)(2,1)S(1)}, bf16[1,16,48,512]{3,2,1,0:T(8,128)(2,1)}, u32[]{:S(2)}) copy-start(bf16[1,16,48,512]{3,2,1,0:T(8,128)(2,1)} %param.10) | copy-start | bytes 2359300
  106.4 11.0 %collective-permute-start.16 = (bf16[64,1024]{1,0:T(8,128)(2,1)S(1)}, bf16[64,1024]{1,0:T(8,128)(2,1)S(1)}, u32[]{:S(2)}, u32[]{:S(2)}) collective-permute-start(bf16[64,1024]{1,0:T(8,128)(2,1)S(1)} %get-tuple-element.100), channel_id=1, source_target_pairs={{0,8},{8,16},{16,24},{24,0},{32,40},{40,48},{48,56},{56,32},{64,72... | collective-permute-start | bytes 393224 | tf_op jit(solution)/shard_map/ppermute | solution.py:455
  108.0 9.5 %collective-permute-start.17 = (bf16[64,1024]{1,0:T(8,128)(2,1)S(1)}, bf16[64,1024]{1,0:T(8,128)(2,1)S(1)}, u32[]{:S(2)}, u32[]{:S(2)}) collective-permute-start(bf16[64,1024]{1,0:T(8,128)(2,1)S(1)} %get-tuple-element.101), channel_id=1, source_target_pairs={{0,16},{8,24},{16,0},{24,8},{32,48},{40,56},{48,32},{56,40},{64,80... | collective-permute-start | bytes 393224 | tf_op jit(solution)/shard_map/ppermute | solution.py:455
  109.9 7.6 %collective-permute-start.18 = (bf16[64,1024]{1,0:T(8,128)(2,1)S(1)}, bf16[64,1024]{1,0:T(8,128)(2,1)S(1)}, u32[]{:S(2)}, u32[]{:S(2)}) collective-permute-start(bf16[64,1024]{1,0:T(8,128)(2,1)S(1)} %get-tuple-element.102), channel_id=1, source_target_pairs={{0,24},{8,0},{16,8},{24,16},{32,56},{40,32},{48,40},{56,48},{64,88... | collective-permute-start | bytes 393224 | tf_op jit(solution)/shard_map/ppermute | solution.py:455
  112.4 11.2 %collective-permute-start.11 = (bf16[176,512]{1,0:T(8,128)(2,1)S(1)}, bf16[176,512]{1,0:T(8,128)(2,1)S(1)}, u32[]{:S(2)}, u32[]{:S(2)}) collective-permute-start(bf16[176,512]{1,0:T(8,128)(2,1)S(1)} %get-tuple-element.93), channel_id=1, source_target_pairs={{0,32},{32,64},{64,96},{1,33},{33,65},{65,97},{2,34},{34,66},{66,9... | collective-permute-start | bytes 540680 | tf_op jit(solution)/shard_map/ppermute | solution.py:470
  116.1 8.3 %collective-permute-start.12 = (bf16[176,512]{1,0:T(8,128)(2,1)S(1)}, bf16[176,512]{1,0:T(8,128)(2,1)S(1)}, u32[]{:S(2)}, u32[]{:S(2)}) collective-permute-start(bf16[176,512]{1,0:T(8,128)(2,1)S(1)} %get-tuple-element.94), channel_id=1, source_target_pairs={{32,0},{64,32},{96,64},{33,1},{65,33},{97,65},{34,2},{66,34},{98,6... | collective-permute-start | bytes 540680 | tf_op jit(solution)/shard_map/ppermute | solution.py:471
  117.7 13.1 %collective-permute-start.25 = (bf16[64,1024]{1,0:T(8,128)(2,1)S(1)}, bf16[64,1024]{1,0:T(8,128)(2,1)S(1)}, u32[]{:S(2)}, u32[]{:S(2)}) collective-permute-start(bf16[64,1024]{1,0:T(8,128)(2,1)S(1)} %get-tuple-element.114), channel_id=1, source_target_pairs={{0,4},{4,0},{32,36},{36,32},{64,68},{68,64},{96,100},{100,96},{8,1... | collective-permute-start | bytes 393224 | tf_op jit(solution)/shard_map/ppermute | solution.py:455
  130.9 6.1 %collective-permute-start.26 = (bf16[16,1024]{1,0:T(8,128)(2,1)S(1)}, bf16[16,1024]{1,0:T(8,128)(2,1)S(1)}, u32[]{:S(2)}, u32[]{:S(2)}) collective-permute-start(bf16[16,1024]{1,0:T(8,128)(2,1)S(1)} %get-tuple-element.117), channel_id=1, source_target_pairs={{0,32},{32,64},{64,96},{96,0},{4,36},{36,68},{68,100},{100,4},{8,4... | collective-permute-start | bytes 98312 | tf_op jit(solution)/shard_map/ppermute | solution.py:455
  132.8 4.8 %collective-permute-start.27 = (bf16[16,1024]{1,0:T(8,128)(2,1)S(1)}, bf16[16,1024]{1,0:T(8,128)(2,1)S(1)}, u32[]{:S(2)}, u32[]{:S(2)}) collective-permute-start(bf16[16,1024]{1,0:T(8,128)(2,1)S(1)} %get-tuple-element.118), channel_id=1, source_target_pairs={{0,64},{32,96},{64,0},{96,32},{4,68},{36,100},{68,4},{100,36},{8,7... | collective-permute-start | bytes 98312 | tf_op jit(solution)/shard_map/ppermute | solution.py:455
  134.2 4.4 %collective-permute-start.28 = (bf16[16,1024]{1,0:T(8,128)(2,1)S(1)}, bf16[16,1024]{1,0:T(8,128)(2,1)S(1)}, u32[]{:S(2)}, u32[]{:S(2)}) collective-permute-start(bf16[16,1024]{1,0:T(8,128)(2,1)S(1)} %get-tuple-element.119), channel_id=1, source_target_pairs={{0,96},{32,0},{64,32},{96,64},{4,100},{36,4},{68,36},{100,68},{8,1... | collective-permute-start | bytes 98312 | tf_op jit(solution)/shard_map/ppermute | solution.py:455
  (8 other events, 70.6 us)

commit v4 on v3

--- a/solution.py
+++ b/solution.py
@@ -101,7 +101,7 @@
 
 
 def import_kernel(
-    source_ref, state_ref, weight_ref, fields_ref, one_ref, two_ref, above_ref, below_ref, after_ref,
+    source_ref, state_ref, weight_ref, fields_ref, one_ref, two_ref, above_ref, below_ref,
     forced_ref, send_one_ref, send_two_ref, tiles, cells, left, right, flat,
 ):
     lat, lon = lax.axis_index("lat"), lax.axis_index("lon")
@@ -237,10 +237,7 @@
     lax.fori_loop(0, len(blocks), one_block, 0)
 
 
-def d_active_kernel(
-    upstream_ref, mask_ref, w_out_ref, after_ref, update_ref, keep_ref, by_x_ref, by_y_ref, token_ref
-):
-    token_ref[...] = jnp.zeros((8, LANES), F32)
+def masked_kernel(upstream_ref, mask_ref, after_ref, update_ref, keep_ref):
     mask = jnp.where(lax.axis_index("group") == 1, mask_ref[...].astype(F32), 1.0).T
     for row in range(ROWS):
         rows = slice(row * COLS, (row + 1) * COLS)
@@ -248,16 +245,6 @@
     for at in range(BLOCKS):
         lanes = slice(at * LANES, (at + 1) * LANES)
         update_ref[:, lanes] = (keep_ref[...] * upstream_ref[:, lanes].astype(F32)).astype(BF)
-    update = update_ref[...]
-    for step in range(4):
-        mine = slice(step * PART, (step + 1) * PART)
-        chunk = lax.rem(along("x") + step, 4)
-        by_x_ref[:, mine] = dot(update, w_out_ref[0:16, chunk].reshape(PART, CH), 1, 1)
-        chunk = lax.rem(along("y") + step, 4)
-        for part in range(2):
-            rows = w_out_ref[pl.ds(16 + 8 * part + 2 * chunk, 2)].reshape(LANES, CH)
-            spot = slice(step * PART + part * LANES, step * PART + (part + 1) * LANES)
-            by_y_ref[:, spot] = dot(update, rows, 1, 1)
 
 
 def conv_norm_kernel(
@@ -290,7 +277,7 @@
             normed_ref[row, :, lanes] = (hat * gain_ref[:, lanes]).astype(BF)
         return carry
 
-    lax.fori_loop(0, ROWS, one_row, 0)
+    lax.fori_loop(0, ROWS, one_row, 0, unroll=4)
 
 
 def dot(a, b, left, right):
@@ -307,30 +294,40 @@
 
 
 def mlp_kernel(
-    normed_ref, update_ref, d_active_ref, w_in_ref, w_out_ref,
+    normed_ref, update_ref, w_in_ref, w_out_ref,
     grad0_ref, grad1_ref, grad2_ref, grad3_ref, act_ref, pre_ref, w_in_out_ref, w_out_out_ref,
     *, by_x,
 ):
-    normed = normed_ref[...]
-    update = update_ref[...]
-    for step, grad_ref in enumerate((grad0_ref, grad1_ref, grad2_ref, grad3_ref)):
+    def units(step):
+        return slice(step * PART, (step + 1) * PART)
+
+    for step in range(4):
         chunk = lax.rem(along("x" if by_x else "y") + step, 4)
-        first = w_in_ref[0, :, chunk].reshape(PART, CH)
-        second = w_out_ref[0, :, chunk].reshape(PART, CH)
-        mine = slice(step * PART, (step + 1) * PART)
-        w_in_out_ref[mine, :] = first
-        w_out_out_ref[mine, :] = second
-        value = dot(normed, first, 1, 1)
+        w_in_out_ref[units(step), :] = w_in_ref[0, :, chunk].reshape(PART, CH)
+        w_out_out_ref[units(step), :] = w_out_ref[0, :, chunk].reshape(PART, CH)
+
+    def expand(step, rows):
+        value = dot(normed_ref[rows, :], w_in_out_ref[units(step), :], 1, 1)
+        return value, dot(update_ref[rows, :], w_out_out_ref[units(step), :], 1, 1)
+
+    def bend(step, rows, value, back):
         square = value * value
         bent = jnp.tanh(value * (GELU_A + GELU_B * square))
         cdf = 0.5 + 0.5 * bent
-        act = (value * cdf).astype(BF)
+        act_ref[rows, units(step)] = (value * cdf).astype(BF)
         slope = cdf + (0.5 * value) * (1.0 - bent * bent) * (GELU_A + 3.0 * GELU_B * square)
-        pre = (d_active_ref[:, mine] * slope).astype(BF)
-        act_ref[:, mine] = act
-        pre_ref[:, mine] = pre
-        grad_ref[:, :CH] = dot(pre, normed, 0, 0).astype(BF)
-        grad_ref[:, CH:] = dot(act, update, 0, 0).astype(BF)
+        pre_ref[rows, units(step)] = (back * slope).astype(BF)
+
+    grads = (grad0_ref, grad1_ref, grad2_ref, grad3_ref)
+    pieces = [(step, slice(at, at + 256)) for step in range(4) for at in range(0, CELLS, 256)]
+    held = expand(*pieces[0])
+    for at, (step, rows) in enumerate(pieces):
+        following = expand(*pieces[at + 1]) if at + 1 < len(pieces) else None
+        bend(step, rows, *held)
+        held = following
+        if rows.stop == CELLS:
+            grads[step][:, :CH] = dot(pre_ref[:, units(step)], normed_ref[...], 0, 0).astype(BF)
+            grads[step][:, CH:] = dot(act_ref[:, units(step)], update_ref[...], 0, 0).astype(BF)
 
 
 def advance_kernel(
@@ -360,7 +357,7 @@
         d_hidden_ref[rows, :] = back.astype(BF)
         return carry
 
-    lax.fori_loop(0, ROWS, one_row, 0)
+    lax.fori_loop(0, ROWS, one_row, 0, unroll=4)
     for row in range(ROWS):
         start = row * COLS
         left[3 * row : 3 * row + 3, :] = wide[start : start + 3, :]
@@ -497,22 +494,20 @@
     )
     above, below = swap_lat(up, down)
     anywhere = pl.BlockSpec(memory_space=pl.ANY)
-    update, keep, by_x, by_y, token = run(
-        d_active_kernel, "d_active",
-        [shape((CELLS, CH), BF), shape((CELLS, LANES), F32)] + [shape((CELLS, HALF), F32)] * 2
-        + [shape((8, LANES), F32)],
-        upstream.reshape(CELLS, CH), land_mask, w_out[0].reshape(32, 4, 16, CH), up, views={3: anywhere}, room=12,
-    )
     forced, f_one, f_two = run(
         import_kernel, "import", [shape((CELLS, LANES), BF)] + [shape((48, LANES), BF)] * 2,
-        sources, state, weights, fields, one, two, above, below, token, smem=1, views={8: anywhere},
+        sources, state, weights, fields, one, two, above, below, smem=1,
         scratch=[vm((9, 48, LANES), F32), vm((CELLS, LANES), F32)] + [vm((48, LANES), F32)] * 2
         + [vm((8, CELLS), F32)],
     )
     f_one, f_two = swap_lon(f_one, f_two)
+    update, keep = run(
+        masked_kernel, "masked", [shape((CELLS, CH), BF), shape((CELLS, LANES), F32)],
+        upstream.reshape(CELLS, CH), land_mask, forced, views={2: anywhere},
+    )
     (hidden,) = run(
         functools.partial(conv_wide_kernel, blocks=(0,)), "conv_one", [shape((1, ROWS, COLS, LANES), F32)],
-        state, one, two, above, below, taps, forced, views={6: anywhere},
+        state, one, two, above, below, taps, keep, views={6: anywhere},
         scratch=[vm((1, PAD_ROWS, PAD_COLS, LANES), F32), vm((1, 49, 8, LANES), F32)], room=6,
     )
     f_up, f_down = run(
@@ -536,7 +531,7 @@
     hat = hat.reshape(CELLS, CH)
     inv = inv.reshape(CELLS, LANES)
 
-    def half(by_x, d_active):
+    def half(by_x):
         if by_x:
             dims, block, at = (2, 16, 4, 16, CH), (1, 16, 4, 16, CH), lambda i: (0, 0, 0, 0, 0)
         else:
@@ -545,18 +540,18 @@
         outs = run(
             functools.partial(mlp_kernel, by_x=by_x), "mlp_x" if by_x else "mlp_y",
             [shape((PART, 2 * CH), BF)] * 4 + [shape((CELLS, HALF), BF)] * 2 + [shape((HALF, CH), BF)] * 2,
-            normed, update, d_active, w_in[0].reshape(dims), w_out[0].reshape(dims), views={3: view, 4: view}, room=12,
+            normed, update, w_in[0].reshape(dims), w_out[0].reshape(dims), views={2: view, 3: view}, room=12,
         )
         return outs[:4], outs[4:]
 
-    grads_b, kept_b = half(False, by_y)
+    grads_b, kept_b = half(False)
     grads_b = around(grads_b, "y")
-    grads_a, kept_a = half(True, by_x)
-    a_one, a_two = send(grads_a[1], "x", 1), send(grads_a[2], "x", 2)
-    d_hidden, d_one, d_two, a_three = run(
+    grads_a, kept_a = half(True)
+    a_one, a_three = send(grads_a[1], "x", 1), send(grads_a[3], "x", 3)
+    d_hidden, d_one, d_two, a_two = run(
         finish_kernel, "finish",
         [shape((CELLS, CH), BF)] + [shape((48, CH), BF)] * 2 + [shape((PART, 2 * CH), BF)],
-        kept_a[1], kept_b[1], kept_a[2], kept_b[2], norm_gain, hat, inv, grads_a[3], same={7: 3},
+        kept_a[1], kept_b[1], kept_a[2], kept_b[2], norm_gain, hat, inv, grads_a[2], same={7: 3},
         scratch=[vm((CELLS, CH), F32)] + [vm((48, CH), F32)] * 2, room=12,
     )
     advanced, token = run(
@@ -569,7 +564,7 @@
         *grads_b, token, views={4: anywhere}, scratch=[vm((2, 2, 4, 16, 2 * CH), BF)],
     )
     d_one, d_two = swap_lon(d_one, d_two)
-    grads_a = [grads_a[0], a_one, a_two, send(a_three, "x", 3)]
+    grads_a = [grads_a[0], a_one, send(a_two, "x", 2), a_three]
     grads_b = around(grads_b, "x")
     grads_a = run(
         functools.partial(sum_four_kernel, by_x=True), "sum_x", [shape((64, 2 * CH), BF)] * 4,

time: 140 us -> 129 us (0.921)
  starting transfers between devices: 88.3 us -> 75.8 us
  waiting for transfers between devices: 11.2 us -> 18.7 us
  Pallas kernels: 36.4 us -> 31.4 us
    ppermute x3, starting transfers between devices: 29.6 us -> 20.4 us  [swap_lon(): two = lax.ppermute(two, 'lon', other)]
    pallas_call x20, Pallas kernels: 36.4 us -> 31.4 us  [run(): pl.pallas_call(kernel, out_shape=outs, grid=(1,), in_specs=in_specs, out_...]
    ppermute x16, waiting for transfers between devices: 1.63 us -> 5.72 us  [send(): return lax.ppermute(piece, ('lat', 'lon'), pairs)]
    ppermute x3, waiting for transfers between devices: 4.67 us -> 6.84 us  [swap_lat(): below = lax.ppermute(up, 'lat', [(i + 1, i) for i in range(3)])]
    ppermute x16, starting transfers between devices: 41.1 us -> 39.4 us  [send(): return lax.ppermute(piece, ('lat', 'lon'), pairs)]
    ppermute x3, waiting for transfers between devices: 0.01 us -> 1.6 us  [swap_lat(): above = lax.ppermute(down, 'lat', [(i, i + 1) for i in range(3)])]
  transfers between devices with their start and end apart: 29 -> 29, of which waited for: 8 -> 11; matrix products, arithmetic and copies ran while one was open for 0% -> 0% of each run, Pallas kernels for 18% -> 18%
where the time goes in v4:
time: 129 us; the launch traced here: 128 us
  starting transfers between devices  75.8 us (59%)
  Pallas kernels  31.4 us (24%)
  waiting for transfers between devices  18.7 us (14%)
    ppermute x16, starting transfers between devices, send(): return lax.ppermute(piece, ('lat', 'lon'), pairs)  39.4 us
    pallas_call x20, Pallas kernels, run(): pl.pallas_call(kernel, out_shape=outs, grid=(1,), in_specs=in_specs, out_...  31.4 us
    ppermute x3, starting transfers between devices, swap_lon(): two = lax.ppermute(two, 'lon', other)  20.4 us
    ppermute x3, starting transfers between devices, swap_lat(): above = lax.ppermute(down, 'lat', [(i, i + 1) for i in range(3)])  10.7 us
    ppermute x3, waiting for transfers between devices, swap_lat(): below = lax.ppermute(up, 'lat', [(i + 1, i) for i in range(3)])  6.84 us
    ppermute x16, waiting for transfers between devices, send(): return lax.ppermute(piece, ('lat', 'lon'), pairs)  5.72 us
    ppermute x3, starting transfers between devices, swap_lat(): below = lax.ppermute(up, 'lat', [(i + 1, i) for i in range(3)])  4.19 us
    ppermute x3, waiting for transfers between devices, swap_lon(): two = lax.ppermute(two, 'lon', other)  3.42 us
  transfers between devices with their start and end apart: 29, of which 11 were waited for; matrix products, arithmetic and copies ran while one was open for 0% of the time, Pallas kernels for 18%

profile of v4, /device:TPU:6, one launch (start us, length us, event | category | flops | bytes accessed | tf_op | source)
XLA Modules:
  0.0 128.0 jit_solution(4036367893365805004)
XLA Ops:
  4.1 7.8 %collective-permute-start.2 = (bf16[48,512]{1,0:T(8,128)(2,1)S(1)}, bf16[48,512]{1,0:T(8,128)(2,1)S(1)}, u32[]{:S(2)}, u32[]{:S(2)}) collective-permute-start(bf16[48,512]{1,0:T(8,128)(2,1)S(1)} %get-tuple-element.61), channel_id=1, source_target_pairs={{0,31},{1,2},{2,1},{3,4},{4,3},{5,6},{6,5},{7,8},{8,7},{9,10},{10,... | collective-permute-start | bytes 147464 | tf_op jit(solution)/shard_map/ppermute | solution.py:462
  11.9 2.4 %collective-permute-done.2.two_ref = bf16[48,512]{1,0:T(8,128)(2,1)S(1)} collective-permute-done((bf16[48,512]{1,0:T(8,128)(2,1)S(1)}, bf16[48,512]{1,0:T(8,128)(2,1)S(1)}, u32[]{:S(2)}, u32[]{:S(2)}) %collective-permute-start.2) | collective-permute-done | bytes 49184 | tf_op jit(solution)/shard_map/ppermute | solution.py:462
  14.4 3.7 %collective-permute-start.3 = (bf16[224,384]{1,0:T(8,128)(2,1)S(1)}, bf16[224,384]{1,0:T(8,128)(2,1)S(1)}, u32[]{:S(2)}, u32[]{:S(2)}) collective-permute-start(bf16[224,384]{1,0:T(8,128)(2,1)S(1)} %get-tuple-element.62), channel_id=1, source_target_pairs={{0,32},{32,64},{64,96},{1,33},{33,65},{65,97},{2,34},{34,66},{66,9... | collective-permute-start | bytes 516104 | tf_op jit(solution)/shard_map/ppermute | solution.py:467
  19.4 1.6 %collective-permute-done.3.above_ref = bf16[224,384]{1,0:T(8,128)(2,1)S(1)} collective-permute-done((bf16[224,384]{1,0:T(8,128)(2,1)S(1)}, bf16[224,384]{1,0:T(8,128)(2,1)S(1)}, u32[]{:S(2)}, u32[]{:S(2)}) %collective-permute-start.3) | collective-permute-done | bytes 172064 | tf_op jit(solution)/shard_map/ppermute | solution.py:467
  21.0 4.4 %collective-permute-done.4.below_ref = bf16[224,384]{1,0:T(8,128)(2,1)S(1)} collective-permute-done((bf16[224,384]{1,0:T(8,128)(2,1)S(1)}, bf16[224,384]{1,0:T(8,128)(2,1)S(1)}, u32[]{:S(2)}, u32[]{:S(2)}) %collective-permute-start.4) | collective-permute-done | bytes 172064 | tf_op jit(solution)/shard_map/ppermute | solution.py:468
  26.4 7.1 %collective-permute-start.6 = (bf16[48,128]{1,0:T(8,128)(2,1)S(1)}, bf16[48,128]{1,0:T(8,128)(2,1)S(1)}, u32[]{:S(2)}, u32[]{:S(2)}) collective-permute-start(bf16[48,128]{1,0:T(8,128)(2,1)S(1)} %get-tuple-element.66), channel_id=1, source_target_pairs={{0,31},{1,2},{2,1},{3,4},{4,3},{5,6},{6,5},{7,8},{8,7},{9,10},{10,... | collective-permute-start | bytes 36872 | tf_op jit(solution)/shard_map/ppermute | solution.py:462
  36.2 3.9 %collective-permute-start.7 = (bf16[176,128]{1,0:T(8,128)(2,1)S(1)}, bf16[176,128]{1,0:T(8,128)(2,1)S(1)}, u32[]{:S(2)}, u32[]{:S(2)}) collective-permute-start(bf16[176,128]{1,0:T(8,128)(2,1)S(1)} %get-tuple-element.68), channel_id=1, source_target_pairs={{0,32},{32,64},{64,96},{1,33},{33,65},{65,97},{2,34},{34,66},{66,9... | collective-permute-start | bytes 135176 | tf_op jit(solution)/shard_map/ppermute | solution.py:467
  40.2 1.6 %collective-permute-start.8 = (bf16[176,128]{1,0:T(8,128)(2,1)S(1)}, bf16[176,128]{1,0:T(8,128)(2,1)S(1)}, u32[]{:S(2)}, u32[]{:S(2)}) collective-permute-start(bf16[176,128]{1,0:T(8,128)(2,1)S(1)} %get-tuple-element.69.after_ref), channel_id=1, source_target_pairs={{32,0},{64,32},{96,64},{33,1},{65,33},{97,65},{34,2},{66,34},{98,6... | collective-permute-start | bytes 135176 | tf_op jit(solution)/shard_map/ppermute | solution.py:468
  41.8 2.7 %conv_two.1.more_ref = f32[2,16,48,128]{3,2,1,0:T(8,128)S(1)} custom-call(bf16[16,48,512]{2,1,0:T(8,128)(2,1)S(1)} %bitcast.25, bf16[48,512]{1,0:T(8,128)(2,1)S(1)} %collective-permute-done.1.one_ref, bf16[48,512]{1,0:T(8,128)(2,1)S(1)} %collective-permute-done.2.two_ref, bf16[224,384]{1,0:T(8,128)(2,1)S(1)} %collective-permute-done.3.above_ref, ...), custom_call_target="tpu_custom_call" | custom-call | bytes 1024 | tf_op jit(solution)/shard_map/conv_two/pallas_call | solution.py:39
  44.5 1.8 %collective-permute-done.8.below_ref = bf16[176,128]{1,0:T(8,128)(2,1)S(1)} collective-permute-done((bf16[176,128]{1,0:T(8,128)(2,1)S(1)}, bf16[176,128]{1,0:T(8,128)(2,1)S(1)}, u32[]{:S(2)}, u32[]{:S(2)}) %collective-permute-start.8) | collective-permute-done | bytes 45088 | tf_op jit(solution)/shard_map/ppermute | solution.py:468
  46.2 2.3 %conv_norm.1 = (bf16[16,48,512]{2,1,0:T(8,128)(2,1)S(1)}, f32[16,48,512]{2,1,0:T(8,128)S(1)}, f32[16,48,128]{2,1,0:T(8,128)S(1)}) custom-call(bf16[768,128]{1,0:T(8,128)(2,1)S(1)} %get-tuple-element.64.after_ref.cells_ref.forced_ref, bf16[48,128]{1,0:T(8,128)(2,1)S(1)} %collective-permute-done.5.one_ref, bf16[48,128]{1,0:T(8,128)(2,1)S(1)} %collective-permute-done.6.two_ref, ...), custom_call_target="tpu_custom_call" | custom-call | bytes 1024 | tf_op jit(solution)/shard_map/conv_norm/pallas_call | solution.py:39
  48.5 4.6 %mlp_y.1 = (bf16[256,1024]{1,0:T(8,128)(2,1)S(1)}, bf16[256,1024]{1,0:T(8,128)(2,1)S(1)}, bf16[256,1024]{1,0:T(8,128)(2,1)S(1)}, bf16[256,1024]{1,0:T(8,128)(2,1...) custom-call(bf16[768,512]{1,0:T(8,128)(2,1)S(1)} %bitcast.33, ...), custom_call_target="tpu_custom_call" | custom-call | bytes 1024 | tf_op jit(solution)/shard_map/mlp_y/pallas_call | solution.py:39
  53.1 1.7 %collective-permute-start.19 = (bf16[256,1024]{1,0:T(8,128)(2,1)S(1)}, bf16[256,1024]{1,0:T(8,128)(2,1)S(1)}, u32[]{:S(2)}, u32[]{:S(2)}) collective-permute-start(bf16[256,1024]{1,0:T(8,128)(2,1)S(1)} %get-tuple-element.98), channel_id=1, source_target_pairs={{0,8},{8,16},{16,24},{24,0},{32,40},{40,48},{48,56},{56,32},{64,72... | collective-permute-start | bytes 1572872 | tf_op jit(solution)/shard_map/ppermute | solution.py:452
  54.8 2.9 %collective-permute-start.20 = (bf16[256,1024]{1,0:T(8,128)(2,1)S(1)}, bf16[256,1024]{1,0:T(8,128)(2,1)S(1)}, u32[]{:S(2)}, u32[]{:S(2)}) collective-permute-start(bf16[256,1024]{1,0:T(8,128)(2,1)S(1)} %get-tuple-element.99), channel_id=1, source_target_pairs={{0,16},{8,24},{16,0},{24,8},{32,48},{40,56},{48,32},{56,40},{64,80... | collective-permute-start | bytes 1572872 | tf_op jit(solution)/shard_map/ppermute | solution.py:452
  59.1 4.5 %mlp_x.1 = (bf16[256,1024]{1,0:T(8,128)(2,1)S(1)}, bf16[256,1024]{1,0:T(8,128)(2,1)S(1)}, bf16[256,1024]{1,0:T(8,128)(2,1)S(1)}, bf16[256,1024]{1,0:T(8,128)(2,1...) custom-call(bf16[768,512]{1,0:T(8,128)(2,1)S(1)} %bitcast.34, ...), custom_call_target="tpu_custom_call" | custom-call | bytes 1024 | tf_op jit(solution)/shard_map/mlp_x/pallas_call | solution.py:39
  63.6 3.6 %finish.1 = (bf16[768,512]{1,0:T(8,128)(2,1)S(1)}, bf16[48,512]{1,0:T(8,128)(2,1)S(1)}, bf16[48,512]{1,0:T(8,128)(2,1)S(1)}, bf16[256,1024]{1,0:T(8,128)(2,1)S(1)}) custom-call(bf16[768,1024]{1,0:T(8,128)(2,1)S(1)} %get-tuple-element.76.pre_a_ref, bf16[768,1024]{1,0:T(8,128)(2,1)S(1)} %get-tuple-element.77.pre_b_ref, ...), custom_call_target="tpu_custom_call", output_to_operand_aliasing={{3}: (7, {})} | custom-call | bytes 1024 | tf_op jit(solution)/shard_map/finish/pallas_call | solution.py:39
  67.3 3.4 %collective-permute-start.13 = (bf16[256,1024]{1,0:T(8,128)(2,1)S(1)}, bf16[256,1024]{1,0:T(8,128)(2,1)S(1)}, u32[]{:S(2)}, u32[]{:S(2)}) collective-permute-start(bf16[256,1024]{1,0:T(8,128)(2,1)S(1)} %get-tuple-element.90), channel_id=1, source_target_pairs={{0,1},{1,2},{2,3},{3,0},{32,33},{33,34},{34,35},{35,32},{64,65},{6... | collective-permute-start | bytes 1572872 | tf_op jit(solution)/shard_map/ppermute | solution.py:452
  71.4 2.7 %advance.1 = (bf16[768,512]{1,0:T(8,128)(2,1)}, f32[8,128]{1,0:T(8,128)S(1)}) custom-call(bf16[768,1024]{1,0:T(8,128)(2,1)S(1)} %get-tuple-element.72.act_a_ref, bf16[768,1024]{1,0:T(8,128)(2,1)S(1)} %get-tuple-element.73.act_b_ref, bf16[1024,512]{1,0:T(8,128)(2,1)S(1)} %get-tuple-element.74.w_out_a_ref, ...), custom_call_target="tpu_custom_call" | custom-call | bytes 1024 | tf_op jit(solution)/shard_map/advance/pallas_call | solution.py:39
  74.1 1.9 %collective-permute-done.20.c = bf16[256,1024]{1,0:T(8,128)(2,1)S(1)} collective-permute-done((bf16[256,1024]{1,0:T(8,128)(2,1)S(1)}, bf16[256,1024]{1,0:T(8,128)(2,1)S(1)}, u32[]{:S(2)}, u32[]{:S(2)}) %collective-permute-start.20) | collective-permute-done | bytes 524320 | tf_op jit(solution)/shard_map/ppermute | solution.py:452
  76.6 6.9 %collective-permute-start.22 = (bf16[64,1024]{1,0:T(8,128)(2,1)S(1)}, bf16[64,1024]{1,0:T(8,128)(2,1)S(1)}, u32[]{:S(2)}, u32[]{:S(2)}) collective-permute-start(bf16[64,1024]{1,0:T(8,128)(2,1)S(1)} %get-tuple-element.103), channel_id=1, source_target_pairs={{0,1},{1,2},{2,3},{3,0},{32,33},{33,34},{34,35},{35,32},{64,65},{6... | collective-permute-start | bytes 393224 | tf_op jit(solution)/shard_map/ppermute | solution.py:452
  83.4 5.6 %collective-permute-start.10 = (bf16[48,512]{1,0:T(8,128)(2,1)S(1)}, bf16[48,512]{1,0:T(8,128)(2,1)S(1)}, u32[]{:S(2)}, u32[]{:S(2)}) collective-permute-start(bf16[48,512]{1,0:T(8,128)(2,1)S(1)} %get-tuple-element.86), channel_id=1, source_target_pairs={{0,31},{1,2},{2,1},{3,4},{4,3},{5,6},{6,5},{7,8},{8,7},{9,10},{10,... | collective-permute-start | bytes 147464 | tf_op jit(solution)/shard_map/ppermute | solution.py:462
  89.0 1.6 %collective-permute-done.13.b = bf16[256,1024]{1,0:T(8,128)(2,1)S(1)} collective-permute-done((bf16[256,1024]{1,0:T(8,128)(2,1)S(1)}, bf16[256,1024]{1,0:T(8,128)(2,1)S(1)}, u32[]{:S(2)}, u32[]{:S(2)}) %collective-permute-start.13) | collective-permute-done | bytes 524320 | tf_op jit(solution)/shard_map/ppermute | solution.py:452
  91.5 3.6 %collective-permute-start.24 = (bf16[64,1024]{1,0:T(8,128)(2,1)S(1)}, bf16[64,1024]{1,0:T(8,128)(2,1)S(1)}, u32[]{:S(2)}, u32[]{:S(2)}) collective-permute-start(bf16[64,1024]{1,0:T(8,128)(2,1)S(1)} %get-tuple-element.105), channel_id=1, source_target_pairs={{0,3},{1,0},{2,1},{3,2},{32,35},{33,32},{34,33},{35,34},{64,67},{6... | collective-permute-start | bytes 393224 | tf_op jit(solution)/shard_map/ppermute | solution.py:452
  95.6 1.6 %collective-permute-start.16 = (bf16[64,1024]{1,0:T(8,128)(2,1)S(1)}, bf16[64,1024]{1,0:T(8,128)(2,1)S(1)}, u32[]{:S(2)}, u32[]{:S(2)}) collective-permute-start(bf16[64,1024]{1,0:T(8,128)(2,1)S(1)} %get-tuple-element.94), channel_id=1, source_target_pairs={{0,8},{8,16},{16,24},{24,0},{32,40},{40,48},{48,56},{56,32},{64,72... | collective-permute-start | bytes 393224 | tf_op jit(solution)/shard_map/ppermute | solution.py:452
  97.1 2.5 %collective-permute-start.17 = (bf16[64,1024]{1,0:T(8,128)(2,1)S(1)}, bf16[64,1024]{1,0:T(8,128)(2,1)S(1)}, u32[]{:S(2)}, u32[]{:S(2)}) collective-permute-start(bf16[64,1024]{1,0:T(8,128)(2,1)S(1)} %get-tuple-element.95), channel_id=1, source_target_pairs={{0,16},{8,24},{16,0},{24,8},{32,48},{40,56},{48,32},{56,40},{64,80... | collective-permute-start | bytes 393224 | tf_op jit(solution)/shard_map/ppermute | solution.py:452
  99.6 2.5 %collective-permute-start.18 = (bf16[64,1024]{1,0:T(8,128)(2,1)S(1)}, bf16[64,1024]{1,0:T(8,128)(2,1)S(1)}, u32[]{:S(2)}, u32[]{:S(2)}) collective-permute-start(bf16[64,1024]{1,0:T(8,128)(2,1)S(1)} %get-tuple-element.96), channel_id=1, source_target_pairs={{0,24},{8,0},{16,8},{24,16},{32,56},{40,32},{48,40},{56,48},{64,88... | collective-permute-start | bytes 393224 | tf_op jit(solution)/shard_map/ppermute | solution.py:452
  102.2 3.0 %collective-permute-start.11 = (bf16[176,512]{1,0:T(8,128)(2,1)S(1)}, bf16[176,512]{1,0:T(8,128)(2,1)S(1)}, u32[]{:S(2)}, u32[]{:S(2)}) collective-permute-start(bf16[176,512]{1,0:T(8,128)(2,1)S(1)} %get-tuple-element.87), channel_id=1, source_target_pairs={{0,32},{32,64},{64,96},{1,33},{33,65},{65,97},{2,34},{34,66},{66,9... | collective-permute-start | bytes 540680 | tf_op jit(solution)/shard_map/ppermute | solution.py:467
  106.8 5.9 %collective-permute-start.25 = (bf16[64,1024]{1,0:T(8,128)(2,1)S(1)}, bf16[64,1024]{1,0:T(8,128)(2,1)S(1)}, u32[]{:S(2)}, u32[]{:S(2)}) collective-permute-start(bf16[64,1024]{1,0:T(8,128)(2,1)S(1)} %get-tuple-element.108), channel_id=1, source_target_pairs={{0,4},{4,0},{32,36},{36,32},{64,68},{68,64},{96,100},{100,96},{8,1... | collective-permute-start | bytes 393224 | tf_op jit(solution)/shard_map/ppermute | solution.py:452
  113.4 6.3 %conv_back.1 = (bf16[16,48,512]{2,1,0:T(8,128)(2,1)}, f32[8,128]{1,0:T(8,128)S(1)}) custom-call(bf16[768,512]{1,0:T(8,128)(2,1)S(1)} %get-tuple-element.83.after_ref.cells_ref.after.d_hidden_ref, bf16[48,512]{1,0:T(8,128)(2,1)S(1)} %collective-permute-done.9.one_ref.after_ref, bf16[48,512]{1,0:T(8,128)(2,1)S(1)} %collective-permute-done.10.two_ref, ...), custom_call_target="tpu_custom_call" | custom-call | bytes 1024 | tf_op jit(solution)/shard_map/conv_back/pallas_call | solution.py:39
  119.8 2.5 %collective-permute-start.26 = (bf16[16,1024]{1,0:T(8,128)(2,1)S(1)}, bf16[16,1024]{1,0:T(8,128)(2,1)S(1)}, u32[]{:S(2)}, u32[]{:S(2)}) collective-permute-start(bf16[16,1024]{1,0:T(8,128)(2,1)S(1)} %get-tuple-element.111), channel_id=1, source_target_pairs={{0,32},{32,64},{64,96},{96,0},{4,36},{36,68},{68,100},{100,4},{8,4... | collective-permute-start | bytes 98312 | tf_op jit(solution)/shard_map/ppermute | solution.py:452
  122.3 2.8 %collective-permute-start.28 = (bf16[16,1024]{1,0:T(8,128)(2,1)S(1)}, bf16[16,1024]{1,0:T(8,128)(2,1)S(1)}, u32[]{:S(2)}, u32[]{:S(2)}) collective-permute-start(bf16[16,1024]{1,0:T(8,128)(2,1)S(1)} %get-tuple-element.113), channel_id=1, source_target_pairs={{0,96},{32,0},{64,32},{96,64},{4,100},{36,4},{68,36},{100,68},{8,1... | collective-permute-start | bytes 98312 | tf_op jit(solution)/shard_map/ppermute | solution.py:452
  125.5 1.8 %collective-permute-done.27.refs_2_ = bf16[16,1024]{1,0:T(8,128)(2,1)S(1)} collective-permute-done((bf16[16,1024]{1,0:T(8,128)(2,1)S(1)}, bf16[16,1024]{1,0:T(8,128)(2,1)S(1)}, u32[]{:S(2)}, u32[]{:S(2)}) %collective-permute-start.27) | collective-permute-done | bytes 32800 | tf_op jit(solution)/shard_map/ppermute | solution.py:452
  (66 shorter events, 16.0 us)
Async XLA Ops:
  1.9 31.6 %copy-start.4 = (bf16[1,16,48,512]{3,2,1,0:T(8,128)(2,1)S(1)}, bf16[1,16,48,512]{3,2,1,0:T(8,128)(2,1)}, u32[]{:S(2)}) copy-start(bf16[1,16,48,512]{3,2,1,0:T(8,128)(2,1)} %param.10) | copy-start | bytes 2359300
  1.9 31.6 %copy-start.7 = (s32[16,48]{1,0:T(8,128)S(1)}, s32[16,48]{1,0:T(8,128)}, u32[]{:S(2)}) copy-start(s32[16,48]{1,0:T(8,128)} %mask_ref.1) | copy-start | bytes 9220
  1.9 1.3 collective-permute-start
  3.2 8.7 %collective-permute-start.1 = (bf16[48,512]{1,0:T(8,128)(2,1)S(1)}, bf16[48,512]{1,0:T(8,128)(2,1)S(1)}, u32[]{:S(2)}, u32[]{:S(2)}) collective-permute-start(bf16[48,512]{1,0:T(8,128)(2,1)S(1)} %get-tuple-element.60), channel_id=1, source_target_pairs={{0,1},{1,0},{2,3},{3,2},{4,5},{5,4},{6,7},{7,6},{8,9},{9,8},{10,11... | collective-permute-start | bytes 147464 | tf_op jit(solution)/shard_map/ppermute | solution.py:463
  4.1 29.7 %copy-start.5 = (f32[1,7,7,512]{3,0,2,1:T(1,128)S(1)}, f32[1,7,7,512]{3,0,2,1:T(1,128)}, u32[]{:S(2)}) copy-start(f32[1,7,7,512]{3,0,2,1:T(1,128)} %param.11) | copy-start | bytes 301060
  4.1 10.2 %collective-permute-start.2 = (bf16[48,512]{1,0:T(8,128)(2,1)S(1)}, bf16[48,512]{1,0:T(8,128)(2,1)S(1)}, u32[]{:S(2)}, u32[]{:S(2)}) collective-permute-start(bf16[48,512]{1,0:T(8,128)(2,1)S(1)} %get-tuple-element.61), channel_id=1, source_target_pairs={{0,31},{1,2},{2,1},{3,4},{4,3},{5,6},{6,5},{7,8},{8,7},{9,10},{10,... | collective-permute-start | bytes 147464 | tf_op jit(solution)/shard_map/ppermute | solution.py:462
  14.4 6.6 %collective-permute-start.3 = (bf16[224,384]{1,0:T(8,128)(2,1)S(1)}, bf16[224,384]{1,0:T(8,128)(2,1)S(1)}, u32[]{:S(2)}, u32[]{:S(2)}) collective-permute-start(bf16[224,384]{1,0:T(8,128)(2,1)S(1)} %get-tuple-element.62), channel_id=1, source_target_pairs={{0,32},{32,64},{64,96},{1,33},{33,65},{65,97},{2,34},{34,66},{66,9... | collective-permute-start | bytes 516104 | tf_op jit(solution)/shard_map/ppermute | solution.py:467
  18.1 7.3 %collective-permute-start.4 = (bf16[224,384]{1,0:T(8,128)(2,1)S(1)}, bf16[224,384]{1,0:T(8,128)(2,1)S(1)}, u32[]{:S(2)}, u32[]{:S(2)}) collective-permute-start(bf16[224,384]{1,0:T(8,128)(2,1)S(1)} %get-tuple-element.63), channel_id=1, source_target_pairs={{32,0},{64,32},{96,64},{33,1},{65,33},{97,65},{34,2},{66,34},{98,6... | collective-permute-start | bytes 516104 | tf_op jit(solution)/shard_map/ppermute | solution.py:468
  26.3 8.9 %collective-permute-start.5 = (bf16[48,128]{1,0:T(8,128)(2,1)S(1)}, bf16[48,128]{1,0:T(8,128)(2,1)S(1)}, u32[]{:S(2)}, u32[]{:S(2)}) collective-permute-start(bf16[48,128]{1,0:T(8,128)(2,1)S(1)} %get-tuple-element.65), channel_id=1, source_target_pairs={{0,1},{1,0},{2,3},{3,2},{4,5},{5,4},{6,7},{7,6},{8,9},{9,8},{10,11... | collective-permute-start | bytes 36872 | tf_op jit(solution)/shard_map/ppermute | solution.py:463
  26.4 9.8 %collective-permute-start.6 = (bf16[48,128]{1,0:T(8,128)(2,1)S(1)}, bf16[48,128]{1,0:T(8,128)(2,1)S(1)}, u32[]{:S(2)}, u32[]{:S(2)}) collective-permute-start(bf16[48,128]{1,0:T(8,128)(2,1)S(1)} %get-tuple-element.66), channel_id=1, source_target_pairs={{0,31},{1,2},{2,1},{3,4},{4,3},{5,6},{6,5},{7,8},{8,7},{9,10},{10,... | collective-permute-start | bytes 36872 | tf_op jit(solution)/shard_map/ppermute | solution.py:462
  36.2 8.2 %collective-permute-start.7 = (bf16[176,128]{1,0:T(8,128)(2,1)S(1)}, bf16[176,128]{1,0:T(8,128)(2,1)S(1)}, u32[]{:S(2)}, u32[]{:S(2)}) collective-permute-start(bf16[176,128]{1,0:T(8,128)(2,1)S(1)} %get-tuple-element.68), channel_id=1, source_target_pairs={{0,32},{32,64},{64,96},{1,33},{33,65},{65,97},{2,34},{34,66},{66,9... | collective-permute-start | bytes 135176 | tf_op jit(solution)/shard_map/ppermute | solution.py:467
  40.2 6.1 %collective-permute-start.8 = (bf16[176,128]{1,0:T(8,128)(2,1)S(1)}, bf16[176,128]{1,0:T(8,128)(2,1)S(1)}, u32[]{:S(2)}, u32[]{:S(2)}) collective-permute-start(bf16[176,128]{1,0:T(8,128)(2,1)S(1)} %get-tuple-element.69.after_ref), channel_id=1, source_target_pairs={{32,0},{64,32},{96,64},{33,1},{65,33},{97,65},{34,2},{66,34},{98,6... | collective-permute-start | bytes 135176 | tf_op jit(solution)/shard_map/ppermute | solution.py:468
  53.1 17.5 %collective-permute-start.19 = (bf16[256,1024]{1,0:T(8,128)(2,1)S(1)}, bf16[256,1024]{1,0:T(8,128)(2,1)S(1)}, u32[]{:S(2)}, u32[]{:S(2)}) collective-permute-start(bf16[256,1024]{1,0:T(8,128)(2,1)S(1)} %get-tuple-element.98), channel_id=1, source_target_pairs={{0,8},{8,16},{16,24},{24,0},{32,40},{40,48},{48,56},{56,32},{64,72... | collective-permute-start | bytes 1572872 | tf_op jit(solution)/shard_map/ppermute | solution.py:452
  54.8 21.1 %collective-permute-start.20 = (bf16[256,1024]{1,0:T(8,128)(2,1)S(1)}, bf16[256,1024]{1,0:T(8,128)(2,1)S(1)}, u32[]{:S(2)}, u32[]{:S(2)}) collective-permute-start(bf16[256,1024]{1,0:T(8,128)(2,1)S(1)} %get-tuple-element.99), channel_id=1, source_target_pairs={{0,16},{8,24},{16,0},{24,8},{32,48},{40,56},{48,32},{56,40},{64,80... | collective-permute-start | bytes 1572872 | tf_op jit(solution)/shard_map/ppermute | solution.py:452
  57.7 18.3 %collective-permute-start.21 = (bf16[256,1024]{1,0:T(8,128)(2,1)S(1)}, bf16[256,1024]{1,0:T(8,128)(2,1)S(1)}, u32[]{:S(2)}, u32[]{:S(2)}) collective-permute-start(bf16[256,1024]{1,0:T(8,128)(2,1)S(1)} %get-tuple-element.100), channel_id=1, source_target_pairs={{0,24},{8,0},{16,8},{24,16},{32,56},{40,32},{48,40},{56,48},{64,88... | collective-permute-start | bytes 1572872 | tf_op jit(solution)/shard_map/ppermute | solution.py:452
  67.2 16.2 %collective-permute-start.14 = (bf16[256,1024]{1,0:T(8,128)(2,1)S(1)}, bf16[256,1024]{1,0:T(8,128)(2,1)S(1)}, u32[]{:S(2)}, u32[]{:S(2)}) collective-permute-start(bf16[256,1024]{1,0:T(8,128)(2,1)S(1)} %get-tuple-element.91), channel_id=1, source_target_pairs={{0,2},{1,3},{2,0},{3,1},{32,34},{33,35},{34,32},{35,33},{64,66},{6... | collective-permute-start | bytes 1572872 | tf_op jit(solution)/shard_map/ppermute | solution.py:452
  67.3 23.3 %collective-permute-start.13 = (bf16[256,1024]{1,0:T(8,128)(2,1)S(1)}, bf16[256,1024]{1,0:T(8,128)(2,1)S(1)}, u32[]{:S(2)}, u32[]{:S(2)}) collective-permute-start(bf16[256,1024]{1,0:T(8,128)(2,1)S(1)} %get-tuple-element.90), channel_id=1, source_target_pairs={{0,1},{1,2},{2,3},{3,0},{32,33},{33,34},{34,35},{35,32},{64,65},{6... | collective-permute-start | bytes 1572872 | tf_op jit(solution)/shard_map/ppermute | solution.py:452
  70.7 20.8 %collective-permute-start.15 = (bf16[256,1024]{1,0:T(8,128)(2,1)S(1)}, bf16[256,1024]{1,0:T(8,128)(2,1)S(1)}, u32[]{:S(2)}, u32[]{:S(2)}) collective-permute-start(bf16[256,1024]{1,0:T(8,128)(2,1)S(1)} %get-tuple-element.92), channel_id=1, source_target_pairs={{0,3},{1,0},{2,1},{3,2},{32,35},{33,32},{34,33},{35,34},{64,67},{6... | collective-permute-start | bytes 1572872 | tf_op jit(solution)/shard_map/ppermute | solution.py:452
  76.6 23.1 %collective-permute-start.22 = (bf16[64,1024]{1,0:T(8,128)(2,1)S(1)}, bf16[64,1024]{1,0:T(8,128)(2,1)S(1)}, u32[]{:S(2)}, u32[]{:S(2)}) collective-permute-start(bf16[64,1024]{1,0:T(8,128)(2,1)S(1)} %get-tuple-element.103), channel_id=1, source_target_pairs={{0,1},{1,2},{2,3},{3,0},{32,33},{33,34},{34,35},{35,32},{64,65},{6... | collective-permute-start | bytes 393224 | tf_op jit(solution)/shard_map/ppermute | solution.py:452
  83.4 12.1 %collective-permute-start.9 = (bf16[48,512]{1,0:T(8,128)(2,1)S(1)}, bf16[48,512]{1,0:T(8,128)(2,1)S(1)}, u32[]{:S(2)}, u32[]{:S(2)}) collective-permute-start(bf16[48,512]{1,0:T(8,128)(2,1)S(1)} %get-tuple-element.85), channel_id=1, source_target_pairs={{0,1},{1,0},{2,3},{3,2},{4,5},{5,4},{6,7},{7,6},{8,9},{9,8},{10,11... | collective-permute-start | bytes 147464 | tf_op jit(solution)/shard_map/ppermute | solution.py:463
  83.4 13.7 %collective-permute-start.10 = (bf16[48,512]{1,0:T(8,128)(2,1)S(1)}, bf16[48,512]{1,0:T(8,128)(2,1)S(1)}, u32[]{:S(2)}, u32[]{:S(2)}) collective-permute-start(bf16[48,512]{1,0:T(8,128)(2,1)S(1)} %get-tuple-element.86), channel_id=1, source_target_pairs={{0,31},{1,2},{2,1},{3,4},{4,3},{5,6},{6,5},{7,8},{8,7},{9,10},{10,... | collective-permute-start | bytes 147464 | tf_op jit(solution)/shard_map/ppermute | solution.py:462
  90.6 11.7 %collective-permute-start.23 = (bf16[64,1024]{1,0:T(8,128)(2,1)S(1)}, bf16[64,1024]{1,0:T(8,128)(2,1)S(1)}, u32[]{:S(2)}, u32[]{:S(2)}) collective-permute-start(bf16[64,1024]{1,0:T(8,128)(2,1)S(1)} %get-tuple-element.104), channel_id=1, source_target_pairs={{0,2},{1,3},{2,0},{3,1},{32,34},{33,35},{34,32},{35,33},{64,66},{6... | collective-permute-start | bytes 393224 | tf_op jit(solution)/shard_map/ppermute | solution.py:452
  91.5 13.8 %collective-permute-start.24 = (bf16[64,1024]{1,0:T(8,128)(2,1)S(1)}, bf16[64,1024]{1,0:T(8,128)(2,1)S(1)}, u32[]{:S(2)}, u32[]{:S(2)}) collective-permute-start(bf16[64,1024]{1,0:T(8,128)(2,1)S(1)} %get-tuple-element.105), channel_id=1, source_target_pairs={{0,3},{1,0},{2,1},{3,2},{32,35},{33,32},{34,33},{35,34},{64,67},{6... | collective-permute-start | bytes 393224 | tf_op jit(solution)/shard_map/ppermute | solution.py:452
  95.6 11.0 %collective-permute-start.16 = (bf16[64,1024]{1,0:T(8,128)(2,1)S(1)}, bf16[64,1024]{1,0:T(8,128)(2,1)S(1)}, u32[]{:S(2)}, u32[]{:S(2)}) collective-permute-start(bf16[64,1024]{1,0:T(8,128)(2,1)S(1)} %get-tuple-element.94), channel_id=1, source_target_pairs={{0,8},{8,16},{16,24},{24,0},{32,40},{40,48},{48,56},{56,32},{64,72... | collective-permute-start | bytes 393224 | tf_op jit(solution)/shard_map/ppermute | solution.py:452
  97.1 9.4 %collective-permute-start.17 = (bf16[64,1024]{1,0:T(8,128)(2,1)S(1)}, bf16[64,1024]{1,0:T(8,128)(2,1)S(1)}, u32[]{:S(2)}, u32[]{:S(2)}) collective-permute-start(bf16[64,1024]{1,0:T(8,128)(2,1)S(1)} %get-tuple-element.95), channel_id=1, source_target_pairs={{0,16},{8,24},{16,0},{24,8},{32,48},{40,56},{48,32},{56,40},{64,80... | collective-permute-start | bytes 393224 | tf_op jit(solution)/shard_map/ppermute | solution.py:452
  99.6 6.9 %collective-permute-start.18 = (bf16[64,1024]{1,0:T(8,128)(2,1)S(1)}, bf16[64,1024]{1,0:T(8,128)(2,1)S(1)}, u32[]{:S(2)}, u32[]{:S(2)}) collective-permute-start(bf16[64,1024]{1,0:T(8,128)(2,1)S(1)} %get-tuple-element.96), channel_id=1, source_target_pairs={{0,24},{8,0},{16,8},{24,16},{32,56},{40,32},{48,40},{56,48},{64,88... | collective-permute-start | bytes 393224 | tf_op jit(solution)/shard_map/ppermute | solution.py:452
  102.2 10.5 %collective-permute-start.11 = (bf16[176,512]{1,0:T(8,128)(2,1)S(1)}, bf16[176,512]{1,0:T(8,128)(2,1)S(1)}, u32[]{:S(2)}, u32[]{:S(2)}) collective-permute-start(bf16[176,512]{1,0:T(8,128)(2,1)S(1)} %get-tuple-element.87), channel_id=1, source_target_pairs={{0,32},{32,64},{64,96},{1,33},{33,65},{65,97},{2,34},{34,66},{66,9... | collective-permute-start | bytes 540680 | tf_op jit(solution)/shard_map/ppermute | solution.py:467
  105.2 8.1 %collective-permute-start.12 = (bf16[176,512]{1,0:T(8,128)(2,1)S(1)}, bf16[176,512]{1,0:T(8,128)(2,1)S(1)}, u32[]{:S(2)}, u32[]{:S(2)}) collective-permute-start(bf16[176,512]{1,0:T(8,128)(2,1)S(1)} %get-tuple-element.88), channel_id=1, source_target_pairs={{32,0},{64,32},{96,64},{33,1},{65,33},{97,65},{34,2},{66,34},{98,6... | collective-permute-start | bytes 540680 | tf_op jit(solution)/shard_map/ppermute | solution.py:468
  106.8 12.9 %collective-permute-start.25 = (bf16[64,1024]{1,0:T(8,128)(2,1)S(1)}, bf16[64,1024]{1,0:T(8,128)(2,1)S(1)}, u32[]{:S(2)}, u32[]{:S(2)}) collective-permute-start(bf16[64,1024]{1,0:T(8,128)(2,1)S(1)} %get-tuple-element.108), channel_id=1, source_target_pairs={{0,4},{4,0},{32,36},{36,32},{64,68},{68,64},{96,100},{100,96},{8,1... | collective-permute-start | bytes 393224 | tf_op jit(solution)/shard_map/ppermute | solution.py:452
  119.8 5.8 %collective-permute-start.26 = (bf16[16,1024]{1,0:T(8,128)(2,1)S(1)}, bf16[16,1024]{1,0:T(8,128)(2,1)S(1)}, u32[]{:S(2)}, u32[]{:S(2)}) collective-permute-start(bf16[16,1024]{1,0:T(8,128)(2,1)S(1)} %get-tuple-element.111), channel_id=1, source_target_pairs={{0,32},{32,64},{64,96},{96,0},{4,36},{36,68},{68,100},{100,4},{8,4... | collective-permute-start | bytes 98312 | tf_op jit(solution)/shard_map/ppermute | solution.py:452
  122.3 5.1 %collective-permute-start.27 = (bf16[16,1024]{1,0:T(8,128)(2,1)S(1)}, bf16[16,1024]{1,0:T(8,128)(2,1)S(1)}, u32[]{:S(2)}, u32[]{:S(2)}) collective-permute-start(bf16[16,1024]{1,0:T(8,128)(2,1)S(1)} %get-tuple-element.112), channel_id=1, source_target_pairs={{0,64},{32,96},{64,0},{96,32},{4,68},{36,100},{68,4},{100,36},{8,7... | collective-permute-start | bytes 98312 | tf_op jit(solution)/shard_map/ppermute | solution.py:452
  122.3 5.1 %collective-permute-start.28 = (bf16[16,1024]{1,0:T(8,128)(2,1)S(1)}, bf16[16,1024]{1,0:T(8,128)(2,1)S(1)}, u32[]{:S(2)}, u32[]{:S(2)}) collective-permute-start(bf16[16,1024]{1,0:T(8,128)(2,1)S(1)} %get-tuple-element.113), channel_id=1, source_target_pairs={{0,96},{32,0},{64,32},{96,64},{4,100},{36,4},{68,36},{100,68},{8,1... | collective-permute-start | bytes 98312 | tf_op jit(solution)/shard_map/ppermute | solution.py:452
  (7 other events, 111.1 us)

commit v5 on v4

--- a/solution.py
+++ b/solution.py
@@ -62,8 +62,11 @@
     return jnp.where(even, a, b)
 
 
-def export_kernel(state_ref, out_ref):
-    cells = state_ref[:, :, 0:LANES].reshape(CELLS, LANES).astype(F32)
+def export_kernel(state_ref, out_ref, held, arrived):
+    copy = pltpu.make_async_copy(state_ref.at[:, :, 0:LANES], held, arrived)
+    copy.start()
+    copy.wait()
+    cells = held[...].reshape(CELLS, LANES).astype(F32)
     out_ref[...] = jnp.concatenate(
         [cells[at * LANES : (at + 1) * LANES].T[:Q] for at in range(CELLS // LANES)], axis=0
     ).astype(BF)
@@ -480,7 +483,8 @@
     weights = regrid_weights[0].transpose(0, 2, 1)
 
     (mine,) = run(
-        export_kernel, "export", [shape((48, LANES), BF)], state,
+        export_kernel, "export", [shape((48, LANES), BF)], state, views={0: pl.BlockSpec(memory_space=pl.ANY)},
+        scratch=[vm((ROWS, COLS, LANES), BF), pltpu.SemaphoreType.DMA], room=60,
     )
     fields = lax.ppermute(mine, "group", [(0, 1), (1, 0)])
     one, two = run(

time: 129 us -> 130 us (level)
  Pallas kernels: 31.4 us -> 32.7 us
    pallas_call x20, Pallas kernels: 31.4 us -> 32.7 us  [run(): pl.pallas_call(kernel, out_shape=outs, grid=(1,), in_specs=in_specs, out_...]
  transfers between devices with their start and end apart: 29 -> 29, of which waited for: 11 -> 11; matrix products, arithmetic and copies ran while one was open for 0% -> 0% of each run, Pallas kernels for 18% -> 17%
where the time goes in v5:
time: 130 us
  starting transfers between devices  75.7 us (58%)
  Pallas kernels  32.7 us (25%)
  waiting for transfers between devices  19.1 us (15%)
    ppermute x16, starting transfers between devices, send(): return lax.ppermute(piece, ('lat', 'lon'), pairs)  39.4 us
    pallas_call x20, Pallas kernels, run(): pl.pallas_call(kernel, out_shape=outs, grid=(1,), in_specs=in_specs, out_...  32.7 us
    ppermute x3, starting transfers between devices, swap_lon(): two = lax.ppermute(two, 'lon', other)  20.4 us
    ppermute x3, starting transfers between devices, swap_lat(): above = lax.ppermute(down, 'lat', [(i, i + 1) for i in range(3)])  10.6 us
    ppermute x3, waiting for transfers between devices, swap_lat(): below = lax.ppermute(up, 'lat', [(i + 1, i) for i in range(3)])  6.89 us
    ppermute x16, waiting for transfers between devices, send(): return lax.ppermute(piece, ('lat', 'lon'), pairs)  5.78 us
    ppermute x3, starting transfers between devices, swap_lat(): below = lax.ppermute(up, 'lat', [(i + 1, i) for i in range(3)])  4.19 us
    ppermute x3, waiting for transfers between devices, swap_lon(): two = lax.ppermute(two, 'lon', other)  3.42 us
  transfers between devices with their start and end apart: 29, of which 11 were waited for; matrix products, arithmetic and copies ran while one was open for 0% of the time, Pallas kernels for 17%

profile of v5, /device:TPU:6, one launch (start us, length us, event | category | flops | bytes accessed | tf_op | source)
XLA Modules:
  0.0 129.6 jit_solution(4915395842006327222)
XLA Ops:
  0.7 1.7 %export.1 = bf16[48,128]{1,0:T(8,128)(2,1)} custom-call(bf16[16,48,512]{2,1,0:T(8,128)(2,1)} %bitcast.20), custom_call_target="tpu_custom_call" | custom-call | bytes 1024 | tf_op jit(solution)/shard_map/export/pallas_call | solution.py:39
  6.0 7.8 %collective-permute-start.2 = (bf16[48,512]{1,0:T(8,128)(2,1)S(1)}, bf16[48,512]{1,0:T(8,128)(2,1)S(1)}, u32[]{:S(2)}, u32[]{:S(2)}) collective-permute-start(bf16[48,512]{1,0:T(8,128)(2,1)S(1)} %get-tuple-element.61), channel_id=1, source_target_pairs={{0,31},{1,2},{2,1},{3,4},{4,3},{5,6},{6,5},{7,8},{8,7},{9,10},{10,... | collective-permute-start | bytes 147464 | tf_op jit(solution)/shard_map/ppermute | solution.py:465
  13.7 2.4 %collective-permute-done.2.two_ref = bf16[48,512]{1,0:T(8,128)(2,1)S(1)} collective-permute-done((bf16[48,512]{1,0:T(8,128)(2,1)S(1)}, bf16[48,512]{1,0:T(8,128)(2,1)S(1)}, u32[]{:S(2)}, u32[]{:S(2)}) %collective-permute-start.2) | collective-permute-done | bytes 49184 | tf_op jit(solution)/shard_map/ppermute | solution.py:465
  16.2 3.7 %collective-permute-start.3 = (bf16[224,384]{1,0:T(8,128)(2,1)S(1)}, bf16[224,384]{1,0:T(8,128)(2,1)S(1)}, u32[]{:S(2)}, u32[]{:S(2)}) collective-permute-start(bf16[224,384]{1,0:T(8,128)(2,1)S(1)} %get-tuple-element.62), channel_id=1, source_target_pairs={{0,32},{32,64},{64,96},{1,33},{33,65},{65,97},{2,34},{34,66},{66,9... | collective-permute-start | bytes 516104 | tf_op jit(solution)/shard_map/ppermute | solution.py:470
  21.3 1.6 %collective-permute-done.3.above_ref = bf16[224,384]{1,0:T(8,128)(2,1)S(1)} collective-permute-done((bf16[224,384]{1,0:T(8,128)(2,1)S(1)}, bf16[224,384]{1,0:T(8,128)(2,1)S(1)}, u32[]{:S(2)}, u32[]{:S(2)}) %collective-permute-start.3) | collective-permute-done | bytes 172064 | tf_op jit(solution)/shard_map/ppermute | solution.py:470
  22.9 4.4 %collective-permute-done.4.below_ref = bf16[224,384]{1,0:T(8,128)(2,1)S(1)} collective-permute-done((bf16[224,384]{1,0:T(8,128)(2,1)S(1)}, bf16[224,384]{1,0:T(8,128)(2,1)S(1)}, u32[]{:S(2)}, u32[]{:S(2)}) %collective-permute-start.4) | collective-permute-done | bytes 172064 | tf_op jit(solution)/shard_map/ppermute | solution.py:471
  28.2 7.1 %collective-permute-start.6 = (bf16[48,128]{1,0:T(8,128)(2,1)S(1)}, bf16[48,128]{1,0:T(8,128)(2,1)S(1)}, u32[]{:S(2)}, u32[]{:S(2)}) collective-permute-start(bf16[48,128]{1,0:T(8,128)(2,1)S(1)} %get-tuple-element.66), channel_id=1, source_target_pairs={{0,31},{1,2},{2,1},{3,4},{4,3},{5,6},{6,5},{7,8},{8,7},{9,10},{10,... | collective-permute-start | bytes 36872 | tf_op jit(solution)/shard_map/ppermute | solution.py:465
  38.1 3.9 %collective-permute-start.7 = (bf16[176,128]{1,0:T(8,128)(2,1)S(1)}, bf16[176,128]{1,0:T(8,128)(2,1)S(1)}, u32[]{:S(2)}, u32[]{:S(2)}) collective-permute-start(bf16[176,128]{1,0:T(8,128)(2,1)S(1)} %get-tuple-element.68), channel_id=1, source_target_pairs={{0,32},{32,64},{64,96},{1,33},{33,65},{65,97},{2,34},{34,66},{66,9... | collective-permute-start | bytes 135176 | tf_op jit(solution)/shard_map/ppermute | solution.py:470
  42.0 1.6 %collective-permute-start.8 = (bf16[176,128]{1,0:T(8,128)(2,1)S(1)}, bf16[176,128]{1,0:T(8,128)(2,1)S(1)}, u32[]{:S(2)}, u32[]{:S(2)}) collective-permute-start(bf16[176,128]{1,0:T(8,128)(2,1)S(1)} %get-tuple-element.69.after_ref), channel_id=1, source_target_pairs={{32,0},{64,32},{96,64},{33,1},{65,33},{97,65},{34,2},{66,34},{98,6... | collective-permute-start | bytes 135176 | tf_op jit(solution)/shard_map/ppermute | solution.py:471
  43.6 2.7 %conv_two.1.more_ref = f32[2,16,48,128]{3,2,1,0:T(8,128)S(1)} custom-call(bf16[16,48,512]{2,1,0:T(8,128)(2,1)S(1)} %bitcast.25, bf16[48,512]{1,0:T(8,128)(2,1)S(1)} %collective-permute-done.1.one_ref, bf16[48,512]{1,0:T(8,128)(2,1)S(1)} %collective-permute-done.2.two_ref, bf16[224,384]{1,0:T(8,128)(2,1)S(1)} %collective-permute-done.3.above_ref, ...), custom_call_target="tpu_custom_call" | custom-call | bytes 1024 | tf_op jit(solution)/shard_map/conv_two/pallas_call | solution.py:39
  46.3 1.8 %collective-permute-done.8.below_ref = bf16[176,128]{1,0:T(8,128)(2,1)S(1)} collective-permute-done((bf16[176,128]{1,0:T(8,128)(2,1)S(1)}, bf16[176,128]{1,0:T(8,128)(2,1)S(1)}, u32[]{:S(2)}, u32[]{:S(2)}) %collective-permute-start.8) | collective-permute-done | bytes 45088 | tf_op jit(solution)/shard_map/ppermute | solution.py:471
  48.1 2.3 %conv_norm.1 = (bf16[16,48,512]{2,1,0:T(8,128)(2,1)S(1)}, f32[16,48,512]{2,1,0:T(8,128)S(1)}, f32[16,48,128]{2,1,0:T(8,128)S(1)}) custom-call(bf16[768,128]{1,0:T(8,128)(2,1)S(1)} %get-tuple-element.64.after_ref.cells_ref.forced_ref, bf16[48,128]{1,0:T(8,128)(2,1)S(1)} %collective-permute-done.5.one_ref, bf16[48,128]{1,0:T(8,128)(2,1)S(1)} %collective-permute-done.6.two_ref, ...), custom_call_target="tpu_custom_call" | custom-call | bytes 1024 | tf_op jit(solution)/shard_map/conv_norm/pallas_call | solution.py:39
  50.4 4.4 %mlp_y.1 = (bf16[256,1024]{1,0:T(8,128)(2,1)S(1)}, bf16[256,1024]{1,0:T(8,128)(2,1)S(1)}, bf16[256,1024]{1,0:T(8,128)(2,1)S(1)}, bf16[256,1024]{1,0:T(8,128)(2,1...) custom-call(bf16[768,512]{1,0:T(8,128)(2,1)S(1)} %bitcast.33, ...), custom_call_target="tpu_custom_call" | custom-call | bytes 1024 | tf_op jit(solution)/shard_map/mlp_y/pallas_call | solution.py:39
  54.8 1.7 %collective-permute-start.19 = (bf16[256,1024]{1,0:T(8,128)(2,1)S(1)}, bf16[256,1024]{1,0:T(8,128)(2,1)S(1)}, u32[]{:S(2)}, u32[]{:S(2)}) collective-permute-start(bf16[256,1024]{1,0:T(8,128)(2,1)S(1)} %get-tuple-element.98), channel_id=1, source_target_pairs={{0,8},{8,16},{16,24},{24,0},{32,40},{40,48},{48,56},{56,32},{64,72... | collective-permute-start | bytes 1572872 | tf_op jit(solution)/shard_map/ppermute | solution.py:455
  56.5 2.9 %collective-permute-start.20 = (bf16[256,1024]{1,0:T(8,128)(2,1)S(1)}, bf16[256,1024]{1,0:T(8,128)(2,1)S(1)}, u32[]{:S(2)}, u32[]{:S(2)}) collective-permute-start(bf16[256,1024]{1,0:T(8,128)(2,1)S(1)} %get-tuple-element.99), channel_id=1, source_target_pairs={{0,16},{8,24},{16,0},{24,8},{32,48},{40,56},{48,32},{56,40},{64,80... | collective-permute-start | bytes 1572872 | tf_op jit(solution)/shard_map/ppermute | solution.py:455
  60.8 4.4 %mlp_x.1 = (bf16[256,1024]{1,0:T(8,128)(2,1)S(1)}, bf16[256,1024]{1,0:T(8,128)(2,1)S(1)}, bf16[256,1024]{1,0:T(8,128)(2,1)S(1)}, bf16[256,1024]{1,0:T(8,128)(2,1...) custom-call(bf16[768,512]{1,0:T(8,128)(2,1)S(1)} %bitcast.34, ...), custom_call_target="tpu_custom_call" | custom-call | bytes 1024 | tf_op jit(solution)/shard_map/mlp_x/pallas_call | solution.py:39
  65.2 3.6 %finish.1 = (bf16[768,512]{1,0:T(8,128)(2,1)S(1)}, bf16[48,512]{1,0:T(8,128)(2,1)S(1)}, bf16[48,512]{1,0:T(8,128)(2,1)S(1)}, bf16[256,1024]{1,0:T(8,128)(2,1)S(1)}) custom-call(bf16[768,1024]{1,0:T(8,128)(2,1)S(1)} %get-tuple-element.76.pre_a_ref, bf16[768,1024]{1,0:T(8,128)(2,1)S(1)} %get-tuple-element.77.pre_b_ref, ...), custom_call_target="tpu_custom_call", output_to_operand_aliasing={{3}: (7, {})} | custom-call | bytes 1024 | tf_op jit(solution)/shard_map/finish/pallas_call | solution.py:39
  68.9 3.4 %collective-permute-start.13 = (bf16[256,1024]{1,0:T(8,128)(2,1)S(1)}, bf16[256,1024]{1,0:T(8,128)(2,1)S(1)}, u32[]{:S(2)}, u32[]{:S(2)}) collective-permute-start(bf16[256,1024]{1,0:T(8,128)(2,1)S(1)} %get-tuple-element.90), channel_id=1, source_target_pairs={{0,1},{1,2},{2,3},{3,0},{32,33},{33,34},{34,35},{35,32},{64,65},{6... | collective-permute-start | bytes 1572872 | tf_op jit(solution)/shard_map/ppermute | solution.py:455
  73.1 2.7 %advance.1 = (bf16[768,512]{1,0:T(8,128)(2,1)}, f32[8,128]{1,0:T(8,128)S(1)}) custom-call(bf16[768,1024]{1,0:T(8,128)(2,1)S(1)} %get-tuple-element.72.act_a_ref, bf16[768,1024]{1,0:T(8,128)(2,1)S(1)} %get-tuple-element.73.act_b_ref, bf16[1024,512]{1,0:T(8,128)(2,1)S(1)} %get-tuple-element.74.w_out_a_ref, ...), custom_call_target="tpu_custom_call" | custom-call | bytes 1024 | tf_op jit(solution)/shard_map/advance/pallas_call | solution.py:39
  75.7 2.0 %collective-permute-done.20.c = bf16[256,1024]{1,0:T(8,128)(2,1)S(1)} collective-permute-done((bf16[256,1024]{1,0:T(8,128)(2,1)S(1)}, bf16[256,1024]{1,0:T(8,128)(2,1)S(1)}, u32[]{:S(2)}, u32[]{:S(2)}) %collective-permute-start.20) | collective-permute-done | bytes 524320 | tf_op jit(solution)/shard_map/ppermute | solution.py:455
  78.3 6.9 %collective-permute-start.22 = (bf16[64,1024]{1,0:T(8,128)(2,1)S(1)}, bf16[64,1024]{1,0:T(8,128)(2,1)S(1)}, u32[]{:S(2)}, u32[]{:S(2)}) collective-permute-start(bf16[64,1024]{1,0:T(8,128)(2,1)S(1)} %get-tuple-element.103), channel_id=1, source_target_pairs={{0,1},{1,2},{2,3},{3,0},{32,33},{33,34},{34,35},{35,32},{64,65},{6... | collective-permute-start | bytes 393224 | tf_op jit(solution)/shard_map/ppermute | solution.py:455
  85.1 5.5 %collective-permute-start.10 = (bf16[48,512]{1,0:T(8,128)(2,1)S(1)}, bf16[48,512]{1,0:T(8,128)(2,1)S(1)}, u32[]{:S(2)}, u32[]{:S(2)}) collective-permute-start(bf16[48,512]{1,0:T(8,128)(2,1)S(1)} %get-tuple-element.86), channel_id=1, source_target_pairs={{0,31},{1,2},{2,1},{3,4},{4,3},{5,6},{6,5},{7,8},{8,7},{9,10},{10,... | collective-permute-start | bytes 147464 | tf_op jit(solution)/shard_map/ppermute | solution.py:465
  90.6 1.6 %collective-permute-done.13.b = bf16[256,1024]{1,0:T(8,128)(2,1)S(1)} collective-permute-done((bf16[256,1024]{1,0:T(8,128)(2,1)S(1)}, bf16[256,1024]{1,0:T(8,128)(2,1)S(1)}, u32[]{:S(2)}, u32[]{:S(2)}) %collective-permute-start.13) | collective-permute-done | bytes 524320 | tf_op jit(solution)/shard_map/ppermute | solution.py:455
  93.1 3.6 %collective-permute-start.24 = (bf16[64,1024]{1,0:T(8,128)(2,1)S(1)}, bf16[64,1024]{1,0:T(8,128)(2,1)S(1)}, u32[]{:S(2)}, u32[]{:S(2)}) collective-permute-start(bf16[64,1024]{1,0:T(8,128)(2,1)S(1)} %get-tuple-element.105), channel_id=1, source_target_pairs={{0,3},{1,0},{2,1},{3,2},{32,35},{33,32},{34,33},{35,34},{64,67},{6... | collective-permute-start | bytes 393224 | tf_op jit(solution)/shard_map/ppermute | solution.py:455
  98.8 2.5 %collective-permute-start.17 = (bf16[64,1024]{1,0:T(8,128)(2,1)S(1)}, bf16[64,1024]{1,0:T(8,128)(2,1)S(1)}, u32[]{:S(2)}, u32[]{:S(2)}) collective-permute-start(bf16[64,1024]{1,0:T(8,128)(2,1)S(1)} %get-tuple-element.95), channel_id=1, source_target_pairs={{0,16},{8,24},{16,0},{24,8},{32,48},{40,56},{48,32},{56,40},{64,80... | collective-permute-start | bytes 393224 | tf_op jit(solution)/shard_map/ppermute | solution.py:455
  101.3 2.5 %collective-permute-start.18 = (bf16[64,1024]{1,0:T(8,128)(2,1)S(1)}, bf16[64,1024]{1,0:T(8,128)(2,1)S(1)}, u32[]{:S(2)}, u32[]{:S(2)}) collective-permute-start(bf16[64,1024]{1,0:T(8,128)(2,1)S(1)} %get-tuple-element.96), channel_id=1, source_target_pairs={{0,24},{8,0},{16,8},{24,16},{32,56},{40,32},{48,40},{56,48},{64,88... | collective-permute-start | bytes 393224 | tf_op jit(solution)/shard_map/ppermute | solution.py:455
  103.8 3.0 %collective-permute-start.11 = (bf16[176,512]{1,0:T(8,128)(2,1)S(1)}, bf16[176,512]{1,0:T(8,128)(2,1)S(1)}, u32[]{:S(2)}, u32[]{:S(2)}) collective-permute-start(bf16[176,512]{1,0:T(8,128)(2,1)S(1)} %get-tuple-element.87), channel_id=1, source_target_pairs={{0,32},{32,64},{64,96},{1,33},{33,65},{65,97},{2,34},{34,66},{66,9... | collective-permute-start | bytes 540680 | tf_op jit(solution)/shard_map/ppermute | solution.py:470
  108.4 5.9 %collective-permute-start.25 = (bf16[64,1024]{1,0:T(8,128)(2,1)S(1)}, bf16[64,1024]{1,0:T(8,128)(2,1)S(1)}, u32[]{:S(2)}, u32[]{:S(2)}) collective-permute-start(bf16[64,1024]{1,0:T(8,128)(2,1)S(1)} %get-tuple-element.108), channel_id=1, source_target_pairs={{0,4},{4,0},{32,36},{36,32},{64,68},{68,64},{96,100},{100,96},{8,1... | collective-permute-start | bytes 393224 | tf_op jit(solution)/shard_map/ppermute | solution.py:455
  115.0 6.3 %conv_back.1 = (bf16[16,48,512]{2,1,0:T(8,128)(2,1)}, f32[8,128]{1,0:T(8,128)S(1)}) custom-call(bf16[768,512]{1,0:T(8,128)(2,1)S(1)} %get-tuple-element.83.after_ref.cells_ref.after.d_hidden_ref, bf16[48,512]{1,0:T(8,128)(2,1)S(1)} %collective-permute-done.9.one_ref.after_ref, bf16[48,512]{1,0:T(8,128)(2,1)S(1)} %collective-permute-done.10.two_ref, ...), custom_call_target="tpu_custom_call" | custom-call | bytes 1024 | tf_op jit(solution)/shard_map/conv_back/pallas_call | solution.py:39
  121.4 2.5 %collective-permute-start.26 = (bf16[16,1024]{1,0:T(8,128)(2,1)S(1)}, bf16[16,1024]{1,0:T(8,128)(2,1)S(1)}, u32[]{:S(2)}, u32[]{:S(2)}) collective-permute-start(bf16[16,1024]{1,0:T(8,128)(2,1)S(1)} %get-tuple-element.111), channel_id=1, source_target_pairs={{0,32},{32,64},{64,96},{96,0},{4,36},{36,68},{68,100},{100,4},{8,4... | collective-permute-start | bytes 98312 | tf_op jit(solution)/shard_map/ppermute | solution.py:455
  123.9 2.8 %collective-permute-start.28 = (bf16[16,1024]{1,0:T(8,128)(2,1)S(1)}, bf16[16,1024]{1,0:T(8,128)(2,1)S(1)}, u32[]{:S(2)}, u32[]{:S(2)}) collective-permute-start(bf16[16,1024]{1,0:T(8,128)(2,1)S(1)} %get-tuple-element.113), channel_id=1, source_target_pairs={{0,96},{32,0},{64,32},{96,64},{4,100},{36,4},{68,36},{100,68},{8,1... | collective-permute-start | bytes 98312 | tf_op jit(solution)/shard_map/ppermute | solution.py:455
  127.2 1.8 %collective-permute-done.27.refs_2_ = bf16[16,1024]{1,0:T(8,128)(2,1)S(1)} collective-permute-done((bf16[16,1024]{1,0:T(8,128)(2,1)S(1)}, bf16[16,1024]{1,0:T(8,128)(2,1)S(1)}, u32[]{:S(2)}, u32[]{:S(2)}) %collective-permute-start.27) | collective-permute-done | bytes 32800 | tf_op jit(solution)/shard_map/ppermute | solution.py:455
  (66 shorter events, 17.7 us)
Async XLA Ops:
  0.6 34.7 %copy-start.4 = (bf16[1,16,48,512]{3,2,1,0:T(8,128)(2,1)S(1)}, bf16[1,16,48,512]{3,2,1,0:T(8,128)(2,1)}, u32[]{:S(2)}) copy-start(bf16[1,16,48,512]{3,2,1,0:T(8,128)(2,1)} %param.10) | copy-start | bytes 2359300
  0.7 34.7 %copy-start.7 = (s32[16,48]{1,0:T(8,128)S(1)}, s32[16,48]{1,0:T(8,128)}, u32[]{:S(2)}) copy-start(s32[16,48]{1,0:T(8,128)} %mask_ref.1) | copy-start | bytes 9220
  2.4 1.5 %collective-permute-start = (bf16[48,128]{1,0:T(8,128)(2,1)}, bf16[48,128]{1,0:T(8,128)(2,1)S(1)}, u32[]{:S(2)}, u32[]{:S(2)}) collective-permute-start(bf16[48,128]{1,0:T(8,128)(2,1)} %export.1), channel_id=1, source_target_pairs={{0,128},{128,0},{1,129},{129,1},{2,130},{130,2},{3,131},{131,3},{4... | collective-permute-start | bytes 36872 | tf_op jit(solution)/shard_map/ppermute | solution.py:489
  5.0 8.7 %collective-permute-start.1 = (bf16[48,512]{1,0:T(8,128)(2,1)S(1)}, bf16[48,512]{1,0:T(8,128)(2,1)S(1)}, u32[]{:S(2)}, u32[]{:S(2)}) collective-permute-start(bf16[48,512]{1,0:T(8,128)(2,1)S(1)} %get-tuple-element.60), channel_id=1, source_target_pairs={{0,1},{1,0},{2,3},{3,2},{4,5},{5,4},{6,7},{7,6},{8,9},{9,8},{10,11... | collective-permute-start | bytes 147464 | tf_op jit(solution)/shard_map/ppermute | solution.py:466
  6.0 29.7 %copy-start.5 = (f32[1,7,7,512]{3,0,2,1:T(1,128)S(1)}, f32[1,7,7,512]{3,0,2,1:T(1,128)}, u32[]{:S(2)}) copy-start(f32[1,7,7,512]{3,0,2,1:T(1,128)} %param.11) | copy-start | bytes 301060
  6.0 10.2 %collective-permute-start.2 = (bf16[48,512]{1,0:T(8,128)(2,1)S(1)}, bf16[48,512]{1,0:T(8,128)(2,1)S(1)}, u32[]{:S(2)}, u32[]{:S(2)}) collective-permute-start(bf16[48,512]{1,0:T(8,128)(2,1)S(1)} %get-tuple-element.61), channel_id=1, source_target_pairs={{0,31},{1,2},{2,1},{3,4},{4,3},{5,6},{6,5},{7,8},{8,7},{9,10},{10,... | collective-permute-start | bytes 147464 | tf_op jit(solution)/shard_map/ppermute | solution.py:465
  16.2 6.6 %collective-permute-start.3 = (bf16[224,384]{1,0:T(8,128)(2,1)S(1)}, bf16[224,384]{1,0:T(8,128)(2,1)S(1)}, u32[]{:S(2)}, u32[]{:S(2)}) collective-permute-start(bf16[224,384]{1,0:T(8,128)(2,1)S(1)} %get-tuple-element.62), channel_id=1, source_target_pairs={{0,32},{32,64},{64,96},{1,33},{33,65},{65,97},{2,34},{34,66},{66,9... | collective-permute-start | bytes 516104 | tf_op jit(solution)/shard_map/ppermute | solution.py:470
  20.0 7.3 %collective-permute-start.4 = (bf16[224,384]{1,0:T(8,128)(2,1)S(1)}, bf16[224,384]{1,0:T(8,128)(2,1)S(1)}, u32[]{:S(2)}, u32[]{:S(2)}) collective-permute-start(bf16[224,384]{1,0:T(8,128)(2,1)S(1)} %get-tuple-element.63), channel_id=1, source_target_pairs={{32,0},{64,32},{96,64},{33,1},{65,33},{97,65},{34,2},{66,34},{98,6... | collective-permute-start | bytes 516104 | tf_op jit(solution)/shard_map/ppermute | solution.py:471
  28.1 8.9 %collective-permute-start.5 = (bf16[48,128]{1,0:T(8,128)(2,1)S(1)}, bf16[48,128]{1,0:T(8,128)(2,1)S(1)}, u32[]{:S(2)}, u32[]{:S(2)}) collective-permute-start(bf16[48,128]{1,0:T(8,128)(2,1)S(1)} %get-tuple-element.65), channel_id=1, source_target_pairs={{0,1},{1,0},{2,3},{3,2},{4,5},{5,4},{6,7},{7,6},{8,9},{9,8},{10,11... | collective-permute-start | bytes 36872 | tf_op jit(solution)/shard_map/ppermute | solution.py:466
  28.2 9.8 %collective-permute-start.6 = (bf16[48,128]{1,0:T(8,128)(2,1)S(1)}, bf16[48,128]{1,0:T(8,128)(2,1)S(1)}, u32[]{:S(2)}, u32[]{:S(2)}) collective-permute-start(bf16[48,128]{1,0:T(8,128)(2,1)S(1)} %get-tuple-element.66), channel_id=1, source_target_pairs={{0,31},{1,2},{2,1},{3,4},{4,3},{5,6},{6,5},{7,8},{8,7},{9,10},{10,... | collective-permute-start | bytes 36872 | tf_op jit(solution)/shard_map/ppermute | solution.py:465
  38.1 8.2 %collective-permute-start.7 = (bf16[176,128]{1,0:T(8,128)(2,1)S(1)}, bf16[176,128]{1,0:T(8,128)(2,1)S(1)}, u32[]{:S(2)}, u32[]{:S(2)}) collective-permute-start(bf16[176,128]{1,0:T(8,128)(2,1)S(1)} %get-tuple-element.68), channel_id=1, source_target_pairs={{0,32},{32,64},{64,96},{1,33},{33,65},{65,97},{2,34},{34,66},{66,9... | collective-permute-start | bytes 135176 | tf_op jit(solution)/shard_map/ppermute | solution.py:470
  42.0 6.1 %collective-permute-start.8 = (bf16[176,128]{1,0:T(8,128)(2,1)S(1)}, bf16[176,128]{1,0:T(8,128)(2,1)S(1)}, u32[]{:S(2)}, u32[]{:S(2)}) collective-permute-start(bf16[176,128]{1,0:T(8,128)(2,1)S(1)} %get-tuple-element.69.after_ref), channel_id=1, source_target_pairs={{32,0},{64,32},{96,64},{33,1},{65,33},{97,65},{34,2},{66,34},{98,6... | collective-permute-start | bytes 135176 | tf_op jit(solution)/shard_map/ppermute | solution.py:471
  54.8 17.5 %collective-permute-start.19 = (bf16[256,1024]{1,0:T(8,128)(2,1)S(1)}, bf16[256,1024]{1,0:T(8,128)(2,1)S(1)}, u32[]{:S(2)}, u32[]{:S(2)}) collective-permute-start(bf16[256,1024]{1,0:T(8,128)(2,1)S(1)} %get-tuple-element.98), channel_id=1, source_target_pairs={{0,8},{8,16},{16,24},{24,0},{32,40},{40,48},{48,56},{56,32},{64,72... | collective-permute-start | bytes 1572872 | tf_op jit(solution)/shard_map/ppermute | solution.py:455
  56.5 21.1 %collective-permute-start.20 = (bf16[256,1024]{1,0:T(8,128)(2,1)S(1)}, bf16[256,1024]{1,0:T(8,128)(2,1)S(1)}, u32[]{:S(2)}, u32[]{:S(2)}) collective-permute-start(bf16[256,1024]{1,0:T(8,128)(2,1)S(1)} %get-tuple-element.99), channel_id=1, source_target_pairs={{0,16},{8,24},{16,0},{24,8},{32,48},{40,56},{48,32},{56,40},{64,80... | collective-permute-start | bytes 1572872 | tf_op jit(solution)/shard_map/ppermute | solution.py:455
  59.4 18.2 %collective-permute-start.21 = (bf16[256,1024]{1,0:T(8,128)(2,1)S(1)}, bf16[256,1024]{1,0:T(8,128)(2,1)S(1)}, u32[]{:S(2)}, u32[]{:S(2)}) collective-permute-start(bf16[256,1024]{1,0:T(8,128)(2,1)S(1)} %get-tuple-element.100), channel_id=1, source_target_pairs={{0,24},{8,0},{16,8},{24,16},{32,56},{40,32},{48,40},{56,48},{64,88... | collective-permute-start | bytes 1572872 | tf_op jit(solution)/shard_map/ppermute | solution.py:455
  68.8 16.3 %collective-permute-start.14 = (bf16[256,1024]{1,0:T(8,128)(2,1)S(1)}, bf16[256,1024]{1,0:T(8,128)(2,1)S(1)}, u32[]{:S(2)}, u32[]{:S(2)}) collective-permute-start(bf16[256,1024]{1,0:T(8,128)(2,1)S(1)} %get-tuple-element.91), channel_id=1, source_target_pairs={{0,2},{1,3},{2,0},{3,1},{32,34},{33,35},{34,32},{35,33},{64,66},{6... | collective-permute-start | bytes 1572872 | tf_op jit(solution)/shard_map/ppermute | solution.py:455
  68.9 23.3 %collective-permute-start.13 = (bf16[256,1024]{1,0:T(8,128)(2,1)S(1)}, bf16[256,1024]{1,0:T(8,128)(2,1)S(1)}, u32[]{:S(2)}, u32[]{:S(2)}) collective-permute-start(bf16[256,1024]{1,0:T(8,128)(2,1)S(1)} %get-tuple-element.90), channel_id=1, source_target_pairs={{0,1},{1,2},{2,3},{3,0},{32,33},{33,34},{34,35},{35,32},{64,65},{6... | collective-permute-start | bytes 1572872 | tf_op jit(solution)/shard_map/ppermute | solution.py:455
  72.3 20.8 %collective-permute-start.15 = (bf16[256,1024]{1,0:T(8,128)(2,1)S(1)}, bf16[256,1024]{1,0:T(8,128)(2,1)S(1)}, u32[]{:S(2)}, u32[]{:S(2)}) collective-permute-start(bf16[256,1024]{1,0:T(8,128)(2,1)S(1)} %get-tuple-element.92), channel_id=1, source_target_pairs={{0,3},{1,0},{2,1},{3,2},{32,35},{33,32},{34,33},{35,34},{64,67},{6... | collective-permute-start | bytes 1572872 | tf_op jit(solution)/shard_map/ppermute | solution.py:455
  78.3 23.0 %collective-permute-start.22 = (bf16[64,1024]{1,0:T(8,128)(2,1)S(1)}, bf16[64,1024]{1,0:T(8,128)(2,1)S(1)}, u32[]{:S(2)}, u32[]{:S(2)}) collective-permute-start(bf16[64,1024]{1,0:T(8,128)(2,1)S(1)} %get-tuple-element.103), channel_id=1, source_target_pairs={{0,1},{1,2},{2,3},{3,0},{32,33},{33,34},{34,35},{35,32},{64,65},{6... | collective-permute-start | bytes 393224 | tf_op jit(solution)/shard_map/ppermute | solution.py:455
  85.1 12.1 %collective-permute-start.9 = (bf16[48,512]{1,0:T(8,128)(2,1)S(1)}, bf16[48,512]{1,0:T(8,128)(2,1)S(1)}, u32[]{:S(2)}, u32[]{:S(2)}) collective-permute-start(bf16[48,512]{1,0:T(8,128)(2,1)S(1)} %get-tuple-element.85), channel_id=1, source_target_pairs={{0,1},{1,0},{2,3},{3,2},{4,5},{5,4},{6,7},{7,6},{8,9},{9,8},{10,11... | collective-permute-start | bytes 147464 | tf_op jit(solution)/shard_map/ppermute | solution.py:466
  85.1 13.6 %collective-permute-start.10 = (bf16[48,512]{1,0:T(8,128)(2,1)S(1)}, bf16[48,512]{1,0:T(8,128)(2,1)S(1)}, u32[]{:S(2)}, u32[]{:S(2)}) collective-permute-start(bf16[48,512]{1,0:T(8,128)(2,1)S(1)} %get-tuple-element.86), channel_id=1, source_target_pairs={{0,31},{1,2},{2,1},{3,4},{4,3},{5,6},{6,5},{7,8},{8,7},{9,10},{10,... | collective-permute-start | bytes 147464 | tf_op jit(solution)/shard_map/ppermute | solution.py:465
  92.2 11.6 %collective-permute-start.23 = (bf16[64,1024]{1,0:T(8,128)(2,1)S(1)}, bf16[64,1024]{1,0:T(8,128)(2,1)S(1)}, u32[]{:S(2)}, u32[]{:S(2)}) collective-permute-start(bf16[64,1024]{1,0:T(8,128)(2,1)S(1)} %get-tuple-element.104), channel_id=1, source_target_pairs={{0,2},{1,3},{2,0},{3,1},{32,34},{33,35},{34,32},{35,33},{64,66},{6... | collective-permute-start | bytes 393224 | tf_op jit(solution)/shard_map/ppermute | solution.py:455
  93.1 13.8 %collective-permute-start.24 = (bf16[64,1024]{1,0:T(8,128)(2,1)S(1)}, bf16[64,1024]{1,0:T(8,128)(2,1)S(1)}, u32[]{:S(2)}, u32[]{:S(2)}) collective-permute-start(bf16[64,1024]{1,0:T(8,128)(2,1)S(1)} %get-tuple-element.105), channel_id=1, source_target_pairs={{0,3},{1,0},{2,1},{3,2},{32,35},{33,32},{34,33},{35,34},{64,67},{6... | collective-permute-start | bytes 393224 | tf_op jit(solution)/shard_map/ppermute | solution.py:455
  97.2 10.9 %collective-permute-start.16 = (bf16[64,1024]{1,0:T(8,128)(2,1)S(1)}, bf16[64,1024]{1,0:T(8,128)(2,1)S(1)}, u32[]{:S(2)}, u32[]{:S(2)}) collective-permute-start(bf16[64,1024]{1,0:T(8,128)(2,1)S(1)} %get-tuple-element.94), channel_id=1, source_target_pairs={{0,8},{8,16},{16,24},{24,0},{32,40},{40,48},{48,56},{56,32},{64,72... | collective-permute-start | bytes 393224 | tf_op jit(solution)/shard_map/ppermute | solution.py:455
  98.8 9.4 %collective-permute-start.17 = (bf16[64,1024]{1,0:T(8,128)(2,1)S(1)}, bf16[64,1024]{1,0:T(8,128)(2,1)S(1)}, u32[]{:S(2)}, u32[]{:S(2)}) collective-permute-start(bf16[64,1024]{1,0:T(8,128)(2,1)S(1)} %get-tuple-element.95), channel_id=1, source_target_pairs={{0,16},{8,24},{16,0},{24,8},{32,48},{40,56},{48,32},{56,40},{64,80... | collective-permute-start | bytes 393224 | tf_op jit(solution)/shard_map/ppermute | solution.py:455
  101.3 6.9 %collective-permute-start.18 = (bf16[64,1024]{1,0:T(8,128)(2,1)S(1)}, bf16[64,1024]{1,0:T(8,128)(2,1)S(1)}, u32[]{:S(2)}, u32[]{:S(2)}) collective-permute-start(bf16[64,1024]{1,0:T(8,128)(2,1)S(1)} %get-tuple-element.96), channel_id=1, source_target_pairs={{0,24},{8,0},{16,8},{24,16},{32,56},{40,32},{48,40},{56,48},{64,88... | collective-permute-start | bytes 393224 | tf_op jit(solution)/shard_map/ppermute | solution.py:455
  103.8 10.5 %collective-permute-start.11 = (bf16[176,512]{1,0:T(8,128)(2,1)S(1)}, bf16[176,512]{1,0:T(8,128)(2,1)S(1)}, u32[]{:S(2)}, u32[]{:S(2)}) collective-permute-start(bf16[176,512]{1,0:T(8,128)(2,1)S(1)} %get-tuple-element.87), channel_id=1, source_target_pairs={{0,32},{32,64},{64,96},{1,33},{33,65},{65,97},{2,34},{34,66},{66,9... | collective-permute-start | bytes 540680 | tf_op jit(solution)/shard_map/ppermute | solution.py:470
  106.9 8.1 %collective-permute-start.12 = (bf16[176,512]{1,0:T(8,128)(2,1)S(1)}, bf16[176,512]{1,0:T(8,128)(2,1)S(1)}, u32[]{:S(2)}, u32[]{:S(2)}) collective-permute-start(bf16[176,512]{1,0:T(8,128)(2,1)S(1)} %get-tuple-element.88), channel_id=1, source_target_pairs={{32,0},{64,32},{96,64},{33,1},{65,33},{97,65},{34,2},{66,34},{98,6... | collective-permute-start | bytes 540680 | tf_op jit(solution)/shard_map/ppermute | solution.py:471
  108.4 12.9 %collective-permute-start.25 = (bf16[64,1024]{1,0:T(8,128)(2,1)S(1)}, bf16[64,1024]{1,0:T(8,128)(2,1)S(1)}, u32[]{:S(2)}, u32[]{:S(2)}) collective-permute-start(bf16[64,1024]{1,0:T(8,128)(2,1)S(1)} %get-tuple-element.108), channel_id=1, source_target_pairs={{0,4},{4,0},{32,36},{36,32},{64,68},{68,64},{96,100},{100,96},{8,1... | collective-permute-start | bytes 393224 | tf_op jit(solution)/shard_map/ppermute | solution.py:455
  121.4 5.8 %collective-permute-start.26 = (bf16[16,1024]{1,0:T(8,128)(2,1)S(1)}, bf16[16,1024]{1,0:T(8,128)(2,1)S(1)}, u32[]{:S(2)}, u32[]{:S(2)}) collective-permute-start(bf16[16,1024]{1,0:T(8,128)(2,1)S(1)} %get-tuple-element.111), channel_id=1, source_target_pairs={{0,32},{32,64},{64,96},{96,0},{4,36},{36,68},{68,100},{100,4},{8,4... | collective-permute-start | bytes 98312 | tf_op jit(solution)/shard_map/ppermute | solution.py:455
  123.9 5.1 %collective-permute-start.27 = (bf16[16,1024]{1,0:T(8,128)(2,1)S(1)}, bf16[16,1024]{1,0:T(8,128)(2,1)S(1)}, u32[]{:S(2)}, u32[]{:S(2)}) collective-permute-start(bf16[16,1024]{1,0:T(8,128)(2,1)S(1)} %get-tuple-element.112), channel_id=1, source_target_pairs={{0,64},{32,96},{64,0},{96,32},{4,68},{36,100},{68,4},{100,36},{8,7... | collective-permute-start | bytes 98312 | tf_op jit(solution)/shard_map/ppermute | solution.py:455
  123.9 5.1 %collective-permute-start.28 = (bf16[16,1024]{1,0:T(8,128)(2,1)S(1)}, bf16[16,1024]{1,0:T(8,128)(2,1)S(1)}, u32[]{:S(2)}, u32[]{:S(2)}) collective-permute-start(bf16[16,1024]{1,0:T(8,128)(2,1)S(1)} %get-tuple-element.113), channel_id=1, source_target_pairs={{0,96},{32,0},{64,32},{96,64},{4,100},{36,4},{68,36},{100,68},{8,1... | collective-permute-start | bytes 98312 | tf_op jit(solution)/shard_map/ppermute | solution.py:455
  (7 other events, 111.6 us)
